TPU v7x, 32 devices: a whole 2x2x4 slice. The times are simulated.
32 devices in a mesh: seq: 4 (over z), fsdp: 8 (over y, x, core).
Axes of the slice: x: 2, y: 2, z: 4, core: 2. Of those that a mesh axis runs over, the one named last changes fastest.
Arguments:
- tokens: bfloat16 [8, 1280, 2048], P('fsdp', 'seq'), may hold values from -6 to 6
- cotangent: bfloat16 [8, 1280, 2048], P('fsdp', 'seq'), may hold values from -6 to 6
- lengths: int32 [8, 3], P('fsdp'), may hold values from 1 to 1200, 1280 in all within a row
- sets: int32 [8, 3], P('fsdp'), may hold values from 0 to 7
- routes: int32 [8, 1280, 8], P('fsdp', 'seq'), may hold values from 0 to 15, all different within a row; in each aligned block of 320 rows (0 to 319, 320 to 639, ..., all dimensions but the last counted through in order) at most 200 rows name the same one
- gain_attn: float32 [2048], replicated, may hold values from 0.25 to 1.75
- gain_query: float32 [2048], replicated, may hold values from 0.25 to 1.75
- gain_key: float32 [2048], replicated, may hold values from 0.25 to 1.75
- gain_mlp: float32 [2048], replicated, may hold values from 0.25 to 1.75
- query_key_value_weight: bfloat16 [2048, 6144], P('fsdp'), may hold values from -0.125 to 0.125
- out_weight: bfloat16 [2048, 2048], P('fsdp'), may hold values from -1 to 1
- router_weight: bfloat16 [2048, 16], P('fsdp'), may hold values from -0.0625 to 0.0625
- gate_up_weight: bfloat16 [16, 2048, 2048], P('fsdp'), may hold values from -0.125 to 0.125
- down_weight: bfloat16 [16, 1024, 2048], P('fsdp'), may hold values from -0.75 to 0.75
- attention_down_factors: bfloat16 [2048, 512], P('fsdp'), may hold values from -0.125 to 0.125
- attention_up_factors: bfloat16 [512, 2048], P('fsdp'), may hold values from -1.5 to 1.5
- router_down_factors: bfloat16 [2048, 128], P('fsdp'), may hold values from -0.125 to 0.125
- router_up_factors: bfloat16 [128, 16], P('fsdp'), may hold values from -0.375 to 0.375
- expert_input_down: bfloat16 [16, 2048, 256], P('fsdp'), may hold values from -0.125 to 0.125
- expert_input_up: bfloat16 [16, 2, 128, 1024], P('fsdp'), may hold values from -1.5 to 1.5
- expert_output_down: bfloat16 [16, 1024, 128], P('fsdp'), may hold values from -0.1875 to 0.1875
- expert_output_up: bfloat16 [16, 128, 2048], P('fsdp'), may hold values from -0.75 to 0.75
Outputs:
- output: bfloat16 [8, 1280, 2048], P('fsdp', 'seq')
- grad_tokens: float32 [8, 1280, 2048], P('fsdp', 'seq')
- grad_attn_down: float32 [2048, 512], P(('seq', 'fsdp'))
- grad_attn_up: float32 [512, 2048], P(('seq', 'fsdp'))
- grad_router_down: float32 [2048, 128], P(('seq', 'fsdp'))
- grad_router_up: float32 [128, 16], P(('seq', 'fsdp'))
- grad_in_down: float32 [16, 2048, 256], P('fsdp', 'seq')
- grad_in_up: float32 [16, 2, 128, 1024], P('fsdp', None, None, 'seq')
- grad_out_down: float32 [16, 1024, 128], P('fsdp', 'seq')
- grad_out_up: float32 [16, 128, 2048], P('fsdp', None, 'seq')
Inputs may be any that keep to these rules, and one draw needn't show every extreme that they name: `routes`: each row names 8 different experts; among the 320 rows of one device (aligned blocks of 320 rows) no expert is named more than 200 times, a bound that some block reaches. `lengths`: each row sums to 1280; its largest entry is exactly 1200.
All inputs are finite; a program needn't handle non-finite values.
Results may differ from a plain program's by a relative error of at most 0.019.
Values may be sent and summed in bfloat16 or wider, within the bound.
A program may use at most 384 MiB of HBM per device.

v0:
```python
import jax
import jax.numpy as jnp
from jax import lax
from jax.sharding import PartitionSpec as P

MODEL_WIDTH = 2048
H = 16
HD = 128
EXPERT_HIDDEN = 1024
TOP = 8
EXP_DEV = 2
SETS = 8
ADAPTER_RANK = 16
ADAPTER_COLUMNS = 128


EPSILON = 1e-05
THETA = 10000.0
HIGHEST = lax.Precision.HIGHEST


def matrix_product(form, left, right):
    return jnp.einsum(form, left, right, preferred_element_type=jnp.float32)


def exact(form, left, right):
    return jnp.einsum(form, left, right, precision=HIGHEST, preferred_element_type=jnp.float32)


def against(left, weight):
    return lax.dot_general(
        left, weight, (((1,), (1,)), ((), ())), preferred_element_type=jnp.float32
    )


def rms_scale(values, gain):
    return values * lax.rsqrt(jnp.mean(values * values, axis=-1, keepdims=True) + EPSILON) * gain


def rms_back(values, gain, grad):
    inverse = lax.rsqrt(jnp.mean(values * values, axis=-1, keepdims=True) + EPSILON)
    scaled = grad * gain
    return inverse * scaled - values * inverse * inverse * inverse * jnp.mean(
        values * scaled, axis=-1, keepdims=True
    )


def rotary(values, positions, direction):
    half = values.shape[-1] // 2
    freqs = THETA ** (-(jnp.arange(half, dtype=jnp.float32) * 2.0 / values.shape[-1]))
    angles = positions.astype(jnp.float32)[:, None] * freqs[None, :]
    cosine = jnp.cos(angles)[:, None, :]
    sine = direction * jnp.sin(angles)[:, None, :]
    first = values[..., :half]
    second = values[..., half:]
    return jnp.concatenate(
        [first * cosine - second * sine, second * cosine + first * sine], axis=-1
    )


def token_meta(lengths_row, sets_row, places):
    ends = jnp.cumsum(lengths_row, dtype=jnp.int32)
    starts = ends - lengths_row
    member = ((places[:, None] >= starts[None, :]) & (places[:, None] < ends[None, :])).astype(
        jnp.int32
    )
    seq_ids = jnp.sum(
        member * jnp.arange(lengths_row.shape[0], dtype=jnp.int32)[None, :], axis=1, dtype=jnp.int32
    )
    offsets = places - jnp.sum(member * starts[None, :], axis=1, dtype=jnp.int32)
    chosen = jnp.sum(member * sets_row[None, :], axis=1, dtype=jnp.int32)
    return (seq_ids, offsets, chosen)


def set_mask(chosen):
    column_range = jnp.arange(ADAPTER_COLUMNS, dtype=jnp.int32) // ADAPTER_RANK
    return (chosen[..., None] == column_range).astype(jnp.float32)


def on_device(
    tokens,
    cotangent,
    lengths,
    sets,
    routes,
    gain_attn,
    gain_query,
    gain_key,
    gain_mlp,
    query_key_value_weight,
    out_weight,
    router_weight,
    gate_up_weight,
    down_weight,
    attention_down_factors,
    attention_up_factors,
    router_down_factors,
    router_up_factors,
    expert_input_down,
    expert_input_up,
    expert_output_down,
    expert_output_up,
):
    n_seq = lax.axis_size("seq")
    n_fsdp = lax.axis_size("fsdp")
    tok_dev = tokens.shape[1]
    block = tok_dev * n_seq
    experts = EXP_DEV * n_fsdp
    capacity = 5 * tok_dev * TOP // (4 * experts)
    column_span = ADAPTER_COLUMNS
    heads_local = H // n_seq
    scale = HD ** (-0.5)
    score_rows = block // max(1, block // 512)
    count = block // score_rows
    gathered = (
        lax.all_gather(query_key_value_weight, "fsdp", axis=0, tiled=True),
        lax.all_gather(out_weight, "fsdp", axis=0, tiled=True),
        lax.all_gather(attention_down_factors, "fsdp", axis=0, tiled=True),
        lax.all_gather(attention_up_factors, "fsdp", axis=0, tiled=True),
        lax.all_gather(router_weight, "fsdp", axis=0, tiled=True),
        lax.all_gather(router_down_factors, "fsdp", axis=0, tiled=True),
        lax.all_gather(router_up_factors, "fsdp", axis=0, tiled=True),
    )
    query_key_value_rows, out_full, down_full, up_full, router_full, rdown_full, rup_full = gathered
    seq_index = lax.axis_index("seq")
    local_places = seq_index * tok_dev + jnp.arange(tok_dev, dtype=jnp.int32)
    seq_local, offsets, chosen = token_meta(lengths[0], sets[0], local_places)
    block_places = jnp.arange(block, dtype=jnp.int32)
    seq_block, block_offsets, block_sets = token_meta(lengths[0], sets[0], block_places)
    mask = set_mask(chosen)
    triple_mask = jnp.tile(mask, (1, 3))
    inputs = tokens[0].astype(jnp.float32)
    normalized_input = rms_scale(inputs, gain_attn).astype(jnp.bfloat16)
    reduced_rows = (
        matrix_product("td,dr->tr", normalized_input, down_full[:, : 3 * column_span]) * triple_mask
    ).astype(jnp.bfloat16)
    adapter_term = jnp.concatenate(
        [
            matrix_product(
                "tr,rd->td",
                reduced_rows[
                    :, projection_index * column_span : (projection_index + 1) * column_span
                ],
                up_full[projection_index * column_span : (projection_index + 1) * column_span],
            )
            for projection_index in range(3)
        ],
        axis=1,
    )
    projection_rows = (
        matrix_product("xm,mn->xn", normalized_input, query_key_value_rows) + adapter_term
    )
    queries = rotary(
        rms_scale(projection_rows[:, :MODEL_WIDTH], gain_query).reshape(tok_dev, H, HD),
        offsets,
        1.0,
    ).astype(jnp.bfloat16)
    keys = rotary(
        rms_scale(projection_rows[:, MODEL_WIDTH : 2 * MODEL_WIDTH], gain_key).reshape(
            tok_dev, H, HD
        ),
        offsets,
        1.0,
    ).astype(jnp.bfloat16)
    values = projection_rows[:, 2 * MODEL_WIDTH :].reshape(tok_dev, H, HD).astype(jnp.bfloat16)
    head_q, head_k, head_v = (
        lax.all_to_all(queries, "seq", split_axis=1, concat_axis=0, tiled=True),
        lax.all_to_all(keys, "seq", split_axis=1, concat_axis=0, tiled=True),
        lax.all_to_all(values, "seq", split_axis=1, concat_axis=0, tiled=True),
    )

    def scores_of(start):
        rows = lax.dynamic_slice_in_dim(head_q, start, score_rows, 0)
        row_ids = lax.dynamic_slice_in_dim(seq_block, start, score_rows, 0)
        row_places = start + jnp.arange(score_rows, dtype=jnp.int32)
        raw = matrix_product("qhd,khd->hqk", rows, head_k) * scale
        allowed = (block_places[None, :] <= row_places[:, None]) & (
            seq_block[None, :] == row_ids[:, None]
        )
        return (jnp.where(allowed[None], raw, -1e30), rows)

    def forward_block(start):
        scores, rows = scores_of(start)
        top = jnp.max(scores, axis=-1, keepdims=True)
        weights = jnp.exp(scores - top)
        total = jnp.sum(weights, axis=-1, keepdims=True)
        probs_rows = (weights / total).astype(jnp.bfloat16)
        result_rows = matrix_product("hqk,khd->qhd", probs_rows, head_v)
        return (result_rows.astype(jnp.bfloat16), (top + jnp.log(total))[..., 0])

    starts = jnp.arange(count, dtype=jnp.int32) * score_rows
    attended_blocks, log_totals = lax.map(forward_block, starts)
    attended_heads = attended_blocks.reshape(block, heads_local, HD)
    attended = lax.all_to_all(
        attended_heads, "seq", split_axis=0, concat_axis=1, tiled=True
    ).reshape(tok_dev, MODEL_WIDTH)
    out_lower = (
        matrix_product("td,dr->tr", attended, down_full[:, 3 * column_span :]) * mask
    ).astype(jnp.bfloat16)
    branch = matrix_product("td,de->te", attended, out_full) + matrix_product(
        "tr,rd->td", out_lower, up_full[3 * column_span :]
    )
    middle = inputs + branch
    normed2 = rms_scale(middle, gain_mlp).astype(jnp.bfloat16)
    router_lower = (matrix_product("td,dr->tr", normed2, rdown_full) * mask).astype(jnp.bfloat16)
    logits = matrix_product("td,de->te", normed2, router_full) + matrix_product(
        "tr,re->te", router_lower, rup_full
    )
    probs = jax.nn.softmax(logits, axis=-1)
    route_rows = routes[0]
    onehot_routes = (
        route_rows[:, :, None] == jnp.arange(experts, dtype=jnp.int32)[None, None, :]
    ).astype(jnp.float32)
    gates = jnp.sum(onehot_routes * probs[:, None, :], axis=-1)
    flat = route_rows.reshape(-1)
    rows_total = flat.shape[0]
    hits = (flat[:, None] == jnp.arange(experts, dtype=jnp.int32)[None, :]).astype(jnp.int32)
    ranks = jnp.sum(
        (jnp.cumsum(hits, axis=0, dtype=jnp.int32) - hits) * hits, axis=1, dtype=jnp.int32
    )
    owner = flat // EXP_DEV
    within = flat % EXP_DEV
    slots = within * (n_fsdp * capacity) + owner * capacity + ranks
    buffer_size = experts * capacity
    row_of_slot = (
        jnp.full((buffer_size,), rows_total, jnp.int32)
        .at[slots]
        .set(jnp.arange(rows_total, dtype=jnp.int32))
    )
    token_of_slot = row_of_slot // TOP
    normed2_pad = jnp.concatenate([normed2, jnp.zeros((1, MODEL_WIDTH), jnp.bfloat16)], axis=0)
    chosen_pad = jnp.concatenate([chosen, jnp.full((1,), SETS, jnp.int32)])
    send_rows = normed2_pad[token_of_slot].reshape(EXP_DEV, n_fsdp * capacity, MODEL_WIDTH)
    send_sets = chosen_pad[token_of_slot].reshape(EXP_DEV, n_fsdp * capacity)
    grad_out = cotangent[0].astype(jnp.float32)
    gate_of_slot = jnp.concatenate([gates.reshape(-1), jnp.zeros((1,), jnp.float32)])[row_of_slot]
    grad_out_pad = jnp.concatenate([grad_out, jnp.zeros((1, MODEL_WIDTH), jnp.float32)], axis=0)
    grad_send = (
        (gate_of_slot[:, None] * grad_out_pad[token_of_slot])
        .astype(jnp.bfloat16)
        .reshape(EXP_DEV, n_fsdp * capacity, MODEL_WIDTH)
    )
    recv_rows, recv_sets = (
        lax.all_to_all(send_rows, "fsdp", split_axis=1, concat_axis=1, tiled=True),
        lax.all_to_all(send_sets, "fsdp", split_axis=1, concat_axis=1, tiled=True),
    )
    row_mask = set_mask(recv_sets)
    double_mask = jnp.concatenate([row_mask, row_mask], axis=-1)
    gate_up = matrix_product("emd,edf->emf", recv_rows, gate_up_weight)
    lower_in = (matrix_product("emd,edr->emr", recv_rows, expert_input_down) * double_mask).astype(
        jnp.bfloat16
    )
    gate_part = gate_up[..., :EXPERT_HIDDEN] + matrix_product(
        "emr,erf->emf", lower_in[..., :column_span], expert_input_up[:, 0]
    )
    up_part = gate_up[..., EXPERT_HIDDEN:] + matrix_product(
        "emr,erf->emf", lower_in[..., column_span:], expert_input_up[:, 1]
    )
    sigmoid_gate = jax.nn.sigmoid(gate_part)
    activated = gate_part * sigmoid_gate
    hidden = (activated * up_part).astype(jnp.bfloat16)
    lower_out = (matrix_product("emf,efr->emr", hidden, expert_output_down) * row_mask).astype(
        jnp.bfloat16
    )
    result = (
        matrix_product("emf,efd->emd", hidden, down_weight)
        + matrix_product("emr,erd->emd", lower_out, expert_output_up)
    ).astype(jnp.bfloat16)
    result, saved = (
        result,
        (
            recv_rows,
            row_mask,
            double_mask,
            lower_in,
            gate_part,
            up_part,
            sigmoid_gate,
            activated,
            hidden,
            lower_out,
        ),
    )
    returned_buffer = lax.all_to_all(result, "fsdp", split_axis=1, concat_axis=1, tiled=True)
    grad_result = lax.all_to_all(grad_send, "fsdp", split_axis=1, concat_axis=1, tiled=True)
    (
        recv_rows,
        row_mask,
        double_mask,
        lower_in,
        gate_part,
        up_part,
        sigmoid_gate,
        activated,
        hidden,
        lower_out,
    ) = saved
    grad_lower_out = (
        matrix_product("emd,erd->emr", grad_result, expert_output_up) * row_mask
    ).astype(jnp.bfloat16)
    grad_hidden = matrix_product("emd,efd->emf", grad_result, down_weight) + matrix_product(
        "emr,efr->emf", grad_lower_out, expert_output_down
    )
    grad_out_up = matrix_product("emr,emd->erd", lower_out, grad_result)
    grad_out_down = matrix_product("emf,emr->efr", hidden, grad_lower_out)
    grad_up = (grad_hidden * activated).astype(jnp.bfloat16)
    grad_gate = (
        grad_hidden * up_part * sigmoid_gate * (1.0 + gate_part * (1.0 - sigmoid_gate))
    ).astype(jnp.bfloat16)
    grad_both = jnp.concatenate([grad_gate, grad_up], axis=-1)
    grad_lower_in = (
        jnp.concatenate(
            [
                matrix_product("emf,erf->emr", grad_gate, expert_input_up[:, 0]),
                matrix_product("emf,erf->emr", grad_up, expert_input_up[:, 1]),
            ],
            axis=-1,
        )
        * double_mask
    ).astype(jnp.bfloat16)
    grad_rows = matrix_product("emf,edf->emd", grad_both, gate_up_weight) + matrix_product(
        "emr,edr->emd", grad_lower_in, expert_input_down
    )
    grad_in_up = jnp.stack(
        [
            matrix_product("emr,emf->erf", lower_in[..., :column_span], grad_gate),
            matrix_product("emr,emf->erf", lower_in[..., column_span:], grad_up),
        ],
        axis=1,
    )
    grad_in_down = matrix_product("emd,emr->edr", recv_rows, grad_lower_in)
    grad_rows_low = grad_rows.astype(jnp.bfloat16)
    expert_terms = (grad_in_down, grad_in_up, grad_out_down, grad_out_up)
    grad_back = lax.all_to_all(grad_rows_low, "fsdp", split_axis=1, concat_axis=1, tiled=True)
    returned = (
        returned_buffer.reshape(buffer_size, MODEL_WIDTH)[slots]
        .reshape(tok_dev, TOP, MODEL_WIDTH)
        .astype(jnp.float32)
    )
    mixed = jnp.sum(gates[:, :, None] * returned, axis=1)
    output = (middle + mixed).astype(jnp.bfloat16)
    grad_gates = jnp.sum(grad_out[:, None, :] * returned, axis=-1)
    grad_normed2 = jnp.sum(
        grad_back.reshape(buffer_size, MODEL_WIDTH)[slots]
        .reshape(tok_dev, TOP, MODEL_WIDTH)
        .astype(jnp.float32),
        axis=1,
    )
    refetched = (
        lax.all_gather(query_key_value_weight, "fsdp", axis=0, tiled=True),
        lax.all_gather(out_weight, "fsdp", axis=0, tiled=True),
        lax.all_gather(attention_down_factors, "fsdp", axis=0, tiled=True),
        lax.all_gather(attention_up_factors, "fsdp", axis=0, tiled=True),
        lax.all_gather(router_weight, "fsdp", axis=0, tiled=True),
        lax.all_gather(router_down_factors, "fsdp", axis=0, tiled=True),
        lax.all_gather(router_up_factors, "fsdp", axis=0, tiled=True),
    )
    query_key_value_rows, out_full, down_full, up_full, router_full, rdown_full, rup_full = (
        refetched
    )
    grad_probs = jnp.sum(onehot_routes * grad_gates[:, :, None], axis=1)
    grad_logits = probs * (grad_probs - jnp.sum(probs * grad_probs, axis=-1, keepdims=True))
    grad_router_lower = exact("te,re->tr", grad_logits, rup_full) * mask
    grad_normed2 = (
        grad_normed2
        + exact("te,de->td", grad_logits, router_full)
        + exact("tr,dr->td", grad_router_lower, rdown_full)
    )
    grad_rup = exact("tr,te->re", router_lower, grad_logits)
    grad_rdown = exact("td,tr->dr", normed2, grad_router_lower)
    grad_middle = grad_out + rms_back(middle, gain_mlp, grad_normed2)
    grad_branch = grad_middle.astype(jnp.bfloat16)
    grad_out_lower = against(grad_branch, up_full[3 * column_span :]) * mask
    grad_attended = against(grad_branch, out_full) + exact(
        "tr,dr->td", grad_out_lower, down_full[:, 3 * column_span :]
    )
    grad_up_o = matrix_product("tr,td->rd", out_lower, grad_branch)
    grad_down_o = exact("td,tr->dr", attended, grad_out_lower)
    head_grad = lax.all_to_all(
        grad_attended.astype(jnp.bfloat16).reshape(tok_dev, H, HD),
        "seq",
        split_axis=1,
        concat_axis=0,
        tiled=True,
    )

    def backward_block(carry, inputs_block):
        grad_keys, grad_values = carry
        start, log_total = inputs_block
        scores, rows = scores_of(start)
        probs_block = jnp.exp(scores - log_total[..., None])
        grad_rows_out = lax.dynamic_slice_in_dim(head_grad, start, score_rows, 0)
        grad_probs_block = matrix_product("qhd,khd->hqk", grad_rows_out, head_v)
        delta = jnp.sum(probs_block * grad_probs_block, axis=-1, keepdims=True)
        grad_scores = (probs_block * (grad_probs_block - delta)).astype(jnp.bfloat16)
        grad_rows_q = matrix_product("hqk,khd->qhd", grad_scores, head_k) * scale
        grad_keys = grad_keys + matrix_product("hqk,qhd->khd", grad_scores, rows) * scale
        grad_values = grad_values + matrix_product(
            "hqk,qhd->khd", probs_block.astype(jnp.bfloat16), grad_rows_out
        )
        return ((grad_keys, grad_values), grad_rows_q)

    empty = jnp.zeros((block, heads_local, HD), jnp.float32)
    (grad_k_heads, grad_v_heads), grad_q_blocks = lax.scan(
        backward_block, (empty, empty), (starts, log_totals)
    )
    grad_q_heads = grad_q_blocks.reshape(block, heads_local, HD)
    grad_q_tok, grad_k_tok, grad_v_tok = (
        lax.all_to_all(
            grad_q_heads.astype(jnp.bfloat16), "seq", split_axis=0, concat_axis=1, tiled=True
        ),
        lax.all_to_all(
            grad_k_heads.astype(jnp.bfloat16), "seq", split_axis=0, concat_axis=1, tiled=True
        ),
        lax.all_to_all(
            grad_v_heads.astype(jnp.bfloat16), "seq", split_axis=0, concat_axis=1, tiled=True
        ),
    )
    grad_q_pre = rms_back(
        projection_rows[:, :MODEL_WIDTH],
        gain_query,
        rotary(grad_q_tok.astype(jnp.float32), offsets, -1.0).reshape(tok_dev, MODEL_WIDTH),
    )
    grad_k_pre = rms_back(
        projection_rows[:, MODEL_WIDTH : 2 * MODEL_WIDTH],
        gain_key,
        rotary(grad_k_tok.astype(jnp.float32), offsets, -1.0).reshape(tok_dev, MODEL_WIDTH),
    )
    grad_projected = jnp.concatenate(
        [grad_q_pre, grad_k_pre, grad_v_tok.reshape(tok_dev, MODEL_WIDTH).astype(jnp.float32)],
        axis=1,
    ).astype(jnp.bfloat16)
    grad_lower_qkv = (
        jnp.concatenate(
            [
                against(
                    grad_projected[
                        :, projection_index * MODEL_WIDTH : (projection_index + 1) * MODEL_WIDTH
                    ],
                    up_full[projection_index * column_span : (projection_index + 1) * column_span],
                )
                for projection_index in range(3)
            ],
            axis=1,
        )
        * triple_mask
    )
    grad_normed = against(grad_projected, query_key_value_rows) + exact(
        "tr,dr->td", grad_lower_qkv, down_full[:, : 3 * column_span]
    )
    grad_up_qkv = [
        matrix_product(
            "tr,td->rd",
            reduced_rows[:, projection_index * column_span : (projection_index + 1) * column_span],
            grad_projected[
                :, projection_index * MODEL_WIDTH : (projection_index + 1) * MODEL_WIDTH
            ],
        )
        for projection_index in range(3)
    ]
    grad_down_qkv = exact("td,tr->dr", normalized_input, grad_lower_qkv)
    grad_inputs = grad_middle + rms_back(inputs, gain_attn, grad_normed)
    grad_attn_down = jnp.concatenate([grad_down_qkv, grad_down_o], axis=1)
    grad_attn_up = jnp.concatenate(
        [grad_up_qkv[0], grad_up_qkv[1], grad_up_qkv[2], grad_up_o], axis=0
    )
    summed = (
        lax.psum_scatter(grad_attn_down, ("seq", "fsdp"), scatter_dimension=0, tiled=True),
        lax.psum_scatter(grad_attn_up, ("seq", "fsdp"), scatter_dimension=0, tiled=True),
        lax.psum_scatter(grad_rdown, ("seq", "fsdp"), scatter_dimension=0, tiled=True),
        lax.psum_scatter(grad_rup, ("seq", "fsdp"), scatter_dimension=0, tiled=True),
    )
    expert_sums = (
        lax.psum_scatter(
            expert_terms[0].astype(jnp.bfloat16), "seq", scatter_dimension=1, tiled=True
        ).astype(jnp.float32),
        lax.psum_scatter(
            expert_terms[1].astype(jnp.bfloat16), "seq", scatter_dimension=3, tiled=True
        ).astype(jnp.float32),
        lax.psum_scatter(
            expert_terms[2].astype(jnp.bfloat16), "seq", scatter_dimension=1, tiled=True
        ).astype(jnp.float32),
        lax.psum_scatter(
            expert_terms[3].astype(jnp.bfloat16), "seq", scatter_dimension=2, tiled=True
        ).astype(jnp.float32),
    )
    return (
        output[None],
        grad_inputs[None],
        summed[0],
        summed[1],
        summed[2],
        summed[3],
        expert_sums[0],
        expert_sums[1],
        expert_sums[2],
        expert_sums[3],
    )


def solution(mesh):
    in_specs = (
        P("fsdp", "seq", None),
        P("fsdp", "seq", None),
        P("fsdp", None),
        P("fsdp", None),
        P("fsdp", "seq", None),
        P(),
        P(),
        P(),
        P(),
        P("fsdp", None),
        P("fsdp", None),
        P("fsdp", None),
        P("fsdp", None, None),
        P("fsdp", None, None),
        P("fsdp", None),
        P("fsdp", None),
        P("fsdp", None),
        P("fsdp", None),
        P("fsdp", None, None),
        P("fsdp", None, None, None),
        P("fsdp", None, None),
        P("fsdp", None, None),
    )
    out_specs = (
        P("fsdp", "seq", None),
        P("fsdp", "seq", None),
        P(("seq", "fsdp"), None),
        P(("seq", "fsdp"), None),
        P(("seq", "fsdp"), None),
        P(("seq", "fsdp"), None),
        P("fsdp", "seq", None),
        P("fsdp", None, None, "seq"),
        P("fsdp", "seq", None),
        P("fsdp", None, "seq"),
    )
    return jax.shard_map(
        on_device, mesh=mesh, in_specs=in_specs, out_specs=out_specs, check_vma=False
    )
```

profile of v0, /device:TPU:9, one launch (start us, length us, event | category | flops | bytes accessed | tf_op | source)
XLA Modules:
  0.0 2056.7 jit_solution(15409973730441715562)
XLA Ops:
  18.5 21.0 %all-gather.7.cloned.1.call-done = bf16[2048,512]{1,0:T(8,128)(2,1)} async-done(((bf16[256,512]{1,0:T(8,128)(2,1)}), bf16[2048,512]{1,0:T(8,128)(2,1)}) %all-gather.7.cloned.1.call-update) | async-done | bytes 2097168 | tf_op jit(solution)/shard_map/all_gather | solution.py:118
  42.6 26.7 %all-gather.9.cloned.1.call-done = bf16[512,2048]{1,0:T(8,128)(2,1)} async-done(((bf16[64,2048]{1,0:T(8,128)(2,1)}), bf16[512,2048]{1,0:T(8,128)(2,1)}) %all-gather.9.cloned.1.call-update) | async-done | bytes 2097168 | tf_op jit(solution)/shard_map/all_gather | solution.py:119
  76.5 120.0 %all-gather.5.cloned.1.call-done = bf16[2048,6144]{1,0:T(8,128)(2,1)} async-done(((bf16[256,6144]{1,0:T(8,128)(2,1)}), bf16[2048,6144]{1,0:T(8,128)(2,1)}) %all-gather.5.cloned.1.call-update) | async-done | bytes 25165840 | tf_op jit(solution)/shard_map/all_gather | solution.py:116
  196.5 20.5 convolution_add_fusion
  240.2 24.4 %all-to-all-done.1 = bf16[320,16,128]{2,0,1:T(8,128)(2,1)S(1)} async-done(((bf16[320,16,128]{2,0,1:T(8,128)(2,1)}), bf16[320,16,128]{2,0,1:T(8,128)(2,1)S(1)}, u32[]{:S(2)}, u32[]{:S(2)}) %all-to-all-start.1) | async-done | bytes 1310752 | tf_op jit(solution)/shard_map/all_to_all | solution.py:168
  275.5 23.4 %all-to-all-done = bf16[320,16,128]{2,0,1:T(8,128)(2,1)} async-done(((bf16[320,16,128]{2,0,1:T(8,128)(2,1)}), bf16[320,16,128]{2,0,1:T(8,128)(2,1)}, u32[]{:S(2)}, u32[]{:S(2)}) %all-to-all-start) | async-done | bytes 1310752 | tf_op jit(solution)/shard_map/all_to_all | solution.py:167
  311.2 22.9 %all-to-all-done.2 = bf16[320,16,128]{2,0,1:T(8,128)(2,1)} async-done(((bf16[320,16,128]{2,0,1:T(8,128)(2,1)}), bf16[320,16,128]{2,0,1:T(8,128)(2,1)}, u32[]{:S(2)}, u32[]{:S(2)}) %all-to-all-start.2) | async-done | bytes 1310752 | tf_op jit(solution)/shard_map/all_to_all | solution.py:169
  336.6 57.8 %while.28 = (s32[]{:T(128)}, bf16[2,640,4,128]{3,1,0,2:T(8,128)(2,1)}, f32[2,4,640]{2,1,0:T(4,128)S(1)}, s32[2]{0:T(128)S(1)}, s32[1280]{0:T(1024)S(1)}, /*index...) while((s32[]{:T(128)}, ...), condition=%wide.region_10.11_spmd.clone, body=%wide.region_7.10_spmd.clone.sunk | while | flops 1719826560 | bytes 51873988 | solution.py:192
  426.8 19.2 gather_fusion.1
  483.8 24.6 %copy.342 = bf16[2,1600,2048]{2,0,1:T(2,128)(2,1)} copy(bf16[2,1600,2048]{2,1,0:T(8,128)(2,1)} %bitcast.312) | data formatting | bytes 26214400 | tf_op jit(solution)/shard_map/reshape | solution.py:233
  518.2 26.6 %gather_fusion.4 = f32[3200,2048]{1,0:T(8,128)} fusion(f32[321,2048]{1,0:T(8,128)} %concatenate.68, s32[4096]{0:T(1024)S(1)} %get-tuple-element.354), kind=kCustom, calls=%fused_computation.4 | custom fusion | bytes 52441600 | tf_op jit(solution)/shard_map/gather | solution.py:239
  544.7 117.4 %all_gather.34 = bf16[128,16]{1,0:T(8,128)(2,1)S(1)} all-gather(bf16[16,16]{1,0:T(8,128)(2,1)S(1)} %copy-done.114), channel_id=1, replica_groups=mesh['seq'=4,'fsdp'=8] {'fsdp'}, dimensions={0}, use_global_device_ids=true | all-gather | bytes 4608 | tf_op jit(solution)/shard_map/all_gather | solution.py:122
  682.9 16.9 gather_fusion.3
  709.8 38.4 %copy.352 = bf16[2,1600,2048]{2,0,1:T(2,128)(2,1)} copy(bf16[2,1600,2048]{2,1,0:T(8,128)(2,1)S(1)} %multiply_convert_fusion.1) | data formatting | bytes 26214400 | tf_op jit(solution)/shard_map/convert_element_type | solution.py:240
  765.7 60.5 %fusion.54 = f32[2,1600,2048]{2,1,0:T(8,128)} fusion(bf16[2,2048,2048]{2,1,0:T(8,128)(2,1)} %param.38, bf16[2,1600,2048]{2,0,1:T(2,128)(2,1)} %all-to-all-done.4), kind=kOutput, calls=%fused_computation.81 | convolution fusion | flops 26843545600 | bytes 56098816 | tf_op jit(solution)/shard_map/emd,edf->emf/dot_general | solution.py:23
  837.8 57.0 %all-to-all-done.7 = bf16[2,1600,2048]{2,0,1:T(2,128)(2,1)} async-done(((bf16[2,1600,2048]{2,0,1:T(2,128)(2,1)}), bf16[2,1600,2048]{2,0,1:T(2,128)(2,1)}, u32[]{:S(2)}, u32[]{:S(2)}) %all-to-all-start.7) | async-done | bytes 13107232 | tf_op jit(solution)/shard_map/all_to_all | solution.py:285
  894.7 26.1 %fusion.48 = f32[2,1600,1024]{2,1,0:T(8,128)} fusion(bf16[2,1024,2048]{2,1,0:T(8,128)(2,1)} %param.39, bf16[2,1600,2048]{2,0,1:T(2,128)(2,1)} %all-to-all-done.7), kind=kOutput, calls=%fused_computation.75 | convolution fusion | flops 13421772800 | bytes 34603008 | tf_op jit(solution)/shard_map/emd,efd->emf/dot_general | solution.py:23
  939.3 20.6 %multiply_convert_fusion.3 = (bf16[2,1600,1024]{2,1,0:T(8,128)(2,1)}, bf16[2,1600,1024]{2,1,0:T(8,128)(2,1)S(1)}, bf16[2,1600,1024]{2,1,0:T(8,128)(2,1)}) fusion(f32[2,1600,1024]{2,1,0:T(8,128)} %convolution_add_fusion.1, f32[2,1600,1024]{2,1,0:T(8,128)} %slice_add_fusion, bf16[2,2,128,1024]{3,2,1,0:T(8,128)(2,1)} %param.45, ...), kind=kOutput, calls=%fused_computation.67 | convolution fusion | flops 891289600 | bytes 60325888 | tf_op jit(solution)/shard_map/emr,erf->emf/dot_general | solution.py:23
  979.3 37.4 %add_convert_fusion = bf16[2,1600,2048]{2,1,0:T(8,128)(2,1)} fusion(f32[2,1600,2048]{2,1,0:T(8,128)} %fusion.189, bf16[2,2048,2048]{2,1,0:T(8,128)(2,1)} %param.38, bf16[2,1600,1024]{2,1,0:T(8,128)(2,1)} %copy-done.19, bf16[2,1600,1024]{2,1,0:T(8,128)(2,1)} %get-tuple-element.313), kind=kOutput, calls=%fused_computation.53 | convolution fusion | flops 26882867200 | bytes 69206016 | tf_op jit(solution)/shard_map/emf,edf->emd/dot_general | solution.py:23
  1016.6 24.6 %copy.355 = bf16[2,1600,2048]{2,0,1:T(2,128)(2,1)} copy(bf16[2,1600,2048]{2,1,0:T(8,128)(2,1)} %add_convert_fusion) | data formatting | bytes 26214400 | tf_op jit(solution)/shard_map/convert_element_type | solution.py:332
  1055.4 22.9 %fusion.196 = f32[2,1600,2048]{2,1,0:T(8,128)} fusion(bf16[2,1600,1024]{2,1,0:T(8,128)(2,1)} %get-tuple-element.315, bf16[2,1024,2048]{2,1,0:T(8,128)(2,1)} %param.39), kind=kOutput, calls=%fused_computation.321 | convolution fusion | flops 13421772800 | bytes 41156608 | tf_op jit(solution)/shard_map/emf,efd->emd/dot_general | solution.py:23
  1093.5 24.6 %copy.349 = bf16[2,1600,2048]{2,0,1:T(2,128)(2,1)} copy(bf16[2,1600,2048]{2,1,0:T(8,128)(2,1)} %add_convert_fusion.1) | data formatting | bytes 26214400 | tf_op jit(solution)/shard_map/convert_element_type | solution.py:268
  1118.1 73.7 %all-to-all-done.8 = bf16[2,1600,2048]{2,0,1:T(2,128)(2,1)} async-done(((bf16[2,1600,2048]{2,0,1:T(2,128)(2,1)}), bf16[2,1600,2048]{2,0,1:T(2,128)(2,1)}, u32[]{:S(2)}, u32[]{:S(2)}) %all-to-all-start.8) | async-done | bytes 13107232 | tf_op jit(solution)/shard_map/all_to_all | solution.py:334
  1230.0 26.6 %gather_fusion.5 = bf16[2560,2048]{1,0:T(8,128)(2,1)} fusion(bf16[3200,2048]{1,0:T(8,128)(2,1)} %bitcast.305, s32[3072]{0:T(1024)S(1)} %pad_clamp_fusion.2), kind=kCustom, calls=%fused_computation.5 | custom fusion | bytes 20981760 | tf_op jit(solution)/shard_map/gather | solution.py:344
  1266.9 74.9 %all-to-all-done.6 = bf16[2,1600,2048]{2,0,1:T(2,128)(2,1)} async-done(((bf16[2,1600,2048]{2,0,1:T(2,128)(2,1)}), bf16[2,1600,2048]{2,0,1:T(2,128)(2,1)}, u32[]{:S(2)}, u32[]{:S(2)}) %all-to-all-start.6) | async-done | bytes 13107232 | tf_op jit(solution)/shard_map/all_to_all | solution.py:284
  1354.9 26.6 %gather_fusion.2 = bf16[2560,2048]{1,0:T(8,128)(2,1)} fusion(bf16[3200,2048]{1,0:T(8,128)(2,1)} %bitcast.304, s32[3072]{0:T(1024)S(1)} %pad_clamp_fusion.2), kind=kCustom, calls=%fused_computation.2 | custom fusion | bytes 20981760 | tf_op jit(solution)/shard_map/gather | solution.py:336
  1449.0 81.0 %while.29 = (s32[]{:T(128)}, f32[1280,4,128]{0,2,1:T(8,128)}, f32[1280,4,128]{0,2,1:T(8,128)}, bf16[2,640,4,128]{3,1,0,2:T(8,128)(2,1)}, s32[2]{0:T(128)S(1)}, /...) while((s32[]{:T(128)}, f32[1280,4,128]{0,2,1:T(8,128)}, ...), condition=%wide.region_27.28_spmd.clone, body=%wide.region_25.27_spmd.clone.sunk | while | flops 4229855232 | bytes 162926944 | solution.py:404
  1537.5 16.9 all-to-all-start.10
  1596.7 48.5 %all-to-all-done.11 = bf16[1280,4,128]{2,1,0:T(4,128)(2,1)} async-done(((bf16[1280,4,128]{2,1,0:T(4,128)(2,1)}), bf16[1280,4,128]{2,1,0:T(4,128)(2,1)}, u32[]{:S(2)}, u32[]{:S(2)}) %all-to-all-start.11) | async-done | bytes 1310752 | tf_op jit(solution)/shard_map/all_to_all | solution.py:412
  1725.5 42.9 %all-reduce.2 = f32[128,16]{1,0:T(8,128)S(1)} all-reduce(f32[128,16]{1,0:T(8,128)S(1)} %fusion.200), channel_id=5, replica_groups=mesh['seq'=4,'fsdp'=8] {'seq','fsdp'}, use_global_device_ids=true, to_apply=%region_34.35.clone | all-reduce | flops 2048 | bytes 16384
  1791.0 119.1 %reduce-scatter.10.cloned.1.call-done = f32[16,2048]{1,0:T(8,128)} async-done(((f32[512,2048]{1,0:T(8,128)}), f32[16,2048]{1,0:T(8,128)}) %reduce-scatter.10.cloned.1.call-update) | async-done | bytes 131088 | tf_op jit(solution)/shard_map/reduce_scatter | solution.py:469
  1910.1 139.8 %reduce-scatter.22.cloned.1.call-done = f32[64,512]{1,0:T(8,128)} async-done(((f32[2048,512]{1,0:T(8,128)}), f32[64,512]{1,0:T(8,128)}) %reduce-scatter.22.cloned.1.call-update) | async-done | bytes 131088
  (515 shorter events, 688.2 us)
Async XLA Ops:
  7.2 747.2 %copy-start = (bf16[2,2048,256]{2,1,0:T(8,128)(2,1)S(1)}, bf16[2,2048,256]{2,1,0:T(8,128)(2,1)}, u32[]{:S(2)}) copy-start(bf16[2,2048,256]{2,1,0:T(8,128)(2,1)} %param.44) | copy-start | bytes 6291460
  7.2 32.3 %all-gather.7.cloned.1.call-start = ((), (), s32[]{:S(2)}) async-start(), calls=%async_computation.21 | async-start | bytes 2359296 | tf_op jit(solution)/shard_map/all_gather | solution.py:118
  7.9 61.3 %all-gather.9.cloned.1.call-start = ((), (), s32[]{:S(2)}) async-start(), calls=%async_computation.22 | async-start | bytes 2359296 | tf_op jit(solution)/shard_map/all_gather | solution.py:119
  8.7 187.8 %all-gather.5.cloned.1.call-start = ((), (), s32[]{:S(2)}) async-start(), calls=%async_computation.20 | async-start | bytes 28311552 | tf_op jit(solution)/shard_map/all_gather | solution.py:116
  17.1 179.5 %copy-start.109 = (f32[320]{0:T(512)}, f32[320]{0:T(512)S(1)}, u32[]{:S(2)}) copy-start(f32[320]{0:T(512)S(1)} %add_rsqrt_fusion.3) | copy-start | bytes 3844
  232.1 32.5 %all-to-all-start.1 = ((bf16[320,16,128]{2,0,1:T(8,128)(2,1)}), bf16[320,16,128]{2,0,1:T(8,128)(2,1)S(1)}, u32[]{:S(2)}, u32[]{:S(2)}) async-start(bf16[320,16,128]{2,0,1:T(8,128)(2,1)} %pad_maximum_fusion.3), calls=%async_computation.1 | async-start | bytes 2621440 | tf_op jit(solution)/shard_map/all_to_all | solution.py:168
  264.6 34.3 %all-to-all-start = ((bf16[320,16,128]{2,0,1:T(8,128)(2,1)}), bf16[320,16,128]{2,0,1:T(8,128)(2,1)}, u32[]{:S(2)}, u32[]{:S(2)}) async-start(bf16[320,16,128]{2,0,1:T(8,128)(2,1)} %pad_maximum_fusion.2), calls=%async_computation | async-start | bytes 2621440 | tf_op jit(solution)/shard_map/all_to_all | solution.py:167
  271.8 188.0 %all-gather.11.cloned.1.call-start = ((), (), s32[]{:S(2)}) async-start(), calls=%async_computation.23 | async-start | bytes 9437184 | tf_op jit(solution)/shard_map/all_gather | solution.py:117
  298.8 35.3 %all-to-all-start.2 = ((bf16[320,16,128]{2,0,1:T(8,128)(2,1)}), bf16[320,16,128]{2,0,1:T(8,128)(2,1)}, u32[]{:S(2)}, u32[]{:S(2)}) async-start(bf16[320,16,128]{2,0,1:T(8,128)(2,1)} %copy_bitcast_fusion.1), calls=%async_computation.2 | async-start | bytes 2621440 | tf_op jit(solution)/shard_map/all_to_all | solution.py:169
  402.2 44.5 %all-to-all-start.3 = ((bf16[1280,4,128]{2,1,0:T(4,128)(2,1)}), bf16[1280,4,128]{2,1,0:T(4,128)(2,1)}, u32[]{:S(2)}, u32[]{:S(2)}) async-start(bf16[1280,4,128]{2,1,0:T(4,128)(2,1)} %copy.336), calls=%async_computation.3 | async-start | bytes 2621440 | tf_op jit(solution)/shard_map/all_to_all | solution.py:194
  446.7 61.7 %all-to-all-start.5 = ((s32[2,8,200]{2,0,1:T(2,128)}), s32[2,8,200]{2,0,1:T(2,128)S(1)}, u32[]{:S(2)}, u32[]{:S(2)}) async-start(s32[2,8,200]{2,0,1:T(2,128)} %copy.344), calls=%async_computation.5 | async-start | bytes 32768 | tf_op jit(solution)/shard_map/all_to_all | solution.py:245
  508.4 239.8 %all-to-all-start.4 = ((bf16[2,1600,2048]{2,0,1:T(2,128)(2,1)}), bf16[2,1600,2048]{2,0,1:T(2,128)(2,1)}, u32[]{:S(2)}, u32[]{:S(2)}) async-start(bf16[2,1600,2048]{2,0,1:T(2,128)(2,1)} %copy.342), calls=%async_computation.4 | async-start | bytes 26214400 | tf_op jit(solution)/shard_map/all_to_all | solution.py:244
  518.2 144.0 %copy-start.113 = (bf16[256,16]{0,1:T(8,128)(2,1)S(1)}, bf16[256,16]{0,1:T(8,128)(2,1)}, u32[]{:S(2)}) copy-start(bf16[256,16]{0,1:T(8,128)(2,1)} %param.37) | copy-start | bytes 24580
  518.2 152.2 %copy-start.92 = (bf16[256,128]{1,0:T(8,128)(2,1)S(1)}, bf16[256,128]{1,0:T(8,128)(2,1)}, u32[]{:S(2)}) copy-start(bf16[256,128]{1,0:T(8,128)(2,1)} %param.42) | copy-start | bytes 196612
  518.2 161.9 %copy-start.12 = (bf16[320,2048]{1,0:T(8,128)(2,1)S(1)}, bf16[320,2048]{1,0:T(8,128)(2,1)}, u32[]{:S(2)}) copy-start(bf16[320,2048]{1,0:T(8,128)(2,1)} %copy-done.11) | copy-start | bytes 3932164
  518.2 161.9 %copy-start.112 = (s32[128]{0:T(128)S(1)}, s32[128]{0:T(128)}, u32[]{:S(2)}) copy-start(s32[128]{0:T(128)} %copy-done.111) | copy-start | bytes 1540
  748.2 146.5 %all-to-all-start.7 = ((bf16[2,1600,2048]{2,0,1:T(2,128)(2,1)}), bf16[2,1600,2048]{2,0,1:T(2,128)(2,1)}, u32[]{:S(2)}, u32[]{:S(2)}) async-start(bf16[2,1600,2048]{2,0,1:T(2,128)(2,1)} %copy.352), calls=%async_computation.7 | async-start | bytes 26214400 | tf_op jit(solution)/shard_map/all_to_all | solution.py:285
  754.4 213.3 %copy-start.41 = (pred[2,1600,128]{2,1,0:T(32,128)(4,1)}, pred[2,1600,128]{2,1,0:T(32,128)(4,1)S(1)}, u32[]{:S(2)}) copy-start(pred[2,1600,128]{2,1,0:T(32,128)(4,1)S(1)} %broadcast_compare_fusion) | copy-start | bytes 1228804
  1041.2 150.5 %all-to-all-start.8 = ((bf16[2,1600,2048]{2,0,1:T(2,128)(2,1)}), bf16[2,1600,2048]{2,0,1:T(2,128)(2,1)}, u32[]{:S(2)}, u32[]{:S(2)}) async-start(bf16[2,1600,2048]{2,0,1:T(2,128)(2,1)} %copy.355), calls=%async_computation.8 | async-start | bytes 26214400 | tf_op jit(solution)/shard_map/all_to_all | solution.py:334
  1191.8 150.0 %all-to-all-start.6 = ((bf16[2,1600,2048]{2,0,1:T(2,128)(2,1)}), bf16[2,1600,2048]{2,0,1:T(2,128)(2,1)}, u32[]{:S(2)}, u32[]{:S(2)}) async-start(bf16[2,1600,2048]{2,0,1:T(2,128)(2,1)} %copy.349), calls=%async_computation.6 | async-start | bytes 26214400 | tf_op jit(solution)/shard_map/all_to_all | solution.py:284
  1200.7 517.2 %reduce-scatter.18.cloned.1.call-start = ((), (), s32[]{:S(2)}) async-start(), calls=%async_computation.28 | async-start | bytes 655360 | tf_op jit(solution)/shard_map/reduce_scatter | solution.py:480
  1207.6 511.9 %reduce-scatter.16.cloned.1.call-start = ((), (), s32[]{:S(2)}) async-start(), calls=%async_computation.27 | async-start | bytes 1310720 | tf_op jit(solution)/shard_map/reduce_scatter | solution.py:477
  1411.7 34.7 %all-to-all-start.9 = ((bf16[320,16,128]{2,0,1:T(8,128)(2,1)}), bf16[320,16,128]{2,0,1:T(8,128)(2,1)}, u32[]{:S(2)}, u32[]{:S(2)}) async-start(bf16[320,16,128]{2,0,1:T(8,128)(2,1)} %bitcast.269), calls=%async_computation.9 | async-start | bytes 2621440 | tf_op jit(solution)/shard_map/all_to_all | solution.py:379
  1416.3 305.0 %reduce-scatter.20.cloned.1.call-start = ((), (), s32[]{:S(2)}) async-start(), calls=%async_computation.29 | async-start | bytes 1310720 | tf_op jit(solution)/shard_map/reduce_scatter | solution.py:483
  1537.5 42.2 %all-to-all-start.10 = ((bf16[1280,4,128]{2,1,0:T(4,128)(2,1)}), bf16[1280,4,128]{2,1,0:T(4,128)(2,1)S(1)}, u32[]{:S(2)}, u32[]{:S(2)}) async-start(bf16[1280,4,128]{2,1,0:T(4,128)(2,1)} %copy.361), calls=%async_computation.10 | async-start | bytes 2621440 | tf_op jit(solution)/shard_map/all_to_all | solution.py:409
  1554.3 168.8 %reduce-scatter.14.cloned.1.call-start = ((), (), s32[]{:S(2)}) async-start(), calls=%async_computation.26 | async-start | bytes 2621440 | tf_op jit(solution)/shard_map/reduce_scatter | solution.py:474
  1579.7 65.5 %all-to-all-start.11 = ((bf16[1280,4,128]{2,1,0:T(4,128)(2,1)}), bf16[1280,4,128]{2,1,0:T(4,128)(2,1)}, u32[]{:S(2)}, u32[]{:S(2)}) async-start(bf16[1280,4,128]{2,1,0:T(4,128)(2,1)} %copy.365), calls=%async_computation.11 | async-start | bytes 2621440 | tf_op jit(solution)/shard_map/all_to_all | solution.py:412
  1645.2 36.0 %all-to-all-start.12 = ((bf16[1280,4,128]{2,1,0:T(4,128)(2,1)}), bf16[1280,4,128]{2,1,0:T(4,128)(2,1)}, u32[]{:S(2)}, u32[]{:S(2)}) async-start(bf16[1280,4,128]{2,1,0:T(4,128)(2,1)} %copy.369), calls=%async_computation.12 | async-start | bytes 2621440 | tf_op jit(solution)/shard_map/all_to_all | solution.py:415
  1652.9 138.1 %reduce-scatter.12.cloned.1.call-start = ((), (), s32[]{:S(2)}) async-start(), calls=%async_computation.25 | async-start | bytes 1081344 | tf_op jit(solution)/shard_map/reduce_scatter | solution.py:470
  1656.2 253.9 %reduce-scatter.10.cloned.1.call-start = ((), (), s32[]{:S(2)}) async-start(), calls=%async_computation.24 | async-start | bytes 4325376 | tf_op jit(solution)/shard_map/reduce_scatter | solution.py:469
  1697.4 352.5 %reduce-scatter.22.cloned.1.call-start = ((), (), s32[]{:S(2)}) async-start(), calls=%async_computation.30 | async-start | bytes 4325376
  1788.7 261.2 %copy-start.1 = (bf16[2,2048,256]{2,1,0:T(8,128)(2,1)S(1)}, bf16[2,2048,256]{2,1,0:T(8,128)(2,1)}, u32[]{:S(2)}) copy-start(bf16[2,2048,256]{2,1,0:T(8,128)(2,1)} %param.44) | copy-start | bytes 6291460
  (125 other events, 1183.5 us)
Sparse Core Ops, SparseCore 0:
  9.9 29.4 all-gather.6
  41.4 27.8 all-gather.8
  71.2 125.3 all-gather.4
  274.2 55.7 all-gather.10
  1207.7 18.5 reduce-scatter.17
  1228.5 27.2 reduce-scatter.15
  1430.4 34.3 reduce-scatter.19
  1571.3 75.9 reduce-scatter.13
  1656.7 114.0 reduce-scatter.11
  1773.5 136.5 reduce-scatter.9
  1913.0 136.8 reduce-scatter.21
where the time goes:
time: 2090 us; the launch traced here: 2060 us
  waiting for transfers between devices  780 us (37%)
  matrix products  466 us (22%)
  local copies, waits for them, and re-layouts  368 us (18%)
  blocking collectives  178 us (9%)
  other arithmetic  136 us (7%)
  starting transfers between devices  104 us (5%)
    dot_general x48, matrix products, matrix_product(): return jnp.einsum(form, left, right, preferred_element_type=jnp.float32)  421 us
    unnamed x12, waiting for transfers between devices  143 us
    all_gather x1, waiting for transfers between devices, on_device(): lax.all_gather(query_key_value_weight, 'fsdp', axis=0, tiled=True)  120 us
    reduce_scatter x1, waiting for transfers between devices, on_device(): lax.psum_scatter(grad_attn_up, ('seq', 'fsdp'), scatter_dimension=0, tile...  119 us
    all_gather x1, blocking collectives, on_device(): lax.all_gather(router_up_factors, 'fsdp', axis=0, tiled=True)  117 us
    all_to_all x1, waiting for transfers between devices, on_device(): lax.all_to_all(result, 'fsdp', split_axis=1, concat_axis=1, tiled=True)  74.9 us
    all_to_all x1, waiting for transfers between devices, on_device(): lax.all_to_all(grad_rows_low, 'fsdp', split_axis=1, concat_axis=1, tiled=...  73.7 us
    all_to_all x1, waiting for transfers between devices, on_device(): lax.all_to_all(grad_send, 'fsdp', split_axis=1, concat_axis=1, tiled=True)  57 us
  transfers between devices with their start and end apart: 24, of which 15 were waited for; matrix products, arithmetic and copies ran while one was open for 38% of the time, Pallas kernels for 0%

commit v1 on v0

v1 whole, which is shorter than its diff:
```python
import functools

import jax
import jax.numpy as jnp
from jax import lax
from jax.experimental import pallas as pl
from jax.experimental.pallas import tpu as pltpu
from jax.sharding import Mesh
from jax.sharding import PartitionSpec as P

MODEL_WIDTH = 2048
H = 16
HD = 128
EXPERT_HIDDEN = 1024
TOP = 8
EXP_DEV = 2
ADAPTER_RANK = 16
SPAN = 128
GROUPS = 4
GROUP_WIDTH = MODEL_WIDTH // GROUPS
HEADS = H // GROUPS

EPSILON = 1e-05
THETA = 10000.0
NEGATIVE = -1e30
BF = jnp.bfloat16
F32 = jnp.float32
ANY = pl.ANY
VMEM = pltpu.VMEM
SEQ = ("zh", "zl")
FSDP = ("c", "core")


def mm(left, right):
    return lax.dot_general(left, right, (((1,), (0,)), ((), ())), preferred_element_type=F32)


def mm_t(left, right):
    return lax.dot_general(left, right, (((1,), (1,)), ((), ())), preferred_element_type=F32)


def t_mm(left, right):
    return lax.dot_general(left, right, (((0,), (0,)), ((), ())), preferred_element_type=F32)


def exact(form, left, right):
    return jnp.einsum(form, left, right, precision=lax.Precision.HIGHEST, preferred_element_type=F32)


def rms_scale(values, gain):
    return values * lax.rsqrt(jnp.mean(values * values, axis=-1, keepdims=True) + EPSILON) * gain


def rms_back(values, gain, grad):
    inverse = lax.rsqrt(jnp.mean(values * values, axis=-1, keepdims=True) + EPSILON)
    scaled = grad * gain
    return inverse * scaled - values * inverse * inverse * inverse * jnp.mean(
        values * scaled, axis=-1, keepdims=True
    )


def token_meta(lengths_row, sets_row, places):
    count = lengths_row.shape[0]
    running = [lengths_row[0]]
    for n in range(1, count):
        running.append(running[-1] + lengths_row[n])
    ends = jnp.stack(running)
    starts = ends - lengths_row
    member = ((places[:, None] >= starts[None, :]) & (places[:, None] < ends[None, :])).astype(
        jnp.int32
    )
    seq_ids = jnp.sum(member * jnp.arange(count, dtype=jnp.int32)[None, :], axis=1)
    offsets = places - jnp.sum(member * starts[None, :], axis=1)
    chosen = jnp.sum(member * sets_row[None, :], axis=1)
    return (seq_ids, offsets, chosen)


def set_mask(chosen):
    column_range = jnp.arange(SPAN, dtype=jnp.int32) // ADAPTER_RANK
    return (chosen[..., None] == column_range).astype(F32)


def here():
    return tuple(lax.axis_index(n) for n in ("zh", "zl", "c", "core"))


def signal_all(peers):
    barrier = pltpu.get_barrier_semaphore()
    for peer in peers:
        pl.semaphore_signal(barrier, inc=1, device_id=peer, device_id_type=pl.DeviceIdType.MESH)
    pl.semaphore_wait(barrier, len(peers))


def remote(src, dst, send, recv, device):
    return pltpu.make_async_remote_copy(
        src_ref=src,
        dst_ref=dst,
        send_sem=send,
        recv_sem=recv,
        device_id=device,
        device_id_type=pl.DeviceIdType.MESH,
    )


def column_peers(zh, zl, c, core):
    return [
        (zh ^ a, zl ^ b, c, core ^ k)
        for a in range(2)
        for b in range(2)
        for k in range(2)
        if (a, b, k) != (0, 0, 0)
    ]


def gather_kernel(n_c, x_ref, w_ref, xg_ref, wg_ref, xs, xr, fs, fr, ws, wr, own):
    zh, zl, c, core = here()
    tok = x_ref.shape[0]
    half = tok // 2
    rows = w_ref.shape[0]
    plane = [(zh, zl, lax.rem(c + i, n_c), core ^ k) for i in range(n_c) for k in range(2)][2:]
    signal_all(column_peers(zh, zl, c, core) + plane)
    me = zh * 2 + zl
    for a in range(2):
        for k in range(2):
            piece = pl.ds(k * half, half)
            src, dst = x_ref.at[piece], xg_ref.at[me, piece]
            is_self = (core == zh) & (zl == a) & (core == k)

            @pl.when(is_self)
            def _():
                pltpu.make_async_copy(src, dst, xr.at[me]).start()

            @pl.when(jnp.logical_not(is_self))
            def _():
                remote(src, dst, xs.at[a, k], xr.at[me], (core, a, c, k)).start()

    f = c * 2 + core
    row_block = pl.ds(pl.multiple_of(f * rows, rows), rows)

    def pieces(group):
        for j in range(3):
            start = pl.multiple_of(j * MODEL_WIDTH + group * GROUP_WIDTH, GROUP_WIDTH)
            yield (
                w_ref.at[:, pl.ds(start, GROUP_WIDTH)],
                wg_ref.at[row_block, pl.ds(j * GROUP_WIDTH, GROUP_WIDTH)],
            )

    for src, dst in pieces(zl * 2 + core):
        pltpu.make_async_copy(src, dst, own).start()
    slots = [(i, k) for i in range(n_c) for k in range(2)][1:]
    for i, k in slots:
        target_c, target_core = lax.rem(c + i, n_c), core ^ k
        for src, dst in pieces(zl * 2 + target_core):
            remote(
                src, dst, ws.at[i * 2 + k], wr.at[i * 2 + k], (zh, zl, target_c, target_core)
            ).start()
    mine = pl.ds(pl.multiple_of(core * half, half), half)
    theirs = pl.ds(pl.multiple_of((1 - core) * half, half), half)
    sibling = (zh, zl, c, 1 - core)
    order = [zl ^ 0, zl ^ 1]
    for s in range(4):
        pltpu.make_async_copy(xg_ref.at[s, mine], xg_ref.at[s, mine], xr.at[s]).wait()
        remote(xg_ref.at[s, mine], xg_ref.at[s, mine], fs.at[s], fr.at[s], sibling).start()
    for s in range(4):
        got = xg_ref.at[s, theirs]
        pltpu.make_async_copy(got, got, fr.at[s]).wait()
    for s in range(4):
        got = xg_ref.at[s, mine]
        pltpu.make_async_copy(got, got, fs.at[s]).wait()
    for a in range(2):
        for k in range(2):
            is_self = (core == zh) & (zl == a) & (core == k)
            src = x_ref.at[pl.ds(k * half, half)]

            @pl.when(jnp.logical_not(is_self))
            def _():
                pltpu.make_async_copy(src, src, xs.at[a, k]).wait()

    block = wg_ref.at[row_block]
    pltpu.make_async_copy(block, block, own).wait()
    for i, k in slots:
        pltpu.make_async_copy(block, block, ws.at[i * 2 + k]).wait()
        source = lax.rem(c + n_c - i, n_c) * 2 + (core ^ k)
        got = wg_ref.at[pl.ds(pl.multiple_of(source * rows, rows), rows)]
        pltpu.make_async_copy(got, got, wr.at[i * 2 + k]).wait()


def gather_to_heads(x, w, n_c):
    tok, rows = x.shape[0], w.shape[0]
    n_f = 2 * n_c
    dma = pltpu.SemaphoreType.DMA
    return pl.pallas_call(
        functools.partial(gather_kernel, n_c),
        out_shape=(
            jax.ShapeDtypeStruct((4, tok, MODEL_WIDTH), BF),
            jax.ShapeDtypeStruct((n_f * rows, 3 * GROUP_WIDTH), BF),
        ),
        in_specs=[pl.BlockSpec(memory_space=ANY)] * 2,
        out_specs=[pl.BlockSpec(memory_space=ANY)] * 2,
        scratch_shapes=[
            dma((2, 2)),
            dma((4,)),
            dma((4,)),
            dma((4,)),
            dma((n_f,)),
            dma((n_f,)),
            dma,
        ],
        compiler_params=pltpu.CompilerParams(collective_id=0, has_side_effects=True),
        name="gather_to_heads",
    )(x, w)


def to_tokens_kernel(a_ref, o_ref, send, recv):
    zh, zl, c, core = here()
    signal_all(column_peers(zh, zl, c, core))
    group = zl * 2 + core
    columns = pl.ds(pl.multiple_of(group * GROUP_WIDTH, GROUP_WIDTH), GROUP_WIDTH)
    for s in range(4):
        a, b = s // 2, s % 2
        is_self = (a == zh) & (b == zl) & (core == zh)
        src, dst = a_ref.at[s], o_ref.at[:, columns]

        @pl.when(is_self)
        def _():
            pltpu.make_async_copy(src, dst, recv.at[group]).start()

        @pl.when(jnp.logical_not(is_self))
        def _():
            remote(src, dst, send.at[s], recv.at[group], (a, b, c, zh)).start()

    for s in range(4):
        a, b = s // 2, s % 2
        is_self = (a == zh) & (b == zl) & (core == zh)
        got = o_ref.at[:, pl.ds(s * GROUP_WIDTH, GROUP_WIDTH)]
        pltpu.make_async_copy(got, got, recv.at[s]).wait()

        @pl.when(jnp.logical_not(is_self))
        def _():
            pltpu.make_async_copy(a_ref.at[s], a_ref.at[s], send.at[s]).wait()


def to_tokens(rows):
    tok = rows.shape[1]
    dma = pltpu.SemaphoreType.DMA
    return pl.pallas_call(
        to_tokens_kernel,
        out_shape=jax.ShapeDtypeStruct((tok, MODEL_WIDTH), BF),
        in_specs=[pl.BlockSpec(memory_space=ANY)],
        out_specs=pl.BlockSpec(memory_space=ANY),
        scratch_shapes=[dma((4,)), dma((4,))],
        compiler_params=pltpu.CompilerParams(collective_id=1, has_side_effects=True),
        name="to_tokens",
    )(rows)


def to_heads_kernel(a_ref, o_ref, send, recv):
    zh, zl, c, core = here()
    signal_all(column_peers(zh, zl, c, core))
    me = zh * 2 + zl
    for g in range(4):
        b, k = g // 2, g % 2
        is_self = (core == zh) & (b == zl) & (core == k)
        src, dst = a_ref.at[:, pl.ds(g * GROUP_WIDTH, GROUP_WIDTH)], o_ref.at[me]

        @pl.when(is_self)
        def _():
            pltpu.make_async_copy(src, dst, recv.at[me]).start()

        @pl.when(jnp.logical_not(is_self))
        def _():
            remote(src, dst, send.at[g], recv.at[me], (core, b, c, k)).start()

    for g in range(4):
        b, k = g // 2, g % 2
        is_self = (core == zh) & (b == zl) & (core == k)
        pltpu.make_async_copy(o_ref.at[g], o_ref.at[g], recv.at[g]).wait()

        @pl.when(jnp.logical_not(is_self))
        def _():
            pltpu.make_async_copy(o_ref.at[g], o_ref.at[g], send.at[g]).wait()


def to_heads(rows):
    tok = rows.shape[0]
    dma = pltpu.SemaphoreType.DMA
    return pl.pallas_call(
        to_heads_kernel,
        out_shape=jax.ShapeDtypeStruct((4, tok, GROUP_WIDTH), BF),
        in_specs=[pl.BlockSpec(memory_space=ANY)],
        out_specs=pl.BlockSpec(memory_space=ANY),
        scratch_shapes=[dma((4,)), dma((4,))],
        compiler_params=pltpu.CompilerParams(collective_id=2, has_side_effects=True),
        name="to_heads",
    )(rows)


def sum_to_tokens_kernel(p_ref, o_ref, sib, chip, rx, ss, sr, send, recv):
    zh, zl, c, core = here()
    signal_all(column_peers(zh, zl, c, core))
    width = o_ref.shape[1]
    half = width // 2
    sibling = (zh, zl, c, 1 - core)
    mine = pl.ds(pl.multiple_of(core * half, half), half)
    theirs = pl.ds(pl.multiple_of((1 - core) * half, half), half)
    for s in range(4):
        remote(p_ref.at[s, :, theirs], sib.at[s], ss.at[s], sr.at[s], sibling).start()

    def is_self(s):
        return (s // 2 == zh) & (s % 2 == zl) & (core == zh)

    for s in range(4):
        pltpu.make_async_copy(sib.at[s], sib.at[s], sr.at[s]).wait()
        chip[s] = (p_ref[s, :, mine].astype(F32) + sib[s].astype(F32)).astype(BF)
        src, dst = chip.at[s], rx.at[zl, core]

        @pl.when(is_self(s))
        def _():
            pltpu.make_async_copy(src, dst, recv.at[zl, core]).start()

        @pl.when(jnp.logical_not(is_self(s)))
        def _():
            remote(src, dst, send.at[s], recv.at[zl, core], (s // 2, s % 2, c, zh)).start()

    for s in range(4):
        pltpu.make_async_copy(sib.at[s], sib.at[s], ss.at[s]).wait()

        @pl.when(jnp.logical_not(is_self(s)))
        def _():
            pltpu.make_async_copy(chip.at[s], chip.at[s], send.at[s]).wait()

    for k in range(2):
        for b in range(2):
            pltpu.make_async_copy(rx.at[b, k], rx.at[b, k], recv.at[b, k]).wait()
        o_ref[:, k * half : (k + 1) * half] = rx[0, k].astype(F32) + rx[1, k].astype(F32)


def sum_to_tokens(parts):
    _, tok, width = parts.shape
    half = width // 2
    dma = pltpu.SemaphoreType.DMA
    return pl.pallas_call(
        sum_to_tokens_kernel,
        out_shape=jax.ShapeDtypeStruct((tok, width), F32),
        in_specs=[pl.BlockSpec(memory_space=VMEM)],
        out_specs=pl.BlockSpec(memory_space=VMEM),
        scratch_shapes=[
            VMEM((4, tok, half), BF),
            VMEM((4, tok, half), BF),
            VMEM((2, 2, tok, half), BF),
            dma((4,)),
            dma((4,)),
            dma((4,)),
            dma((2, 2)),
        ],
        compiler_params=pltpu.CompilerParams(
            collective_id=3, has_side_effects=True, vmem_limit_bytes=40 * 2**20
        ),
        name="sum_to_tokens",
    )(parts)


def group_sum_kernel(x_ref, o_ref, rx, send, recv):
    zh, zl, c, core = here()
    peers = [(zh, zl, c, 1 - core), (zh, 1 - zl, c, core), (zh, 1 - zl, c, 1 - core)]
    signal_all(peers)
    copies = [remote(x_ref, rx.at[i], send.at[i], recv.at[i], p) for i, p in enumerate(peers)]
    for copy in copies:
        copy.start()
    for copy in copies:
        copy.wait()
    o_ref[...] = (x_ref[...] + rx[0]) + (rx[1] + rx[2])


def group_sum(values, identity):
    dma = pltpu.SemaphoreType.DMA
    return pl.pallas_call(
        group_sum_kernel,
        out_shape=jax.ShapeDtypeStruct(values.shape, F32),
        in_specs=[pl.BlockSpec(memory_space=VMEM)],
        out_specs=pl.BlockSpec(memory_space=VMEM),
        scratch_shapes=[VMEM((3, *values.shape), F32), dma((3,)), dma((3,))],
        compiler_params=pltpu.CompilerParams(collective_id=identity, has_side_effects=True),
        name="group_sum",
    )(values)


def turn(values, cosine, sine):
    return values * cosine + pltpu.roll(values, HD // 2, 1) * sine


def attention_rows(block):
    return 256 if block % 256 == 0 else block


def attend_kernel(
    pq, pk, pv, rq, rk, gq, gk, cosine, sine, seg_c, seg_r, q_ref, k_ref, v_ref, o_ref, lse_ref
):
    block = pq.shape[0]
    rows = attention_rows(block)
    scale = HD**-0.5
    q_ref[...] = turn(pq[...] * rq[...] * gq[...], cosine[...], sine[...]).astype(BF)
    k_ref[...] = turn(pk[...] * rk[...] * gk[...], cosine[...], sine[...]).astype(BF)
    v_ref[...] = pv[...].astype(BF)
    for i in range(block // rows):
        length = (i + 1) * rows
        own = slice(i * rows, length)
        scores = mm_t(q_ref[own], k_ref[:length]) * scale
        row = lax.broadcasted_iota(jnp.int32, (rows, length), 0) + i * rows
        column = lax.broadcasted_iota(jnp.int32, (rows, length), 1)
        allowed = (seg_c[own] == seg_r[:, :length]) & (column <= row)
        scores = jnp.where(allowed, scores, NEGATIVE)
        top = jnp.max(scores, axis=1, keepdims=True)
        weights = jnp.exp(scores - top)
        total = jnp.sum(weights, axis=1, keepdims=True)
        out = mm(weights.astype(BF), v_ref[:length]) / total
        o_ref[own] = out.astype(BF)
        lse_ref[0, own] = top + jnp.log(total)


def attend(projected, rq, rk, gq, gk, cosine, sine, seg_c, seg_r):
    block = projected.shape[0]
    head = lambda off: pl.BlockSpec((block, HD), lambda h: (0, off + h))
    gain = pl.BlockSpec((1, HD), lambda h: (0, h))
    fixed = lambda shape: pl.BlockSpec(shape, lambda h: (0, 0))
    wide = jax.ShapeDtypeStruct((block, GROUP_WIDTH), BF)
    return pl.pallas_call(
        attend_kernel,
        grid=(HEADS,),
        out_shape=(wide, wide, wide, wide, jax.ShapeDtypeStruct((HEADS, block, 1), F32)),
        in_specs=[
            head(0),
            head(HEADS),
            head(2 * HEADS),
            fixed((block, 1)),
            fixed((block, 1)),
            gain,
            gain,
            fixed((block, HD)),
            fixed((block, HD)),
            fixed((block, 1)),
            fixed((1, block)),
        ],
        out_specs=[head(0)] * 4 + [pl.BlockSpec((1, block, 1), lambda h: (h, 0, 0))],
        compiler_params=pltpu.CompilerParams(vmem_limit_bytes=60 * 2**20),
        name="attend",
    )(projected, projected, projected, rq, rk, gq, gk, cosine, sine, seg_c, seg_r)


def attend_back_kernel(
    q_ref,
    k_ref,
    v_ref,
    g_ref,
    lse_ref,
    pq,
    pk,
    gq,
    gk,
    cosine,
    sine,
    seg_c,
    seg_r,
    uq_ref,
    uk_ref,
    dv_ref,
    mq_ref,
    mk_ref,
    dk_acc,
    dv_acc,
):
    block = q_ref.shape[0]
    rows = attention_rows(block)
    scale = HD**-0.5
    dk_acc[...] = jnp.zeros_like(dk_acc)
    dv_acc[...] = jnp.zeros_like(dv_acc)

    def back(grad, raw, gain):
        turned = turn(grad.astype(BF).astype(F32), cosine_of, -sine_of)
        return turned, jnp.sum(raw * gain[...] * turned, axis=1, keepdims=True)

    for i in range(block // rows):
        length = (i + 1) * rows
        own = slice(i * rows, length)
        scores = mm_t(q_ref[own], k_ref[:length]) * scale
        row = lax.broadcasted_iota(jnp.int32, (rows, length), 0) + i * rows
        column = lax.broadcasted_iota(jnp.int32, (rows, length), 1)
        allowed = (seg_c[own] == seg_r[:, :length]) & (column <= row)
        probs = jnp.where(allowed, jnp.exp(scores - lse_ref[0, own]), 0.0)
        grad_probs = mm_t(g_ref[own], v_ref[:length])
        delta = jnp.sum(probs * grad_probs, axis=1, keepdims=True)
        grad_scores = (probs * (grad_probs - delta)).astype(BF)
        grad_q = mm(grad_scores, k_ref[:length]) * scale
        cosine_of, sine_of = cosine[own], sine[own]
        turned, moment = back(grad_q, pq[own], gq)
        uq_ref[own] = turned
        mq_ref[0, own] = moment
        dk_acc[:length] += t_mm(grad_scores, q_ref[own])
        dv_acc[:length] += t_mm(probs.astype(BF), g_ref[own])
    cosine_of, sine_of = cosine[...], sine[...]
    turned, moment = back(dk_acc[...] * scale, pk[...], gk)
    uk_ref[...] = turned
    mk_ref[0] = moment
    dv_ref[...] = dv_acc[...].astype(BF)


def attend_back(q, k, v, grad, lse, projected, gq, gk, cosine, sine, seg_c, seg_r):
    block = q.shape[0]
    head = lambda off: pl.BlockSpec((block, HD), lambda h: (0, off + h))
    gain = pl.BlockSpec((1, HD), lambda h: (0, h))
    fixed = lambda shape: pl.BlockSpec(shape, lambda h: (0, 0))
    column = pl.BlockSpec((1, block, 1), lambda h: (h, 0, 0))
    wide = lambda t: jax.ShapeDtypeStruct((block, GROUP_WIDTH), t)
    moment = jax.ShapeDtypeStruct((HEADS, block, 1), F32)
    return pl.pallas_call(
        attend_back_kernel,
        grid=(HEADS,),
        out_shape=(wide(F32), wide(F32), wide(BF), moment, moment),
        in_specs=[
            head(0),
            head(0),
            head(0),
            head(0),
            column,
            head(0),
            head(HEADS),
            gain,
            gain,
            fixed((block, HD)),
            fixed((block, HD)),
            fixed((block, 1)),
            fixed((1, block)),
        ],
        out_specs=[head(0)] * 3 + [column] * 2,
        scratch_shapes=[VMEM((block, HD), F32), VMEM((block, HD), F32)],
        compiler_params=pltpu.CompilerParams(vmem_limit_bytes=60 * 2**20),
        name="attend_back",
    )(q, k, v, grad, lse, projected, projected, gq, gk, cosine, sine, seg_c, seg_r)


WEIGHTS = 6


def experts_kernel(
    experts,
    slots,
    x_ref,
    g_ref,
    *refs,
):
    hbm = refs[:WEIGHTS]
    out_ref, row_ref = refs[WEIGHTS : WEIGHTS + 2]
    gid, giu, god, gou = refs[WEIGHTS + 2 : WEIGHTS + 6]
    w_gu, w_d, w_id, w_iu, w_od, w_ou, sems = refs[WEIGHTS + 6 :]
    held = (w_gu, w_d, w_id, w_iu, w_od, w_ou)
    tile, e = pl.program_id(0), pl.program_id(1)
    last_tile = pl.num_programs(0) - 1
    sources, tok = x_ref.shape[0], x_ref.shape[1]
    extra = x_ref.shape[2] - MODEL_WIDTH

    def load(n, expert):
        return pltpu.make_async_copy(hbm[n].at[expert], held[n], sems.at[n])

    first = (tile == 0) & (e == 0)
    more = jnp.logical_not((tile == last_tile) & (e == EXP_DEV - 1))
    following = lax.rem(e + 1, EXP_DEV)

    @pl.when(first)
    def _():
        for n in range(WEIGHTS):
            load(n, 0).start()
        for ref in (gid, giu, god, gou):
            ref[...] = jnp.zeros_like(ref)

    def refill(*names):
        @pl.when(more)
        def _():
            for n in names:
                load(n, following).start()

    number = lax.axis_index("c") * (2 * EXP_DEV) + lax.axis_index("core") * EXP_DEV + e
    lane = lax.broadcasted_iota(jnp.int32, (tok, extra), 1)
    slot = lax.broadcasted_iota(jnp.int32, (tok, slots), 1).astype(F32)
    pick, gate = [], []
    rows, grads, masks = [], [], []
    for d in range(sources):
        side = x_ref[d, :, MODEL_WIDTH:].astype(F32)
        read = lambda which: jnp.sum(jnp.where(which, side, 0.0), axis=1, keepdims=True)
        place = read(lane == number)
        gate_d = read((lane == experts + number) | (lane == 2 * experts + number))
        chosen = read(lane == 3 * experts)
        columns = (lax.broadcasted_iota(jnp.int32, (tok, SPAN), 1) // ADAPTER_RANK).astype(F32)
        mask_d = jnp.where(columns == chosen, 1.0, 0.0).astype(BF)
        pick_d = jnp.where(slot == place, 1.0, 0.0).astype(BF)
        pick.append(pick_d)
        gate.append(gate_d)
        rows.append(t_mm(pick_d, x_ref[d, :, :MODEL_WIDTH]))
        grads.append(t_mm(pick_d, (gate_d * g_ref[d].astype(F32)).astype(BF)))
        masks.append(t_mm(pick_d, mask_d))
    x = jnp.concatenate(rows, axis=0).astype(BF)
    grad = jnp.concatenate(grads, axis=0).astype(BF)
    mask = jnp.concatenate(masks, axis=0)
    mask2 = jnp.concatenate([mask, mask], axis=1)
    for n in range(WEIGHTS):
        load(n, e).wait()
    lower_in = (mm(x, w_id[...]) * mask2).astype(BF)
    lower_g, lower_u = lower_in[:, :SPAN], lower_in[:, SPAN:]
    gate_part = mm(x, w_gu[:, :EXPERT_HIDDEN]) + mm(lower_g, w_iu[0])
    up_part = mm(x, w_gu[:, EXPERT_HIDDEN:]) + mm(lower_u, w_iu[1])
    sigmoid = 1.0 / (1.0 + jnp.exp(-gate_part))
    activated = gate_part * sigmoid
    hidden = (activated * up_part).astype(BF)
    lower_out = (mm(hidden, w_od[...]) * mask).astype(BF)
    result = (mm(hidden, w_d[...]) + mm(lower_out, w_ou[...])).astype(BF).astype(F32)
    moments = []
    for d in range(sources):
        back = mm(pick[d], result[d * slots : (d + 1) * slots].astype(BF))
        moments.append(jnp.sum(back * g_ref[d].astype(F32), axis=1, keepdims=True))
        back = back * gate[d]

        @pl.when(e == 0)
        def _():
            out_ref[d] = back.astype(BF)

        @pl.when(e > 0)
        def _():
            out_ref[d] = (out_ref[d].astype(F32) + back).astype(BF)

    grad_lower_out = (mm_t(grad, w_ou[...]) * mask).astype(BF)
    grad_hidden = mm_t(grad, w_d[...]) + mm_t(grad_lower_out, w_od[...])
    refill(1, 4, 5)
    grad_up = (grad_hidden * activated).astype(BF)
    grad_gate = (
        grad_hidden * up_part * sigmoid * (1.0 + gate_part * (1.0 - sigmoid))
    ).astype(BF)
    grad_lower_in = (
        jnp.concatenate([mm_t(grad_gate, w_iu[0]), mm_t(grad_up, w_iu[1])], axis=1) * mask2
    ).astype(BF)
    grad_rows = (
        mm_t(grad_gate, w_gu[:, :EXPERT_HIDDEN])
        + mm_t(grad_up, w_gu[:, EXPERT_HIDDEN:])
        + mm_t(grad_lower_in, w_id[...])
    ).astype(BF).astype(F32)
    refill(0, 2, 3)
    for d in range(sources):
        back = mm(pick[d], grad_rows[d * slots : (d + 1) * slots].astype(BF))
        high = moments[d].astype(BF).astype(F32)
        low = moments[d] - high
        side = jnp.where(lane == number, high, 0.0) + jnp.where(lane == experts + number, low, 0.0)

        @pl.when(e == 0)
        def _():
            row_ref[d, :, :MODEL_WIDTH] = back.astype(BF)
            row_ref[d, :, MODEL_WIDTH:] = side.astype(BF)

        @pl.when(e > 0)
        def _():
            row_ref[d, :, :MODEL_WIDTH] = (row_ref[d, :, :MODEL_WIDTH].astype(F32) + back).astype(BF)
            row_ref[d, :, MODEL_WIDTH:] = (row_ref[d, :, MODEL_WIDTH:].astype(F32) + side).astype(BF)

    gid[e] += t_mm(x, grad_lower_in)
    giu[e, 0] += t_mm(lower_g, grad_gate)
    giu[e, 1] += t_mm(lower_u, grad_up)
    god[e] += t_mm(hidden, grad_lower_out)
    gou[e] += t_mm(lower_out, grad)


def run_experts(x, g, weights, experts, slots):
    sources, tok, wide = x.shape
    pair = 2
    grid = (sources // pair, EXP_DEV)
    by_tile = lambda w: pl.BlockSpec((pair, tok, w), lambda t, e: (t, 0, 0))
    shapes = (
        (EXP_DEV, MODEL_WIDTH, 2 * SPAN),
        (EXP_DEV, 2, SPAN, EXPERT_HIDDEN),
        (EXP_DEV, EXPERT_HIDDEN, SPAN),
        (EXP_DEV, SPAN, MODEL_WIDTH),
    )
    whole = [
        pl.BlockSpec(s, lambda t, e, n=len(s): (0,) * n, pipeline_mode=pl.Buffered(1))
        for s in shapes
    ]
    flops = 2 * sources * EXP_DEV * slots * MODEL_WIDTH * EXPERT_HIDDEN * 8
    return pl.pallas_call(
        functools.partial(experts_kernel, experts, slots),
        grid=grid,
        out_shape=(
            jax.ShapeDtypeStruct((sources, tok, MODEL_WIDTH), BF),
            jax.ShapeDtypeStruct((sources, tok, wide), BF),
            *(jax.ShapeDtypeStruct(s, F32) for s in shapes),
        ),
        in_specs=[by_tile(wide), by_tile(MODEL_WIDTH)]
        + [pl.BlockSpec(memory_space=ANY)] * WEIGHTS,
        out_specs=[by_tile(MODEL_WIDTH), by_tile(wide), *whole],
        scratch_shapes=[VMEM(w.shape[1:], BF) for w in weights]
        + [pltpu.SemaphoreType.DMA((WEIGHTS,))],
        compiler_params=pltpu.CompilerParams(vmem_limit_bytes=63 * 2**20),
        cost_estimate=pl.CostEstimate(flops=flops, bytes_accessed=10**8, transcendentals=10**7),
        name="experts",
    )(x, g, *weights)


def on_device(
    tokens,
    cotangent,
    lengths,
    sets,
    routes,
    gain_attn,
    gain_query,
    gain_key,
    gain_mlp,
    query_key_value_weight,
    out_weight,
    router_weight,
    gate_up_weight,
    down_weight,
    attention_down_factors,
    attention_up_factors,
    router_down_factors,
    router_up_factors,
    expert_input_down,
    expert_input_up,
    expert_output_down,
    expert_output_up,
):
    zh, zl, c, core = here()
    n_c = lax.axis_size("c")
    n_fsdp = 2 * n_c
    n_seq = lax.axis_size("zh") * lax.axis_size("zl")
    tok = tokens.shape[1]
    block = tok * n_seq
    experts = EXP_DEV * n_fsdp
    capacity = 5 * tok * TOP // (4 * experts)
    slots = -(-capacity // 8) * 8
    extra = -(-(3 * experts + 1) // 128) * 128
    span3 = 3 * SPAN
    group = zl * 2 + core
    shard = zh * 2 + zl

    both_lengths = lax.all_gather(
        jnp.concatenate([lengths[0], sets[0]]), "core", axis=0, tiled=False
    )
    held_lengths = lax.dynamic_index_in_dim(both_lengths, zh, 0, keepdims=False)
    count = lengths.shape[1]

    inputs = tokens[0].astype(F32)
    normalized = rms_scale(inputs, gain_attn).astype(BF)
    x_shards, qkv_rows = gather_to_heads(normalized, query_key_value_weight, n_c)

    rows_local = query_key_value_weight.shape[0]
    factors = jnp.concatenate(
        [
            attention_down_factors,
            attention_up_factors.reshape(rows_local, -1),
            router_down_factors,
            router_weight,
            router_up_factors.reshape(rows_local, -1),
        ],
        axis=1,
    )
    factor_width = factors.shape[1]
    factors = jnp.pad(factors, ((0, 0), (0, -factor_width % 128)))
    factors = lax.all_gather(factors, FSDP, axis=0, tiled=True)
    up_columns = attention_up_factors.size // rows_local
    down_full = factors[:, : 4 * SPAN]
    at = 4 * SPAN
    up_full = factors[:, at : at + up_columns].reshape(4 * SPAN, MODEL_WIDTH)
    at += up_columns
    rdown_full = factors[:, at : at + SPAN]
    at += SPAN
    router_full = factors[:, at : at + experts]
    at += experts
    rup_full = factors[:, at:factor_width].reshape(SPAN, experts)
    out_full = lax.all_gather(out_weight, FSDP, axis=0, tiled=True)
    grad_rows_all = lax.all_gather(cotangent[0], FSDP, axis=0, tiled=True)

    seq_local, _, chosen = token_meta(
        lengths[0], sets[0], shard * tok + jnp.arange(tok, dtype=jnp.int32)
    )
    mask = set_mask(chosen)
    seq_block, block_offsets, block_sets = token_meta(
        held_lengths[:count], held_lengths[count:], jnp.arange(block, dtype=jnp.int32)
    )
    mask3 = jnp.tile(set_mask(block_sets), (1, 3))
    half = HD // 2
    freqs = THETA ** (-(jnp.arange(half, dtype=F32) * 2.0 / HD))
    angles = block_offsets.astype(F32)[:, None] * freqs[None, :]
    cosine, sine = jnp.cos(angles), jnp.sin(angles)
    cosine = jnp.concatenate([cosine, cosine], axis=1)
    sine = jnp.concatenate([-sine, sine], axis=1)
    seg_c, seg_r = seq_block[:, None], seq_block[None, :]

    x_all = x_shards.reshape(block, MODEL_WIDTH)
    down3 = down_full[:, :span3]
    lowered = (mm(x_all, down3) * mask3).astype(BF)
    up_own = lax.dynamic_slice_in_dim(up_full[:span3], group * GROUP_WIDTH, GROUP_WIDTH, 1)
    none = jnp.zeros((SPAN, GROUP_WIDTH), BF)
    up_diagonal = jnp.concatenate(
        [
            jnp.concatenate(
                [up_own[j * SPAN : (j + 1) * SPAN] if i == j else none for i in range(3)], axis=1
            )
            for j in range(3)
        ],
        axis=0,
    )
    projected = mm(x_all, qkv_rows) + mm(lowered, up_diagonal)
    part_q, part_k = projected[:, :GROUP_WIDTH], projected[:, GROUP_WIDTH : 2 * GROUP_WIDTH]

    def over_group(first, second, identity):
        both = jnp.stack([first, second]).reshape(-1, 128)
        return group_sum(both, identity).reshape(2, block)

    squares = over_group(jnp.sum(part_q * part_q, axis=1), jnp.sum(part_k * part_k, axis=1), 4)
    inverse = lax.rsqrt(squares / MODEL_WIDTH + EPSILON)
    rq, rk = inverse[0][:, None], inverse[1][:, None]
    gains = [
        lax.dynamic_slice_in_dim(g, group * GROUP_WIDTH, GROUP_WIDTH)[None, :]
        for g in (gain_query, gain_key)
    ]
    q, k, v, attended_heads, lse = attend(
        projected, rq, rk, *gains, cosine, sine, seg_c, seg_r
    )
    attended = to_tokens(attended_heads.reshape(4, tok, GROUP_WIDTH))

    down_o, up_o = down_full[:, span3:], up_full[span3:]
    out_lower = (mm(attended, down_o) * mask).astype(BF)
    branch = mm(attended, out_full) + mm(out_lower, up_o)
    middle = inputs + branch
    normed2 = rms_scale(middle, gain_mlp).astype(BF)
    router_lower = (mm(normed2, rdown_full) * mask).astype(BF)
    logits = mm(normed2, router_full) + mm(router_lower, rup_full)
    probs = jax.nn.softmax(logits, axis=-1)
    hits = jnp.sum(
        (routes[0][:, :, None] == jnp.arange(experts, dtype=jnp.int32)[None, None, :]).astype(F32),
        axis=1,
    )
    place = jnp.arange(tok, dtype=jnp.int32)
    before = (place[None, :] < place[:, None]).astype(BF)
    ranks = jnp.where(hits > 0, mm(before, hits.astype(BF)), -1.0).astype(BF)
    gates = hits * probs
    gates_high = gates.astype(BF)
    gates_low = (gates - gates_high.astype(F32)).astype(BF)
    side = jnp.concatenate(
        [ranks, gates_high, gates_low, chosen.astype(BF)[:, None]], axis=1
    )
    payload = jnp.concatenate(
        [normed2, jnp.pad(side, ((0, 0), (0, extra - side.shape[1])))], axis=1
    )
    rows_all = lax.all_gather(payload, FSDP, axis=0, tiled=True)
    weights = (
        gate_up_weight,
        down_weight,
        expert_input_down,
        expert_input_up,
        expert_output_down,
        expert_output_up,
    )
    out_parts, row_parts, *expert_terms = run_experts(
        rows_all.reshape(n_fsdp, tok, MODEL_WIDTH + extra),
        grad_rows_all.reshape(n_fsdp, tok, MODEL_WIDTH),
        weights,
        experts,
        slots,
    )
    returned = lax.psum_scatter(
        row_parts.reshape(n_fsdp * tok, -1), FSDP, scatter_dimension=0, tiled=True
    )
    mixed = lax.psum_scatter(
        out_parts.reshape(n_fsdp * tok, -1), FSDP, scatter_dimension=0, tiled=True
    )
    output = (middle + mixed.astype(F32)).astype(BF)

    grad_out = cotangent[0].astype(F32)
    returned = returned.astype(F32)
    back = returned[:, MODEL_WIDTH:]
    grad_probs = back[:, :experts] + back[:, experts : 2 * experts]
    grad_logits = probs * (grad_probs - jnp.sum(probs * grad_probs, axis=-1, keepdims=True))
    grad_router_lower = exact("te,re->tr", grad_logits, rup_full.astype(F32)) * mask
    grad_normed2 = (
        returned[:, :MODEL_WIDTH]
        + mm_t(grad_logits.astype(BF), router_full)
        + mm_t(grad_router_lower.astype(BF), rdown_full)
    )
    grad_rup = t_mm(router_lower, grad_logits.astype(BF))
    grad_rdown = t_mm(normed2, grad_router_lower.astype(BF))
    grad_middle = grad_out + rms_back(middle, gain_mlp, grad_normed2)
    grad_branch = grad_middle.astype(BF)
    grad_out_lower = (mm_t(grad_branch, up_o) * mask).astype(BF)
    grad_attended = (mm_t(grad_branch, out_full) + mm_t(grad_out_lower, down_o)).astype(BF)
    head_grad = to_heads(grad_attended).reshape(block, GROUP_WIDTH)
    grad_up_o = t_mm(out_lower, grad_branch)
    grad_down_o = t_mm(attended, grad_out_lower)

    uq, uk, grad_v, mq, mk = attend_back(
        q, k, v, head_grad, lse, projected, *gains, cosine, sine, seg_c, seg_r
    )
    moments = over_group(jnp.sum(mq[..., 0], axis=0), jnp.sum(mk[..., 0], axis=0), 5) / MODEL_WIDTH

    def rms_inner(values, scale, gain, turned, moment):
        return (scale * gain * turned - values * (scale * scale * scale) * moment).astype(BF)

    grad_projected = jnp.concatenate(
        [
            rms_inner(part_q, rq, gains[0], uq, moments[0][:, None]),
            rms_inner(part_k, rk, gains[1], uk, moments[1][:, None]),
            grad_v,
        ],
        axis=1,
    )
    grad_lowered = (mm_t(grad_projected, up_diagonal) * mask3).astype(BF)
    grad_up_own = [
        t_mm(
            lowered[:, j * SPAN : (j + 1) * SPAN],
            grad_projected[:, j * GROUP_WIDTH : (j + 1) * GROUP_WIDTH],
        )
        for j in range(3)
    ]
    grad_down_qkv = t_mm(x_all, grad_lowered)
    grad_normed_part = (mm_t(grad_projected, qkv_rows) + mm_t(grad_lowered, down3)).astype(BF)
    grad_normed = sum_to_tokens(grad_normed_part.reshape(4, tok, MODEL_WIDTH))
    grad_inputs = grad_middle + rms_back(inputs, gain_attn, grad_normed)

    grad_down_all = jnp.concatenate([grad_down_qkv, grad_down_o], axis=1).astype(BF)
    wide_up = lax.dynamic_update_slice_in_dim(
        jnp.zeros((span3, MODEL_WIDTH), F32),
        jnp.concatenate(grad_up_own, axis=0),
        group * GROUP_WIDTH,
        1,
    )
    grad_up_all = jnp.concatenate([wide_up, grad_up_o], axis=0).astype(BF)
    terms = (grad_down_all, grad_up_all, grad_rdown.astype(BF), grad_rup.astype(BF))
    own_shapes = [(t.shape[0] // (n_seq * n_fsdp), t.shape[1]) for t in terms]
    flat = jnp.concatenate(
        [t.reshape(n_seq, n_fsdp, -1).transpose(1, 0, 2) for t in terms], axis=2
    )
    used = flat.shape[2]
    flat = jnp.pad(flat, ((0, 0), (0, 0), (0, -used % 1024))).reshape(n_fsdp * n_seq, -1, 128)
    flat = lax.psum_scatter(flat, FSDP, scatter_dimension=0, tiled=True)
    flat = lax.psum_scatter(flat, SEQ, scatter_dimension=0, tiled=True).astype(F32).reshape(-1)
    summed, at = [], 0
    for shape in own_shapes:
        size = shape[0] * shape[1]
        summed.append(flat[at : at + size].reshape(shape))
        at += size
    expert_sums = [
        lax.psum_scatter(t.astype(BF), SEQ, scatter_dimension=d, tiled=True).astype(F32)
        for t, d in zip(expert_terms, (1, 3, 1, 2), strict=True)
    ]
    return (output[None], grad_inputs[None], *summed, *expert_sums)


def solution(mesh):
    n_seq, n_fsdp = mesh.shape["seq"], mesh.shape["fsdp"]
    fine = Mesh(
        mesh.devices.reshape(2, n_seq // 2, n_fsdp // 2, 2), ("zh", "zl", "c", "core")
    )
    split = P(FSDP, SEQ, None)
    rows = P(FSDP, None)
    three = P(FSDP, None, None)
    in_specs = (
        split,
        split,
        rows,
        rows,
        split,
        P(),
        P(),
        P(),
        P(),
        rows,
        rows,
        rows,
        three,
        three,
        rows,
        rows,
        rows,
        rows,
        three,
        P(FSDP, None, None, None),
        three,
        three,
    )
    owners = P((*SEQ, *FSDP), None)
    out_specs = (
        split,
        split,
        owners,
        owners,
        owners,
        owners,
        split,
        P(FSDP, None, None, SEQ),
        split,
        P(FSDP, None, SEQ),
    )
    return jax.shard_map(
        on_device, mesh=fine, in_specs=in_specs, out_specs=out_specs, check_vma=False
    )
```

time: 2090 us -> 1030 us (0.49); the launches traced: 2060 us -> 1030 us
  Pallas kernels: 0 us -> 550 us
  waiting for transfers between devices: 780 us -> 251 us
  matrix products: 466 us -> 80.9 us
  local copies, waits for them, and re-layouts: 368 us -> 66.5 us
  blocking collectives: 178 us -> 2.15 us
  starting transfers between devices: 104 us -> 0.49 us
  other arithmetic: 136 us -> 54 us
    pallas_call x0 -> x9, Pallas kernels: none -> 550 us  [the longest x1 251 us: run_experts(): pl.pallas_call(functools.partial(experts_kernel, experts, slots), grid=gr...]
    dot_general x63 -> x27, matrix products: 466 us -> 80.9 us  [the longest x8 38.4 us: mm_t(): lax.dot_general(left, right, (((1,), (1,)), ((), ())), preferred_element_...]
    all_to_all x13 -> x0, waiting for transfers between devices: 350 us -> none  [the longest x1 74.9 us: on_device(): lax.all_to_all(result, 'fsdp', split_axis=1, concat_axis=1, tiled=True)]
    unnamed x12 -> x13, waiting for transfers between devices: 143 us -> 2.04 us
    all_gather x3 -> x0, blocking collectives: 135 us -> none  [the longest x1 117 us: on_device(): lax.all_gather(router_up_factors, 'fsdp', axis=0, tiled=True)]
    gather x6 -> x0, local copies, waits for them, and re-layouts: 129 us -> none  [the longest x1 26.6 us: on_device(): returned_buffer.reshape(buffer_size, MODEL_WIDTH)[slots]]
    all_to_all x13 -> x0, starting transfers between devices: 102 us -> none  [the longest x1 16.9 us: on_device(): lax.all_to_all(grad_q_heads.astype(jnp.bfloat16), 'seq', split_axis=0, co...]
    all_gather x4, waiting for transfers between devices: 168 us -> 66.3 us  [the longest x1 66.2 us: on_device(): rows_all = lax.all_gather(payload, FSDP, axis=0, tiled=True)]
  transfers between devices with their start and end apart: 24 -> 12, of which waited for: 15 -> 4; matrix products, arithmetic and copies ran while one was open for 38% -> 18% of each run, Pallas kernels for 0% -> 29%
where the time goes in v1:
time: 1030 us
  Pallas kernels  550 us (53%)
  waiting for transfers between devices  251 us (24%)
  matrix products  80.9 us (8%)
  local copies, waits for them, and re-layouts  66.5 us (6%)
  other arithmetic  54 us (5%)
  between operations  20.3 us (2%)
    pallas_call x1, Pallas kernels, run_experts(): pl.pallas_call(functools.partial(experts_kernel, experts, slots), grid=gr...  251 us
    pallas_call x1, Pallas kernels, gather_to_heads(): pl.pallas_call(functools.partial(gather_kernel, n_c), out_shape=(jax.Shap...  92.6 us
    reduce_scatter x1, waiting for transfers between devices, on_device(): lax.psum_scatter(out_parts.reshape(n_fsdp * tok, -1), FSDP, scatter_dimen...  78 us
    reduce_scatter x1, waiting for transfers between devices, on_device(): lax.psum_scatter(row_parts.reshape(n_fsdp * tok, -1), FSDP, scatter_dimen...  74.1 us
    pallas_call x1, Pallas kernels, sum_to_tokens(): pl.pallas_call(sum_to_tokens_kernel, out_shape=jax.ShapeDtypeStruct((tok,...  69.2 us
    all_gather x1, waiting for transfers between devices, on_device(): rows_all = lax.all_gather(payload, FSDP, axis=0, tiled=True)  66.2 us
    pallas_call x1, Pallas kernels, to_heads(): pl.pallas_call(to_heads_kernel, out_shape=jax.ShapeDtypeStruct((4, tok, G...  49.2 us
    dot_general x8, matrix products, mm_t(): lax.dot_general(left, right, (((1,), (1,)), ((), ())), preferred_element_...  38.4 us
  transfers between devices with their start and end apart: 12, of which 4 were waited for; matrix products, arithmetic and copies ran while one was open for 18% of the time, Pallas kernels for 29%

profile of v1, /device:TPU:9, one launch (start us, length us, event | category | flops | bytes accessed | tf_op | source)
XLA Modules:
  0.0 1025.7 jit_solution(17542687003414500309)
XLA Ops:
  34.7 92.6 %gather_to_heads.1 = (bf16[4,320,2048]{2,1,0:T(8,128)(2,1)}, bf16[2048,1536]{1,0:T(8,128)(2,1)}) custom-call(bf16[320,2048]{1,0:T(8,128)(2,1)} %fusion.6.x_ref, bf16[256,6144]{1,0:T(8,128)(2,1)} %w_ref.1), custom_call_target="tpu_custom_call" | custom-call | tf_op jit(solution)/shard_map/gather_to_heads/pallas_call | solution.py:192
  132.0 12.4 %fusion.67 = f32[1280,1536]{1,0:T(8,128)} fusion(bf16[1280,2048]{1,0:T(8,128)(2,1)S(1)} %bitcast.129, bf16[2048,1536]{1,0:T(8,128)(2,1)} %get-tuple-element.29), kind=kOutput, calls=%fused_computation.164 | convolution fusion | flops 8053063680 | bytes 19398656 | tf_op jit(solution)/shard_map/dot_general | solution.py:35
  145.9 2.5 slice.150
  149.6 6.9 fusion.3
  158.6 3.1 copy-done
  162.8 4.8 group_sum.2
  171.1 21.6 %attend.1 = (bf16[1280,512]{1,0:T(8,128)(2,1)}, bf16[1280,512]{1,0:T(8,128)(2,1)}, bf16[1280,512]{1,0:T(8,128)(2,1)}, bf16[1280,512]{1,0:T(8,128)(2,1)}, f32[4,1280,1]{2,1,0:T(8,128)}) custom-call(f32[1280,1536]{1,0:T(8,128)} %copy-done, f32[1280,1536]{1,0:T(8,128)} %copy-done, f32[1280,1536]{1,0:T(8,128)} %copy-done, f32[1280,1]{1,0:T(8,128)} %bitcast.113, ...), custom_call_target="tpu_custom_call" | custom-call | tf_op jit(solution)/shard_map/attend/pallas_call | solution.py:427
  192.8 32.7 %to_tokens.1 = bf16[320,2048]{1,0:T(8,128)(2,1)} custom-call(bf16[4,320,512]{2,1,0:T(8,128)(2,1)} %bitcast.116), custom_call_target="tpu_custom_call" | custom-call | tf_op jit(solution)/shard_map/to_tokens/pallas_call | solution.py:246
  232.0 5.3 fusion.68
  244.5 66.2 %all-gather.11.cloned.1.call-done = bf16[2560,2176]{1,0:T(8,128)(2,1)} async-done(((bf16[320,2176]{1,0:T(8,128)(2,1)}), bf16[2560,2176]{1,0:T(8,128)(2,1)}) %all-gather.11.cloned.1.call-update) | async-done | bytes 11141136 | tf_op jit(solution)/shard_map/all_gather | solution.py:851
  310.8 250.9 %experts.1 = (bf16[8,320,2048]{2,1,0:T(8,128)(2,1)}, bf16[8,320,2176]{2,1,0:T(8,128)(2,1)}, f32[2,2048,256]{2,1,0:T(8,128)}, f32[2,2,128,1024]{3,2,1,0:T(8,128)}...) custom-call(bf16[8,320,2176]{2,1,0:T(8,128)(2,1)} %bitcast.126, bf16[8,320,2048]{2,1,0:T(8,128)(2,1)} %bitcast.127, ...), custom_call_target="tpu_custom_call" | custom-call | flops 107374182400 | bytes 100000000 | tf_op jit(solution)/shard_map/experts/pallas_call | solution.py:684
  563.9 2.9 convert_element_type.198
  568.1 3.9 convert_element_type.196
  572.1 74.1 %reduce-scatter.13.cloned.1.call-done = bf16[320,2176]{1,0:T(8,128)(2,1)} async-done(((bf16[2560,2176]{1,0:T(8,128)(2,1)}), bf16[320,2176]{1,0:T(8,128)(2,1)}) %reduce-scatter.13.cloned.1.call-update) | async-done | bytes 1392656 | tf_op jit(solution)/shard_map/reduce_scatter | solution.py:867
  650.3 3.1 multiply_reduce_fusion
  653.4 78.0 %reduce-scatter.11.cloned.1.call-done = bf16[320,2048]{1,0:T(8,128)(2,1)} async-done(((bf16[2560,2048]{1,0:T(8,128)(2,1)}), bf16[320,2048]{1,0:T(8,128)(2,1)}) %reduce-scatter.11.cloned.1.call-update) | async-done | bytes 1310736 | tf_op jit(solution)/shard_map/reduce_scatter | solution.py:870
  731.5 5.5 convert_add_fusion.1
  739.6 5.4 fusion.58
  745.0 2.7 fusion.5.a_ref
  747.7 49.2 %to_heads.1 = bf16[4,320,512]{2,1,0:T(8,128)(2,1)} custom-call(bf16[320,2048]{1,0:T(8,128)(2,1)} %fusion.5.a_ref), custom_call_target="tpu_custom_call" | custom-call | tf_op jit(solution)/shard_map/to_heads/pallas_call | solution.py:287
  796.8 24.5 %attend_back.1 = (f32[1280,512]{1,0:T(8,128)}, f32[1280,512]{1,0:T(8,128)}, bf16[1280,512]{1,0:T(8,128)(2,1)}, f32[4,1280,1]{2,1,0:T(8,128)}, f32[4,1280,1]{2,1,0:T(8,128)}) custom-call(bf16[1280,512]{1,0:T(8,128)(2,1)} %get-tuple-element.33.q_ref, bf16[1280,512]{1,0:T(8,128)(2,1)} %get-tuple-element.34.k_ref, bf16[1280,512]{1,0:T(8,128)(2,1)} %get-tuple-element.35.v_ref, ...), custom_call_target="tpu_custom_call" | custom-call | tf_op jit(solution)/shard_map/attend_back/pallas_call | solution.py:515
  826.1 4.8 group_sum.3
  831.7 5.3 subtract_convert_fusion.1
  849.6 4.0 copy.120
  853.6 4.3 convert_element_type.191
  859.6 4.2 convert_element_type.192
  869.5 4.0 pad.16.clone
  873.6 7.6 reshape.306
  888.6 15.0 %fusion.16 = f32[1280,2048]{1,0:T(8,128)} fusion(bf16[2048,1536]{1,0:T(8,128)(2,1)} %get-tuple-element.29, bf16[1280,512]{1,0:T(8,128)(2,1)} %get-tuple-element.41, bf16[1280,512]{1,0:T(8,128)(2,1)} %copy-done.8, bf16[1280,512]{1,0:T(8,128)(2,1)} %copy-done.7), kind=kOutput, calls=%fused_computation.47 | convolution fusion | flops 8064860160 | bytes 20709376 | tf_op jit(solution)/shard_map/dot_general | solution.py:39
  903.5 30.8 %reduce-scatter.15.cloned.1.call-done = bf16[4,584,128]{2,1,0:T(8,128)(2,1)} async-done(((bf16[32,584,128]{2,1,0:T(8,128)(2,1)}), bf16[4,584,128]{2,1,0:T(8,128)(2,1)}) %reduce-scatter.15.cloned.1.call-update) | async-done | bytes 598032 | tf_op jit(solution)/shard_map/reduce_scatter | solution.py:940
  934.3 7.7 add_convert_fusion
  942.1 69.2 %sum_to_tokens.1 = f32[320,2048]{1,0:T(8,128)S(1)} custom-call(bf16[4,320,2048]{2,1,0:T(8,128)(2,1)S(1)} %bitcast.104), custom_call_target="tpu_custom_call" | custom-call | tf_op jit(solution)/shard_map/sum_to_tokens/pallas_call | solution.py:342
  (286 shorter events, 100.6 us)
Async XLA Ops:
  7.2 137.2 %all-gather.7.cloned.1.call-start = ((), (), s32[]{:S(2)}) async-start(), calls=%async_computation.8 | async-start | bytes 5898240 | tf_op jit(solution)/shard_map/all_gather | solution.py:764
  12.0 219.9 %all-gather.9.cloned.1.call-start = ((), (), s32[]{:S(2)}) async-start(), calls=%async_computation.9 | async-start | bytes 9437184 | tf_op jit(solution)/shard_map/all_gather | solution.py:775
  12.8 231.7 %all-gather.13.cloned.1.call-start = ((), (), s32[]{:S(2)}) async-start(), calls=%async_computation.18 | async-start | bytes 11796480 | tf_op jit(solution)/shard_map/all_gather | solution.py:776
  13.5 297.2 %all-gather.11.cloned.1.call-start = ((), (), s32[]{:S(2)}) async-start(), calls=%async_computation.10 | async-start | bytes 12533760 | tf_op jit(solution)/shard_map/all_gather | solution.py:851
  23.8 9.0 copy-start.3
  23.8 9.4 copy-start.40
  32.6 207.8 %copy-start.44 = (s32[320]{0:T(512)}, s32[320]{0:T(512)S(1)}, u32[]{:S(2)}) copy-start(s32[320]{0:T(512)S(1)} %select_reduce_fusion.3) | copy-start | bytes 3844
  33.2 94.0 %copy-start.49 = (f32[320]{0:T(512)}, f32[320]{0:T(512)S(1)}, u32[]{:S(2)}) copy-start(f32[320]{0:T(512)S(1)} %add_rsqrt_fusion.2) | copy-start | bytes 3844
  148.4 8.2 slice-start
  168.3 24.5 %copy-start.37 = (f32[20,128]{1,0:T(8,128)}, f32[20,128]{1,0:T(8,128)S(1)}, u32[]{:S(2)}) copy-start(f32[20,128]{1,0:T(8,128)S(1)} %add_rsqrt_fusion) | copy-start | bytes 30724
  192.8 37.6 %copy-start.56 = (s32[128]{0:T(128)S(1)}, s32[128]{0:T(128)}, u32[]{:S(2)}) copy-start(s32[128]{0:T(128)} %copy-done.55) | copy-start | bytes 1540
  230.3 11.7 %copy-start.35 = (bf16[128,16]{1,0:T(8,128)(2,1)}, bf16[128,16]{1,0:T(8,128)(2,1)S(1)}, u32[]{:S(2)}) copy-start(bf16[128,16]{1,0:T(8,128)(2,1)S(1)} %reshape.296) | copy-start | bytes 12292
  244.4 401.7 %reduce-scatter.13.cloned.1.call-start = ((), (), s32[]{:S(2)}) async-start(), calls=%async_computation.12 | async-start | bytes 12533760 | tf_op jit(solution)/shard_map/reduce_scatter | solution.py:867
  561.7 169.8 %reduce-scatter.11.cloned.1.call-start = ((), (), s32[]{:S(2)}) async-start(), calls=%async_computation.11 | async-start | bytes 11796480 | tf_op jit(solution)/shard_map/reduce_scatter | solution.py:870
  562.3 319.0 %reduce-scatter.21.cloned.1.call-start = ((), (), s32[]{:S(2)}) async-start(), calls=%async_computation.16 | async-start | bytes 655360 | tf_op jit(solution)/shard_map/reduce_scatter | solution.py:948
  563.9 319.0 %reduce-scatter.19.cloned.1.call-start = ((), (), s32[]{:S(2)}) async-start(), calls=%async_computation.15 | async-start | bytes 1310720 | tf_op jit(solution)/shard_map/reduce_scatter | solution.py:948
  566.8 317.9 %reduce-scatter.23.cloned.1.call-start = ((), (), s32[]{:S(2)}) async-start(), calls=%async_computation.17 | async-start | bytes 1310720 | tf_op jit(solution)/shard_map/reduce_scatter | solution.py:948
  568.0 318.5 %reduce-scatter.17.cloned.1.call-start = ((), (), s32[]{:S(2)}) async-start(), calls=%async_computation.14 | async-start | bytes 2621440 | tf_op jit(solution)/shard_map/reduce_scatter | solution.py:948
  572.0 76.1 %copy-start.36 = (bf16[128,16]{1,0:T(8,128)(2,1)S(1)}, bf16[128,16]{1,0:T(8,128)(2,1)}, u32[]{:S(2)}) copy-start(bf16[128,16]{1,0:T(8,128)(2,1)} %copy-done.35) | copy-start | bytes 12292
  572.0 76.1 %copy-start.45 = (s32[320]{0:T(512)S(1)}, s32[320]{0:T(512)}, u32[]{:S(2)}) copy-start(s32[320]{0:T(512)} %copy-done.44) | copy-start | bytes 3844
  572.0 76.1 %copy-start.57 = (s32[128]{0:T(128)S(1)}, s32[128]{0:T(128)}, u32[]{:S(2)}) copy-start(s32[128]{0:T(128)} %copy-done.55) | copy-start | bytes 1540
  572.0 362.3 %reduce-scatter.15.cloned.1.call-start = ((), (), s32[]{:S(2)}) async-start(), calls=%async_computation.13 | async-start | bytes 5382144 | tf_op jit(solution)/shard_map/reduce_scatter | solution.py:940
  650.3 81.2 %copy-start.52 = (f32[320]{0:T(512)S(1)}, f32[320]{0:T(512)}, u32[]{:S(2)}) copy-start(f32[320]{0:T(512)} %copy-done.51) | copy-start | bytes 3844
  821.3 10.3 %copy-start.42 = (f32[512]{0:T(512)S(1)}, f32[512]{0:T(512)}, u32[]{:S(2)}) copy-start(f32[512]{0:T(512)} %dynamic_slice.15) | copy-start | bytes 6148
  821.4 10.2 copy-start.43
  821.4 10.2 copy-start.46
  821.4 10.2 copy-start.47
  831.6 7.5 copy-start.25
  837.0 8.6 slice-start.2
  881.2 133.0 %reduce-scatter.25.cloned.1.call-start = ((), (), s32[]{:S(2)}) async-start(), calls=%async_computation.19 | async-start | bytes 747520
  942.0 69.2 %copy-start.4 = (bf16[1,320,2048]{2,1,0:T(8,128)(2,1)S(1)}, bf16[1,320,2048]{2,1,0:T(8,128)(2,1)}, u32[]{:S(2)}) copy-start(bf16[1,320,2048]{2,1,0:T(8,128)(2,1)} %param.22) | copy-start | bytes 3932164
  942.1 69.2 %copy-start.41 = (f32[2048]{0:T(1024)S(1)}, f32[2048]{0:T(1024)}, u32[]{:S(2)}) copy-start(f32[2048]{0:T(1024)} %param.27) | copy-start | bytes 24580
  (45 other events, 161.9 us)
Sparse Core Ops, SparseCore 0:
  12.2 89.6 all-gather.6
  103.8 60.2 all-gather.8
  166.0 63.2 all-gather.12
  244.6 66.1 all-gather.10
  561.8 84.2 reduce-scatter.12
  649.9 81.5 reduce-scatter.10
  733.9 17.7 reduce-scatter.20
  754.6 44.3 reduce-scatter.18
  801.3 24.4 reduce-scatter.22
  828.1 42.1 reduce-scatter.16
  881.3 52.9 reduce-scatter.14
  936.6 50.7 reduce-scatter.24

commit v2 on v1

--- a/solution.py
+++ b/solution.py
@@ -157,7 +157,6 @@
     mine = pl.ds(pl.multiple_of(core * half, half), half)
     theirs = pl.ds(pl.multiple_of((1 - core) * half, half), half)
     sibling = (zh, zl, c, 1 - core)
-    order = [zl ^ 0, zl ^ 1]
     for s in range(4):
         pltpu.make_async_copy(xg_ref.at[s, mine], xg_ref.at[s, mine], xr.at[s]).wait()
         remote(xg_ref.at[s, mine], xg_ref.at[s, mine], fs.at[s], fr.at[s], sibling).start()
@@ -195,7 +194,7 @@
             jax.ShapeDtypeStruct((4, tok, MODEL_WIDTH), BF),
             jax.ShapeDtypeStruct((n_f * rows, 3 * GROUP_WIDTH), BF),
         ),
-        in_specs=[pl.BlockSpec(memory_space=ANY)] * 2,
+        in_specs=[pl.BlockSpec(memory_space=VMEM)] * 2,
         out_specs=[pl.BlockSpec(memory_space=ANY)] * 2,
         scratch_shapes=[
             dma((2, 2)),
@@ -246,7 +245,7 @@
     return pl.pallas_call(
         to_tokens_kernel,
         out_shape=jax.ShapeDtypeStruct((tok, MODEL_WIDTH), BF),
-        in_specs=[pl.BlockSpec(memory_space=ANY)],
+        in_specs=[pl.BlockSpec(memory_space=VMEM)],
         out_specs=pl.BlockSpec(memory_space=ANY),
         scratch_shapes=[dma((4,)), dma((4,))],
         compiler_params=pltpu.CompilerParams(collective_id=1, has_side_effects=True),
@@ -287,7 +286,7 @@
     return pl.pallas_call(
         to_heads_kernel,
         out_shape=jax.ShapeDtypeStruct((4, tok, GROUP_WIDTH), BF),
-        in_specs=[pl.BlockSpec(memory_space=ANY)],
+        in_specs=[pl.BlockSpec(memory_space=VMEM)],
         out_specs=pl.BlockSpec(memory_space=ANY),
         scratch_shapes=[dma((4,)), dma((4,))],
         compiler_params=pltpu.CompilerParams(collective_id=2, has_side_effects=True),
@@ -538,166 +537,487 @@
     )(q, k, v, grad, lse, projected, projected, gq, gk, cosine, sine, seg_c, seg_r)
 
 
-WEIGHTS = 6
-
-
-def experts_kernel(
-    experts,
-    slots,
-    x_ref,
-    g_ref,
-    *refs,
-):
-    hbm = refs[:WEIGHTS]
-    out_ref, row_ref = refs[WEIGHTS : WEIGHTS + 2]
-    gid, giu, god, gou = refs[WEIGHTS + 2 : WEIGHTS + 6]
-    w_gu, w_d, w_id, w_iu, w_od, w_ou, sems = refs[WEIGHTS + 6 :]
-    held = (w_gu, w_d, w_id, w_iu, w_od, w_ou)
-    tile, e = pl.program_id(0), pl.program_id(1)
-    last_tile = pl.num_programs(0) - 1
-    sources, tok = x_ref.shape[0], x_ref.shape[1]
-    extra = x_ref.shape[2] - MODEL_WIDTH
-
-    def load(n, expert):
-        return pltpu.make_async_copy(hbm[n].at[expert], held[n], sems.at[n])
-
-    first = (tile == 0) & (e == 0)
-    more = jnp.logical_not((tile == last_tile) & (e == EXP_DEV - 1))
-    following = lax.rem(e + 1, EXP_DEV)
-
-    @pl.when(first)
-    def _():
-        for n in range(WEIGHTS):
-            load(n, 0).start()
-        for ref in (gid, giu, god, gou):
-            ref[...] = jnp.zeros_like(ref)
-
-    def refill(*names):
-        @pl.when(more)
-        def _():
-            for n in names:
-                load(n, following).start()
-
-    number = lax.axis_index("c") * (2 * EXP_DEV) + lax.axis_index("core") * EXP_DEV + e
-    lane = lax.broadcasted_iota(jnp.int32, (tok, extra), 1)
-    slot = lax.broadcasted_iota(jnp.int32, (tok, slots), 1).astype(F32)
-    pick, gate = [], []
-    rows, grads, masks = [], [], []
-    for d in range(sources):
-        side = x_ref[d, :, MODEL_WIDTH:].astype(F32)
-        read = lambda which: jnp.sum(jnp.where(which, side, 0.0), axis=1, keepdims=True)
-        place = read(lane == number)
-        gate_d = read((lane == experts + number) | (lane == 2 * experts + number))
-        chosen = read(lane == 3 * experts)
-        columns = (lax.broadcasted_iota(jnp.int32, (tok, SPAN), 1) // ADAPTER_RANK).astype(F32)
-        mask_d = jnp.where(columns == chosen, 1.0, 0.0).astype(BF)
-        pick_d = jnp.where(slot == place, 1.0, 0.0).astype(BF)
-        pick.append(pick_d)
-        gate.append(gate_d)
-        rows.append(t_mm(pick_d, x_ref[d, :, :MODEL_WIDTH]))
-        grads.append(t_mm(pick_d, (gate_d * g_ref[d].astype(F32)).astype(BF)))
-        masks.append(t_mm(pick_d, mask_d))
-    x = jnp.concatenate(rows, axis=0).astype(BF)
-    grad = jnp.concatenate(grads, axis=0).astype(BF)
-    mask = jnp.concatenate(masks, axis=0)
-    mask2 = jnp.concatenate([mask, mask], axis=1)
-    for n in range(WEIGHTS):
-        load(n, e).wait()
-    lower_in = (mm(x, w_id[...]) * mask2).astype(BF)
-    lower_g, lower_u = lower_in[:, :SPAN], lower_in[:, SPAN:]
-    gate_part = mm(x, w_gu[:, :EXPERT_HIDDEN]) + mm(lower_g, w_iu[0])
-    up_part = mm(x, w_gu[:, EXPERT_HIDDEN:]) + mm(lower_u, w_iu[1])
-    sigmoid = 1.0 / (1.0 + jnp.exp(-gate_part))
-    activated = gate_part * sigmoid
-    hidden = (activated * up_part).astype(BF)
-    lower_out = (mm(hidden, w_od[...]) * mask).astype(BF)
-    result = (mm(hidden, w_d[...]) + mm(lower_out, w_ou[...])).astype(BF).astype(F32)
-    moments = []
-    for d in range(sources):
-        back = mm(pick[d], result[d * slots : (d + 1) * slots].astype(BF))
-        moments.append(jnp.sum(back * g_ref[d].astype(F32), axis=1, keepdims=True))
-        back = back * gate[d]
-
-        @pl.when(e == 0)
-        def _():
-            out_ref[d] = back.astype(BF)
+WIDE_IN = MODEL_WIDTH + 2 * SPAN
+WIDE_OUT = MODEL_WIDTH + SPAN
+CHUNK = 16
+
+
+def over_rows(count, body):
+    def step(n, carry):
+        body(pl.ds(pl.multiple_of(n * CHUNK, CHUNK), CHUNK))
+        return carry
+
+    lax.fori_loop(0, count // CHUNK, step, 0)
+
+
+def wait_for(ref, sem):
+    pltpu.make_async_copy(ref, ref, sem).wait()
+
+
+def experts_kernel(n_c, experts, slots, comm, *refs):
+    x_ref, g_ref, h_gu, h_d, h_id, h_iu, h_od, h_ou = refs[:8]
+    refs = refs[8:]
+    out_ref, row_ref, gid_o, giu_o, god_o, gou_o = refs[:6]
+    refs = refs[6:]
+    if comm:
+        xg_ref, final = refs[:2]
+        refs = refs[2:]
+    else:
+        xg_ref = x_ref
+    (wb, db, xw, gw, xl, dr, gu, hl, dh, dgl, res, pick, gate, mom, mask) = refs[:15]
+    (to, tr, gid, giu, god, gou, wsem, csem, osem) = refs[15:24]
+    refs = refs[24:]
+    zh, zl, c, core = here()
+    tok = xw.shape[1]
+    extra = xw.shape[2] - MODEL_WIDTH
+    tiles = n_c
+    f = c * 2 + core
+    near = lambda i: (
+        lax.rem(c // 2 + i // 2, 2) * 2 + lax.rem(lax.rem(c, 2) + lax.rem(i, 2), 2)
+    )
+
+    def pair(ref, p):
+        return ref.at[pl.ds(p * 2, 2)]
+
+    def load_in(expert):
+        yield pltpu.make_async_copy(h_id.at[expert], wb.at[:MODEL_WIDTH, MODEL_WIDTH:], wsem.at[0])
+        yield pltpu.make_async_copy(h_gu.at[expert], wb.at[:MODEL_WIDTH, :MODEL_WIDTH], wsem.at[1])
+        for j in range(2):
+            rows = slice(MODEL_WIDTH + j * SPAN, MODEL_WIDTH + (j + 1) * SPAN)
+            columns = slice(j * EXPERT_HIDDEN, (j + 1) * EXPERT_HIDDEN)
+            yield pltpu.make_async_copy(h_iu.at[expert, j], wb.at[rows, columns], wsem.at[2 + j])
+
+    def load_out(expert):
+        yield pltpu.make_async_copy(h_d.at[expert], db.at[:EXPERT_HIDDEN, :MODEL_WIDTH], wsem.at[4])
+        yield pltpu.make_async_copy(h_od.at[expert], db.at[:EXPERT_HIDDEN, MODEL_WIDTH:], wsem.at[5])
+        yield pltpu.make_async_copy(h_ou.at[expert], db.at[EXPERT_HIDDEN:, :MODEL_WIDTH], wsem.at[6])
+
+    terms = ((gid, gid_o), (giu, giu_o), (god, god_o), (gou, gou_o))
+
+    def term_copies(e):
+        return [pltpu.make_async_copy(a, b.at[e], osem.at[n]) for n, (a, b) in enumerate(terms)]
+
+    if comm:
+        sib, la, lb, fx, fy, sums, sendx, recvx, sends, recvs = refs
+        same = lambda i: (zh, zl, near(i), core)
+        sibling = (zh, zl, c, 1 - core)
+        low_half, high_half = pl.ds(0, tok // 2), pl.ds(tok // 2, tok // 2)
+        signal_all([sibling, same(1), same(2)])
+        first = [
+            remote(x_ref, xg_ref.at[f], sendx.at[n], recvx.at[n], to_)
+            for n, to_ in enumerate((sibling, same(1), same(2)))
+        ]
+        for copy in first:
+            copy.start()
+        fx1, fy1, fd1 = near(1) * 2 + core, near(2) * 2 + core, near(3) * 2 + core
+        forward = [
+            remote(xg_ref.at[fx1, low_half], xg_ref.at[fx1, low_half], sendx.at[3], recvx.at[3], same(2)),
+            remote(xg_ref.at[fy1, high_half], xg_ref.at[fy1, high_half], sendx.at[4], recvx.at[4], same(1)),
+            remote(xg_ref.at[fx1], xg_ref.at[fx1], sendx.at[5], recvx.at[5], sibling),
+            remote(xg_ref.at[fy1], xg_ref.at[fy1], sendx.at[6], recvx.at[6], sibling),
+        ]
+        across = remote(xg_ref.at[fd1], xg_ref.at[fd1], sendx.at[7], recvx.at[7], sibling)
+
+    for copy in (*load_in(0), *load_out(0)):
+        copy.start()
+    spare = EXPERT_HIDDEN
+    wb[MODEL_WIDTH : MODEL_WIDTH + SPAN, spare:] = jnp.zeros((SPAN, WIDE_IN - spare), BF)
+    wb[MODEL_WIDTH + SPAN :, :spare] = jnp.zeros((SPAN, spare), BF)
+    for ref, _ in terms:
+        ref[...] = jnp.zeros_like(ref)
+
+    def order(s):
+        e = s // tiles
+        i = s + e * (2 * tiles - 1 - 2 * s)
+        return e, i, (near(i) if comm else i)
+
+    def fetch_x(p):
+        return pltpu.make_async_copy(pair(xg_ref, p), xw, csem.at[0])
+
+    def fetch_own():
+        other = xg_ref.at[c * 2 + 1 - core]
+        pltpu.make_async_copy(x_ref, xw.at[core], csem.at[0]).start()
+        pltpu.make_async_copy(other, xw.at[1 - core], csem.at[0]).start()
+
+    def fetch_g(p):
+        return pltpu.make_async_copy(pair(g_ref, p), gw, csem.at[1])
+
+    if comm:
+        fetch_g(c).start()
+        wait_for(xg_ref.at[c * 2 + 1 - core], recvx.at[0])
+        fetch_own()
+    else:
+        fetch_g(0).start()
+        fetch_x(0).start()
+
+    def write_out(p):
+        return pltpu.make_async_copy(to, pair(out_ref, p), csem.at[2])
+
+    def write_row(p):
+        return pltpu.make_async_copy(tr, pair(row_ref, p), csem.at[3])
+
+    def read_out(p):
+        return pltpu.make_async_copy(pair(out_ref, p), to, csem.at[4])
+
+    def read_row(p):
+        return pltpu.make_async_copy(pair(row_ref, p), tr, csem.at[5])
+
+    both = 2 * slots
+    steps = 2 * tiles
+    part = lambda d: slice(d * slots, (d + 1) * slots)
+    pieces = [
+        (
+            slice(r, r + CHUNK),
+            slice(h * 512, (h + 1) * 512),
+            slice(EXPERT_HIDDEN + h * 512, EXPERT_HIDDEN + (h + 1) * 512),
+        )
+        for r in range(0, both, CHUNK)
+        for h in range(2)
+    ]
+
+    def step(s, carry):
+        e, i, p = order(s)
+        _, _, after = order(jnp.minimum(s + 1, steps - 1))
+        number = c * (2 * EXP_DEV) + core * EXP_DEV + e
+        fetch_x(p).wait()
+        fetch_g(p).wait()
+        lane = lax.broadcasted_iota(jnp.int32, (tok, extra), 1)
+        lane_s = lax.broadcasted_iota(jnp.int32, (slots, extra), 1)
+        for d in range(2):
+            side = xw[d, :, MODEL_WIDTH:].astype(F32)
+            place = jnp.sum(jnp.where(lane == number, side, 0.0), axis=1, keepdims=True)
+            slot = lax.broadcasted_iota(jnp.int32, (tok, slots), 1).astype(F32)
+            pick[d] = jnp.where(slot == place, 1.0, 0.0).astype(BF)
+            sub = lax.broadcasted_iota(jnp.int32, (extra, tok), 0)
+            place_t = jnp.sum(jnp.where(sub == number, side.T, 0.0), axis=0, keepdims=True)
+            slot_t = lax.broadcasted_iota(jnp.int32, (slots, tok), 0).astype(F32)
+            pickt = jnp.where(slot_t == place_t, 1.0, 0.0).astype(BF)
+            xl[part(d), :MODEL_WIDTH] = mm(pickt, xw[d, :, :MODEL_WIDTH]).astype(BF)
+            dr[part(d), :MODEL_WIDTH] = mm(pickt, gw[d]).astype(BF)
+            side = mm(pickt, xw[d, :, MODEL_WIDTH:])
+            read = lambda which: jnp.sum(jnp.where(which, side, 0.0), axis=1, keepdims=True)
+            gate[part(d)] = read((lane_s == experts + number) | (lane_s == 2 * experts + number))
+            columns = lax.broadcasted_iota(jnp.int32, (slots, SPAN), 1) // ADAPTER_RANK
+            mask[part(d)] = jnp.where(columns.astype(F32) == read(lane_s == 3 * experts), 1.0, 0.0)
+
+        @pl.when((s > 0) & (s <= tiles) if comm else s > 0)
+        def _():
+            write_row(p).wait()
+
+        @pl.when(s > 0)
+        def _():
+            write_out(p).wait()
 
         @pl.when(e > 0)
         def _():
-            out_ref[d] = (out_ref[d].astype(F32) + back).astype(BF)
-
-    grad_lower_out = (mm_t(grad, w_ou[...]) * mask).astype(BF)
-    grad_hidden = mm_t(grad, w_d[...]) + mm_t(grad_lower_out, w_od[...])
-    refill(1, 4, 5)
-    grad_up = (grad_hidden * activated).astype(BF)
-    grad_gate = (
-        grad_hidden * up_part * sigmoid * (1.0 + gate_part * (1.0 - sigmoid))
-    ).astype(BF)
-    grad_lower_in = (
-        jnp.concatenate([mm_t(grad_gate, w_iu[0]), mm_t(grad_up, w_iu[1])], axis=1) * mask2
-    ).astype(BF)
-    grad_rows = (
-        mm_t(grad_gate, w_gu[:, :EXPERT_HIDDEN])
-        + mm_t(grad_up, w_gu[:, EXPERT_HIDDEN:])
-        + mm_t(grad_lower_in, w_id[...])
-    ).astype(BF).astype(F32)
-    refill(0, 2, 3)
-    for d in range(sources):
-        back = mm(pick[d], grad_rows[d * slots : (d + 1) * slots].astype(BF))
-        high = moments[d].astype(BF).astype(F32)
-        low = moments[d] - high
-        side = jnp.where(lane == number, high, 0.0) + jnp.where(lane == experts + number, low, 0.0)
-
-        @pl.when(e == 0)
-        def _():
-            row_ref[d, :, :MODEL_WIDTH] = back.astype(BF)
-            row_ref[d, :, MODEL_WIDTH:] = side.astype(BF)
+            read_out(p).start()
+            read_row(p).start()
+
+        @pl.when(s == 0)
+        def _():
+            for copy in (*load_in(0), *load_out(0)):
+                copy.wait()
+
+        @pl.when(s == tiles)
+        def _():
+            for copy in (*load_in(1), *load_out(1), *term_copies(0)):
+                copy.wait()
+            for ref, _ in terms:
+                ref[...] = jnp.zeros_like(ref)
+
+        mask2 = lambda: jnp.concatenate([mask[...], mask[...]], axis=1)
+        xl[:, MODEL_WIDTH:] = (mm(xl[:, :MODEL_WIDTH], wb[:MODEL_WIDTH, MODEL_WIDTH:]) * mask2()).astype(BF)
+        gu[...] = mm(xl[...], wb[:, :MODEL_WIDTH])
+
+        for rows, a, b in pieces:
+            gate_part = gu[rows, a]
+            hl[rows, a] = (gate_part / (1.0 + jnp.exp(-gate_part)) * gu[rows, b]).astype(BF)
+        hl[:, EXPERT_HIDDEN:] = (
+            mm(hl[:, :EXPERT_HIDDEN], db[:EXPERT_HIDDEN, MODEL_WIDTH:]) * mask[...]
+        ).astype(BF)
+        for n in range(4):
+            a = slice(n * 512, (n + 1) * 512)
+            res[:, a] = (mm(hl[...], db[:, a]) * gate[...]).astype(BF)
 
         @pl.when(e > 0)
         def _():
-            row_ref[d, :, :MODEL_WIDTH] = (row_ref[d, :, :MODEL_WIDTH].astype(F32) + back).astype(BF)
-            row_ref[d, :, MODEL_WIDTH:] = (row_ref[d, :, MODEL_WIDTH:].astype(F32) + side).astype(BF)
-
-    gid[e] += t_mm(x, grad_lower_in)
-    giu[e, 0] += t_mm(lower_g, grad_gate)
-    giu[e, 1] += t_mm(lower_u, grad_up)
-    god[e] += t_mm(hidden, grad_lower_out)
-    gou[e] += t_mm(lower_out, grad)
-
-
-def run_experts(x, g, weights, experts, slots):
-    sources, tok, wide = x.shape
-    pair = 2
-    grid = (sources // pair, EXP_DEV)
-    by_tile = lambda w: pl.BlockSpec((pair, tok, w), lambda t, e: (t, 0, 0))
-    shapes = (
-        (EXP_DEV, MODEL_WIDTH, 2 * SPAN),
-        (EXP_DEV, 2, SPAN, EXPERT_HIDDEN),
-        (EXP_DEV, EXPERT_HIDDEN, SPAN),
-        (EXP_DEV, SPAN, MODEL_WIDTH),
-    )
-    whole = [
-        pl.BlockSpec(s, lambda t, e, n=len(s): (0,) * n, pipeline_mode=pl.Buffered(1))
-        for s in shapes
+            read_out(p).wait()
+
+        def add_picked(target, d):
+            for n in range(4):
+                a = slice(n * 512, (n + 1) * 512)
+                before = jnp.where(e > 0, target[d, :, a].astype(F32), 0.0)
+                target[d, :, a] = (before + mm(pick[d], res[part(d), a])).astype(BF)
+
+        for d in range(2):
+            add_picked(to, d)
+        write_out(p).start()
+
+        @pl.when(s < steps - 1)
+        def _():
+            fetch_g(after).start()
+
+        dr[:, MODEL_WIDTH:] = (
+            mm_t(dr[:, :MODEL_WIDTH], db[EXPERT_HIDDEN:, :MODEL_WIDTH]) * mask[...]
+        ).astype(BF)
+        dh[...] = mm_t(dr[...], db[:EXPERT_HIDDEN, :])
+
+        @pl.when(s == tiles - 1)
+        def _():
+            for copy in load_out(1):
+                copy.start()
+
+        mom[...] = jnp.zeros_like(mom)
+        for rows, a, b in pieces:
+            gate_part, up_part, grad = gu[rows, a], gu[rows, b], dh[rows, a]
+            sigmoid = 1.0 / (1.0 + jnp.exp(-gate_part))
+            activated = gate_part * sigmoid
+            plain = grad * activated
+            mom[rows] += jnp.sum(plain * up_part, axis=1, keepdims=True)
+            dgl[rows, b] = (plain * gate[rows]).astype(BF)
+            slope = sigmoid + activated - activated * sigmoid
+            dgl[rows, a] = (grad * gate[rows] * up_part * slope).astype(BF)
+        dgl[:, MODEL_WIDTH:] = (
+            mm_t(dgl[:, :MODEL_WIDTH], wb[MODEL_WIDTH:, :MODEL_WIDTH]) * mask2()
+        ).astype(BF)
+        for n in range(4):
+            a = slice(n * 512, (n + 1) * 512)
+            res[:, a] = mm_t(dgl[...], wb[a, :]).astype(BF)
+
+        @pl.when(s == tiles - 1)
+        def _():
+            for copy in load_in(1):
+                copy.start()
+
+        if comm:
+            @pl.when(s == 0)
+            def _():
+                wait_for(xg_ref.at[fx1], recvx.at[1])
+                forward[0].start()
+                forward[2].start()
+                wait_for(xg_ref.at[fy1], recvx.at[2])
+                forward[1].start()
+                forward[3].start()
+                wait_for(xg_ref.at[fx1], recvx.at[5])
+
+            @pl.when(s == 1)
+            def _():
+                wait_for(xg_ref.at[fd1, low_half], recvx.at[3])
+                wait_for(xg_ref.at[fd1, high_half], recvx.at[4])
+                across.start()
+                wait_for(xg_ref.at[fy1], recvx.at[6])
+
+            @pl.when(s == 2)
+            def _():
+                wait_for(xg_ref.at[fd1], recvx.at[7])
+
+        @pl.when(s < steps - (2 if comm else 1))
+        def _():
+            fetch_x(after).start()
+
+        if comm:
+
+            @pl.when(s == steps - 2)
+            def _():
+                fetch_own()
+
+        @pl.when(e > 0)
+        def _():
+            read_row(p).wait()
+
+        for d in range(2):
+            add_picked(tr, d)
+            moment = mom[part(d)]
+            high = moment.astype(BF).astype(F32)
+            side = jnp.where(lane_s == number, high, 0.0) + jnp.where(
+                lane_s == experts + number, moment - high, 0.0
+            )
+            before = jnp.where(e > 0, tr[d, :, MODEL_WIDTH:].astype(F32), 0.0)
+            tr[d, :, MODEL_WIDTH:] = (before + mm(pick[d], side.astype(BF))).astype(BF)
+
+        if comm:
+            to_sibling = remote(
+                tr.at[1 - core], sib.at[lax.rem(i, 2)], sends.at[lax.rem(i, 2)],
+                recvs.at[lax.rem(i, 2)], sibling,
+            )
+
+            @pl.when(e == 0)
+            def _():
+                write_row(p).start()
+
+            @pl.when(e > 0)
+            def _():
+                to_sibling.start()
+        else:
+            write_row(p).start()
+
+        gid[...] += t_mm(xl[:, :MODEL_WIDTH], dgl[:, MODEL_WIDTH:])
+        for j in range(2):
+            giu[j] += t_mm(
+                xl[:, MODEL_WIDTH + j * SPAN : MODEL_WIDTH + (j + 1) * SPAN],
+                dgl[:, j * EXPERT_HIDDEN : (j + 1) * EXPERT_HIDDEN],
+            )
+        god[...] += t_mm(hl[:, :EXPERT_HIDDEN], (dr[:, MODEL_WIDTH:].astype(F32) * gate[...]).astype(BF))
+        gou[...] += t_mm((hl[:, EXPERT_HIDDEN:].astype(F32) * gate[...]).astype(BF), dr[:, :MODEL_WIDTH])
+
+        @pl.when(s == tiles - 1)
+        def _():
+            for copy in term_copies(0):
+                copy.start()
+
+        if comm:
+            half = tok // 2
+
+            def chip_sum(at, rows):
+                return tr[core, rows].astype(F32) + sib[at, rows].astype(F32)
+
+            @pl.when(e > 0)
+            def _():
+                to_sibling.wait()
+
+            @pl.when(s == steps - 4)
+            def _():
+                def body(rows):
+                    sums[0, rows] = chip_sum(1, rows).astype(BF)
+
+                over_rows(tok, body)
+                remote(sums.at[0, low_half], la, sends.at[2], recvs.at[2], same(1)).start()
+                remote(sums.at[0, high_half], lb, sends.at[3], recvs.at[3], same(2)).start()
+
+            @pl.when(s == steps - 3)
+            def _():
+                wait_for(la, recvs.at[2])
+
+                def body(rows):
+                    sums[1, rows] = (chip_sum(0, rows) + la[rows].astype(F32)).astype(BF)
+
+                def rest(rows):
+                    rows = pl.ds(pl.multiple_of(rows.start + half, CHUNK), CHUNK)
+                    sums[1, rows] = chip_sum(0, rows).astype(BF)
+
+                over_rows(half, body)
+                over_rows(half, rest)
+                remote(sums.at[1], fy, sends.at[4], recvs.at[4], same(2)).start()
+
+            @pl.when(s == steps - 2)
+            def _():
+                wait_for(lb, recvs.at[3])
+
+                def body(rows):
+                    sums[2, rows] = chip_sum(1, rows).astype(BF)
+
+                def rest(rows):
+                    upper = pl.ds(pl.multiple_of(rows.start + half, CHUNK), CHUNK)
+                    sums[2, upper] = (chip_sum(1, upper) + lb[rows].astype(F32)).astype(BF)
+
+                over_rows(half, body)
+                over_rows(half, rest)
+                remote(sums.at[2], fx, sends.at[5], recvs.at[5], same(1)).start()
+
+        return carry
+
+    lax.fori_loop(0, steps, step, 0)
+    for copy in term_copies(1):
+        copy.start()
+    _, _, last = order(steps - 1)
+    write_out(last).wait()
+    if comm:
+        wait_for(fx, recvs.at[5])
+        wait_for(fy, recvs.at[4])
+
+        def body(rows):
+            total = tr[core, rows].astype(F32) + sib[0, rows].astype(F32)
+            final[rows] = (total + (fx[rows].astype(F32) + fy[rows].astype(F32))).astype(BF)
+
+        over_rows(tok, body)
+        wait_for(la, sends.at[2])
+        wait_for(lb, sends.at[3])
+        wait_for(fy, sends.at[4])
+        wait_for(fx, sends.at[5])
+        for copy in first:
+            copy.wait_send()
+        for copy in forward:
+            copy.wait_send()
+        across.wait_send()
+    else:
+        write_row(last).wait()
+    for copy in term_copies(1):
+        copy.wait()
+
+
+def run_experts(x, g, weights, experts, slots, n_c, comm):
+    tok, wide = x.shape[-2:]
+    sources = 2 * n_c
+    both = 2 * slots
+    dma = pltpu.SemaphoreType.DMA
+    term_shapes = (
+        (MODEL_WIDTH, 2 * SPAN),
+        (2, SPAN, EXPERT_HIDDEN),
+        (EXPERT_HIDDEN, SPAN),
+        (SPAN, MODEL_WIDTH),
+    )
+    any_spec = pl.BlockSpec(memory_space=ANY)
+    out_shape = [
+        jax.ShapeDtypeStruct((sources, tok, MODEL_WIDTH), BF),
+        jax.ShapeDtypeStruct((sources, tok, wide), BF),
+        *(jax.ShapeDtypeStruct((EXP_DEV, *s), F32) for s in term_shapes),
     ]
+    out_specs = [any_spec] * 6
+    scratch = [
+        VMEM((WIDE_IN, WIDE_IN), BF),
+        VMEM((EXPERT_HIDDEN + SPAN, WIDE_OUT), BF),
+        VMEM((2, tok, wide), BF),
+        VMEM((2, tok, MODEL_WIDTH), BF),
+        VMEM((both, WIDE_IN), BF),
+        VMEM((both, WIDE_OUT), BF),
+        VMEM((both, MODEL_WIDTH), F32),
+        VMEM((both, EXPERT_HIDDEN + SPAN), BF),
+        VMEM((both, EXPERT_HIDDEN), F32),
+        VMEM((both, WIDE_IN), BF),
+        VMEM((both, MODEL_WIDTH), BF),
+        VMEM((2, tok, slots), BF),
+        VMEM((both, 1), F32),
+        VMEM((both, 1), F32),
+        VMEM((both, SPAN), F32),
+        VMEM((2, tok, MODEL_WIDTH), BF),
+        VMEM((2, tok, wide), BF),
+        *(VMEM(s, F32) for s in term_shapes),
+        dma((7,)),
+        dma((6,)),
+        dma((4,)),
+    ]
+    params = {}
+    if comm:
+        out_shape += [
+            jax.ShapeDtypeStruct((sources, tok, wide), BF),
+            jax.ShapeDtypeStruct((tok, wide), BF),
+        ]
+        out_specs += [any_spec, pl.BlockSpec(memory_space=VMEM)]
+        scratch += [
+            VMEM((2, tok, wide), BF),
+            VMEM((tok // 2, wide), BF),
+            VMEM((tok // 2, wide), BF),
+            VMEM((tok, wide), BF),
+            VMEM((tok, wide), BF),
+            VMEM((3, tok, wide), BF),
+            dma((8,)),
+            dma((8,)),
+            dma((6,)),
+            dma((6,)),
+        ]
+        params = dict(collective_id=6, has_side_effects=True)
     flops = 2 * sources * EXP_DEV * slots * MODEL_WIDTH * EXPERT_HIDDEN * 8
-    return pl.pallas_call(
-        functools.partial(experts_kernel, experts, slots),
-        grid=grid,
-        out_shape=(
-            jax.ShapeDtypeStruct((sources, tok, MODEL_WIDTH), BF),
-            jax.ShapeDtypeStruct((sources, tok, wide), BF),
-            *(jax.ShapeDtypeStruct(s, F32) for s in shapes),
-        ),
-        in_specs=[by_tile(wide), by_tile(MODEL_WIDTH)]
-        + [pl.BlockSpec(memory_space=ANY)] * WEIGHTS,
-        out_specs=[by_tile(MODEL_WIDTH), by_tile(wide), *whole],
-        scratch_shapes=[VMEM(w.shape[1:], BF) for w in weights]
-        + [pltpu.SemaphoreType.DMA((WEIGHTS,))],
-        compiler_params=pltpu.CompilerParams(vmem_limit_bytes=63 * 2**20),
+    results = pl.pallas_call(
+        functools.partial(experts_kernel, n_c, experts, slots, comm),
+        out_shape=out_shape,
+        in_specs=[any_spec] * 8,
+        out_specs=out_specs,
+        scratch_shapes=scratch,
+        compiler_params=pltpu.CompilerParams(vmem_limit_bytes=63 * 2**20, **params),
         cost_estimate=pl.CostEstimate(flops=flops, bytes_accessed=10**8, transcendentals=10**7),
         name="experts",
     )(x, g, *weights)
+    return results[0], (results[7] if comm else results[1]), results[2:6]
 
 
 def on_device(
@@ -732,7 +1052,7 @@
     block = tok * n_seq
     experts = EXP_DEV * n_fsdp
     capacity = 5 * tok * TOP // (4 * experts)
-    slots = -(-capacity // 8) * 8
+    slots = -(-capacity // 16) * 16
     extra = -(-(3 * experts + 1) // 128) * 128
     span3 = 3 * SPAN
     group = zl * 2 + core
@@ -848,7 +1168,6 @@
     payload = jnp.concatenate(
         [normed2, jnp.pad(side, ((0, 0), (0, extra - side.shape[1])))], axis=1
     )
-    rows_all = lax.all_gather(payload, FSDP, axis=0, tiled=True)
     weights = (
         gate_up_weight,
         down_weight,
@@ -857,16 +1176,19 @@
         expert_output_down,
         expert_output_up,
     )
-    out_parts, row_parts, *expert_terms = run_experts(
-        rows_all.reshape(n_fsdp, tok, MODEL_WIDTH + extra),
-        grad_rows_all.reshape(n_fsdp, tok, MODEL_WIDTH),
-        weights,
-        experts,
-        slots,
-    )
-    returned = lax.psum_scatter(
-        row_parts.reshape(n_fsdp * tok, -1), FSDP, scatter_dimension=0, tiled=True
-    )
+    grads_all = grad_rows_all.reshape(n_fsdp, tok, MODEL_WIDTH)
+    if n_c == 4:
+        out_parts, returned, expert_terms = run_experts(
+            payload, grads_all, weights, experts, slots, n_c, True
+        )
+    else:
+        rows_all = lax.all_gather(payload, FSDP, axis=0, tiled=True)
+        out_parts, row_parts, expert_terms = run_experts(
+            rows_all.reshape(n_fsdp, tok, -1), grads_all, weights, experts, slots, n_c, False
+        )
+        returned = lax.psum_scatter(
+            row_parts.reshape(n_fsdp * tok, -1), FSDP, scatter_dimension=0, tiled=True
+        )
     mixed = lax.psum_scatter(
         out_parts.reshape(n_fsdp * tok, -1), FSDP, scatter_dimension=0, tiled=True
     )

time: 1030 us -> 839 us (0.81)
  waiting for transfers between devices: 251 us -> 89.6 us
  Pallas kernels: 550 us -> 512 us
    reduce_scatter x1 -> x0, waiting for transfers between devices: 74.1 us -> none  [on_device(): lax.psum_scatter(row_parts.reshape(n_fsdp * tok, -1), FSDP, scatter_dimen...]
    all_gather x1 -> x0, waiting for transfers between devices: 66.2 us -> none  [on_device(): rows_all = lax.all_gather(payload, FSDP, axis=0, tiled=True)]
    pallas_call x1, Pallas kernels: 251 us -> 208 us  [run_experts(): pl.pallas_call(functools.partial(experts_kernel, n_c, experts, slots, com...]
    reduce_scatter x1, waiting for transfers between devices: 78 us -> 57 us  [on_device(): lax.psum_scatter(out_parts.reshape(n_fsdp * tok, -1), FSDP, scatter_dimen...]
  transfers between devices with their start and end apart: 12 -> 10, of which waited for: 4 -> 2; matrix products, arithmetic and copies ran while one was open for 18% -> 23% of each run, Pallas kernels for 29% -> 37%
where the time goes in v2:
time: 839 us; the launch traced here: 830 us
  Pallas kernels  512 us (61%)
  waiting for transfers between devices  89.6 us (11%)
  matrix products  78 us (9%)
  local copies, waits for them, and re-layouts  66.9 us (8%)
  other arithmetic  60.5 us (7%)
  between operations  20.3 us (2%)
    pallas_call x1, Pallas kernels, run_experts(): pl.pallas_call(functools.partial(experts_kernel, n_c, experts, slots, com...  208 us
    pallas_call x1, Pallas kernels, gather_to_heads(): pl.pallas_call(functools.partial(gather_kernel, n_c), out_shape=(jax.Shap...  94.6 us
    pallas_call x1, Pallas kernels, sum_to_tokens(): pl.pallas_call(sum_to_tokens_kernel, out_shape=jax.ShapeDtypeStruct((tok,...  69.1 us
    reduce_scatter x1, waiting for transfers between devices, on_device(): lax.psum_scatter(out_parts.reshape(n_fsdp * tok, -1), FSDP, scatter_dimen...  57 us
    pallas_call x1, Pallas kernels, to_heads(): pl.pallas_call(to_heads_kernel, out_shape=jax.ShapeDtypeStruct((4, tok, G...  51 us
    dot_general x8, matrix products, mm_t(): lax.dot_general(left, right, (((1,), (1,)), ((), ())), preferred_element_...  38.3 us
    dot_general x10, matrix products, mm(): lax.dot_general(left, right, (((1,), (0,)), ((), ())), preferred_element_...  33.5 us
    pallas_call x1, Pallas kernels, to_tokens(): pl.pallas_call(to_tokens_kernel, out_shape=jax.ShapeDtypeStruct((tok, MOD...  33.3 us
  transfers between devices with their start and end apart: 10, of which 2 were waited for; matrix products, arithmetic and copies ran while one was open for 23% of the time, Pallas kernels for 37%

profile of v2, /device:TPU:9, one launch (start us, length us, event | category | flops | bytes accessed | tf_op | source)
XLA Modules:
  0.0 830.0 jit_solution(8199598516517239260)
XLA Ops:
  34.6 94.6 %gather_to_heads.1 = (bf16[4,320,2048]{2,1,0:T(8,128)(2,1)}, bf16[2048,1536]{1,0:T(8,128)(2,1)}) custom-call(bf16[320,2048]{1,0:T(8,128)(2,1)} %fusion.6.x_ref, bf16[256,6144]{1,0:T(8,128)(2,1)} %w_ref.1), custom_call_target="tpu_custom_call" | custom-call | tf_op jit(solution)/shard_map/gather_to_heads/pallas_call | solution.py:191
  133.9 12.4 %fusion.67 = f32[1280,1536]{1,0:T(8,128)} fusion(bf16[1280,2048]{1,0:T(8,128)(2,1)S(1)} %bitcast.125, bf16[2048,1536]{1,0:T(8,128)(2,1)} %get-tuple-element.29), kind=kOutput, calls=%fused_computation.164 | convolution fusion | flops 8053063680 | bytes 19398656 | tf_op jit(solution)/shard_map/dot_general | solution.py:35
  147.8 2.5 slice.150
  151.6 6.9 fusion.3
  160.6 3.1 copy-done
  164.8 4.8 group_sum.2
  173.2 21.8 %attend.1 = (bf16[1280,512]{1,0:T(8,128)(2,1)}, bf16[1280,512]{1,0:T(8,128)(2,1)}, bf16[1280,512]{1,0:T(8,128)(2,1)}, bf16[1280,512]{1,0:T(8,128)(2,1)}, f32[4,1280,1]{2,1,0:T(8,128)}) custom-call(f32[1280,1536]{1,0:T(8,128)} %copy-done, f32[1280,1536]{1,0:T(8,128)} %copy-done, f32[1280,1536]{1,0:T(8,128)} %copy-done, f32[1280,1]{1,0:T(8,128)} %bitcast.110, ...), custom_call_target="tpu_custom_call" | custom-call | tf_op jit(solution)/shard_map/attend/pallas_call | solution.py:426
  195.0 33.3 %to_tokens.1 = bf16[320,2048]{1,0:T(8,128)(2,1)} custom-call(bf16[4,320,512]{2,1,0:T(8,128)(2,1)} %bitcast.113), custom_call_target="tpu_custom_call" | custom-call | tf_op jit(solution)/shard_map/to_tokens/pallas_call | solution.py:245
  234.8 5.3 fusion.68
  246.8 208.4 %experts.1 = (bf16[8,320,2048]{2,1,0:T(8,128)(2,1)}, bf16[8,320,2176]{2,1,0:T(8,128)(2,1)}, f32[2,2048,256]{2,1,0:T(8,128)}, f32[2,2,128,1024]{3,2,1,0:T(8,128)}...) custom-call(bf16[320,2176]{1,0:T(8,128)(2,1)} %pad_maximum_fusion.6., ...), custom_call_target="tpu_custom_call" | custom-call | flops 111669149696 | bytes 100000000 | tf_op jit(solution)/shard_map/experts/pallas_call | solution.py:1010
  459.5 3.0 convert_element_type.181
  462.5 3.1 convert_element_type.202
  471.2 4.6 convert_element_type.196
  477.8 3.1 multiply_reduce_fusion
  481.0 57.0 %reduce-scatter.10.cloned.1.call-done = bf16[320,2048]{1,0:T(8,128)(2,1)} async-done(((bf16[2560,2048]{1,0:T(8,128)(2,1)}), bf16[320,2048]{1,0:T(8,128)(2,1)}) %reduce-scatter.10.cloned.1.call-update) | async-done | bytes 1310736 | tf_op jit(solution)/shard_map/reduce_scatter | solution.py:1192
  538.0 5.5 convert_add_fusion.1
  546.0 5.4 fusion.58
  551.4 2.6 fusion.5.a_ref
  554.0 51.0 %to_heads.1 = bf16[4,320,512]{2,1,0:T(8,128)(2,1)} custom-call(bf16[320,2048]{1,0:T(8,128)(2,1)} %fusion.5.a_ref), custom_call_target="tpu_custom_call" | custom-call | tf_op jit(solution)/shard_map/to_heads/pallas_call | solution.py:286
  605.1 24.4 %attend_back.1 = (f32[1280,512]{1,0:T(8,128)}, f32[1280,512]{1,0:T(8,128)}, bf16[1280,512]{1,0:T(8,128)(2,1)}, f32[4,1280,1]{2,1,0:T(8,128)}, f32[4,1280,1]{2,1,0:T(8,128)}) custom-call(bf16[1280,512]{1,0:T(8,128)(2,1)} %get-tuple-element.33.q_ref, bf16[1280,512]{1,0:T(8,128)(2,1)} %get-tuple-element.34.k_ref, bf16[1280,512]{1,0:T(8,128)(2,1)} %get-tuple-element.35.v_ref, ...), custom_call_target="tpu_custom_call" | custom-call | tf_op jit(solution)/shard_map/attend_back/pallas_call | solution.py:514
  634.3 4.8 group_sum.3
  639.9 5.0 subtract_convert_fusion.1
  655.0 4.0 copy.120
  659.0 4.2 convert_element_type.191
  665.0 4.3 convert_element_type.192
  669.2 2.4 pad_maximum_fusion
  673.5 4.0 pad.16.clone
  677.5 7.6 reshape.298
  692.5 15.0 %fusion.16 = f32[1280,2048]{1,0:T(8,128)} fusion(bf16[2048,1536]{1,0:T(8,128)(2,1)} %get-tuple-element.29, bf16[1280,512]{1,0:T(8,128)(2,1)} %get-tuple-element.41, bf16[1280,512]{1,0:T(8,128)(2,1)} %copy-done.9, bf16[1280,512]{1,0:T(8,128)(2,1)} %copy-done.8), kind=kOutput, calls=%fused_computation.47 | convolution fusion | flops 8064860160 | bytes 20709376 | tf_op jit(solution)/shard_map/dot_general | solution.py:39
  707.5 31.0 %reduce-scatter.12.cloned.1.call-done = bf16[4,584,128]{2,1,0:T(8,128)(2,1)} async-done(((bf16[32,584,128]{2,1,0:T(8,128)(2,1)}), bf16[4,584,128]{2,1,0:T(8,128)(2,1)}) %reduce-scatter.12.cloned.1.call-update) | async-done | bytes 598032 | tf_op jit(solution)/shard_map/reduce_scatter | solution.py:1262
  738.6 7.7 add_convert_fusion
  746.3 69.1 %sum_to_tokens.1 = f32[320,2048]{1,0:T(8,128)S(1)} custom-call(bf16[4,320,2048]{2,1,0:T(8,128)(2,1)S(1)} %bitcast.102), custom_call_target="tpu_custom_call" | custom-call | tf_op jit(solution)/shard_map/sum_to_tokens/pallas_call | solution.py:341
  (282 shorter events, 97.8 us)
Async XLA Ops:
  7.2 139.1 %all-gather.6.cloned.1.call-start = ((), (), s32[]{:S(2)}) async-start(), calls=%async_computation.7 | async-start | bytes 5898240 | tf_op jit(solution)/shard_map/all_gather | solution.py:1084
  12.0 222.7 %all-gather.8.cloned.1.call-start = ((), (), s32[]{:S(2)}) async-start(), calls=%async_computation.8 | async-start | bytes 9437184 | tf_op jit(solution)/shard_map/all_gather | solution.py:1095
  12.8 234.0 %all-gather.10.cloned.1.call-start = ((), (), s32[]{:S(2)}) async-start(), calls=%async_computation.15 | async-start | bytes 11796480 | tf_op jit(solution)/shard_map/all_gather | solution.py:1096
  13.5 524.4 %reduce-scatter.10.cloned.1.call-start = ((), (), s32[]{:S(2)}) async-start(), calls=%async_computation.9 | async-start | bytes 11796480 | tf_op jit(solution)/shard_map/reduce_scatter | solution.py:1192
  23.8 9.0 %copy-start.3 = (bf16[1,320,2048]{2,1,0:T(8,128)(2,1)S(1)}, bf16[1,320,2048]{2,1,0:T(8,128)(2,1)}, u32[]{:S(2)}) copy-start(bf16[1,320,2048]{2,1,0:T(8,128)(2,1)} %param.22) | copy-start | bytes 3932164
  23.8 9.3 %copy-start.34 = (f32[2048]{0:T(1024)S(1)}, f32[2048]{0:T(1024)}, u32[]{:S(2)}) copy-start(f32[2048]{0:T(1024)} %param.27) | copy-start | bytes 24580
  32.5 96.7 %copy-start.39 = (s32[320]{0:T(512)}, s32[320]{0:T(512)S(1)}, u32[]{:S(2)}) copy-start(s32[320]{0:T(512)S(1)} %select_reduce_fusion.3) | copy-start | bytes 3844
  33.1 96.0 %copy-start.49 = (f32[320]{0:T(512)}, f32[320]{0:T(512)S(1)}, u32[]{:S(2)}) copy-start(f32[320]{0:T(512)S(1)} %add_rsqrt_fusion.2) | copy-start | bytes 3844
  150.3 8.3 slice-start
  151.5 7.0 copy-start.23
  151.5 7.0 copy-start.25
  151.5 7.0 copy-start.27
  151.6 7.0 slice-start.1
  194.9 38.2 %copy-start.40 = (s32[320]{0:T(512)S(1)}, s32[320]{0:T(512)}, u32[]{:S(2)}) copy-start(s32[320]{0:T(512)} %copy-done.39) | copy-start | bytes 3844
  194.9 38.2 %copy-start.56 = (s32[128]{0:T(128)S(1)}, s32[128]{0:T(128)}, u32[]{:S(2)}) copy-start(s32[128]{0:T(128)} %copy-done.55) | copy-start | bytes 1540
  455.3 229.9 %reduce-scatter.18.cloned.1.call-start = ((), (), s32[]{:S(2)}) async-start(), calls=%async_computation.13 | async-start | bytes 655360 | tf_op jit(solution)/shard_map/reduce_scatter | solution.py:1270
  457.6 229.2 %reduce-scatter.16.cloned.1.call-start = ((), (), s32[]{:S(2)}) async-start(), calls=%async_computation.12 | async-start | bytes 1310720 | tf_op jit(solution)/shard_map/reduce_scatter | solution.py:1270
  458.8 229.8 %reduce-scatter.20.cloned.1.call-start = ((), (), s32[]{:S(2)}) async-start(), calls=%async_computation.14 | async-start | bytes 1310720 | tf_op jit(solution)/shard_map/reduce_scatter | solution.py:1270
  462.5 6.0 copy-start.6
  465.6 224.8 %reduce-scatter.14.cloned.1.call-start = ((), (), s32[]{:S(2)}) async-start(), calls=%async_computation.11 | async-start | bytes 2621440 | tf_op jit(solution)/shard_map/reduce_scatter | solution.py:1270
  477.8 60.2 %copy-start.52 = (f32[320]{0:T(512)S(1)}, f32[320]{0:T(512)}, u32[]{:S(2)}) copy-start(f32[320]{0:T(512)} %copy-done.51) | copy-start | bytes 3844
  480.9 257.7 %reduce-scatter.12.cloned.1.call-start = ((), (), s32[]{:S(2)}) async-start(), calls=%async_computation.10 | async-start | bytes 5382144 | tf_op jit(solution)/shard_map/reduce_scatter | solution.py:1262
  629.5 10.2 %copy-start.36 = (f32[512]{0:T(512)S(1)}, f32[512]{0:T(512)}, u32[]{:S(2)}) copy-start(f32[512]{0:T(512)} %dynamic_slice.15) | copy-start | bytes 6148
  629.5 10.2 %copy-start.37 = (f32[512]{0:T(512)S(1)}, f32[512]{0:T(512)}, u32[]{:S(2)}) copy-start(f32[512]{0:T(512)} %dynamic_slice.16) | copy-start | bytes 6148
  629.5 10.2 %copy-start.43 = (f32[1280]{0:T(1024)S(1)}, f32[1280]{0:T(1024)}, u32[]{:S(2)}) copy-start(f32[1280]{0:T(1024)} %get-tuple-element.62) | copy-start | bytes 15364
  629.6 10.2 %copy-start.44 = (f32[1280]{0:T(1024)S(1)}, f32[1280]{0:T(1024)}, u32[]{:S(2)}) copy-start(f32[1280]{0:T(1024)} %get-tuple-element.63) | copy-start | bytes 15364
  629.6 10.2 %copy-start.45 = (f32[1280]{0:T(1024)S(1)}, f32[1280]{0:T(1024)}, u32[]{:S(2)}) copy-start(f32[1280]{0:T(1024)} %get-tuple-element.66) | copy-start | bytes 15364
  629.6 10.2 %copy-start.46 = (f32[1280]{0:T(1024)S(1)}, f32[1280]{0:T(1024)}, u32[]{:S(2)}) copy-start(f32[1280]{0:T(1024)} %get-tuple-element.67) | copy-start | bytes 15364
  639.8 5.9 copy-start.26
  685.1 133.4 %reduce-scatter.22.cloned.1.call-start = ((), (), s32[]{:S(2)}) async-start(), calls=%async_computation.16 | async-start | bytes 747520
  746.3 69.2 %copy-start.4 = (bf16[1,320,2048]{2,1,0:T(8,128)(2,1)S(1)}, bf16[1,320,2048]{2,1,0:T(8,128)(2,1)}, u32[]{:S(2)}) copy-start(bf16[1,320,2048]{2,1,0:T(8,128)(2,1)} %param.22) | copy-start | bytes 3932164
  746.3 69.2 %copy-start.35 = (f32[2048]{0:T(1024)S(1)}, f32[2048]{0:T(1024)}, u32[]{:S(2)}) copy-start(f32[2048]{0:T(1024)} %param.27) | copy-start | bytes 24580
  (44 other events, 155.3 us)
Sparse Core Ops, SparseCore 0:
  12.2 87.5 all-gather.5
  101.6 62.4 all-gather.7
  166.0 63.2 all-gather.9
  455.4 82.5 reduce-scatter.9
  540.1 17.7 reduce-scatter.17
  560.6 41.6 reduce-scatter.15
  604.7 23.7 reduce-scatter.19
  630.8 42.1 reduce-scatter.13
  685.2 53.2 reduce-scatter.11
  740.7 50.8 reduce-scatter.21

commit v3 on v2

--- a/solution.py
+++ b/solution.py
@@ -357,6 +357,144 @@
         ),
         name="sum_to_tokens",
     )(parts)
+
+
+def finish_kernel(n_c, p_ref, late, early, o_ref, flat, sib, chip, rx, got_l, stage, got_z, ss, sr, send, recv, ls, lr, zs, zr):
+    zh, zl, c, core = here()
+    plane = [(zh, zl, lax.rem(c + i, n_c), core ^ k) for i in range(n_c) for k in range(2)]
+    signal_all(column_peers(zh, zl, c, core) + plane[2:])
+    width = o_ref.shape[1]
+    half = width // 2
+    sibling = (zh, zl, c, 1 - core)
+    mine = pl.ds(pl.multiple_of(core * half, half), half)
+    theirs = pl.ds(pl.multiple_of((1 - core) * half, half), half)
+    for s in range(4):
+        remote(p_ref.at[s, :, theirs], sib.at[s], ss.at[s], sr.at[s], sibling).start()
+    me = c * 2 + core
+    def is_self(s):
+        return (s // 2 == zh) & (s % 2 == zl) & (core == zh)
+
+    for s in range(4):
+        pltpu.make_async_copy(sib.at[s], sib.at[s], sr.at[s]).wait()
+        chip[s] = (p_ref[s, :, mine].astype(F32) + sib[s].astype(F32)).astype(BF)
+        src, dst = chip.at[s], rx.at[zl, core]
+
+        @pl.when(is_self(s))
+        def _():
+            pltpu.make_async_copy(src, dst, recv.at[zl, core]).start()
+
+        @pl.when(jnp.logical_not(is_self(s)))
+        def _():
+            remote(src, dst, send.at[s], recv.at[zl, core], (s // 2, s % 2, c, zh)).start()
+
+    count = len(plane)
+    for n in range(1, count):
+        peer = plane[n]
+        remote(late.at[peer[2] * 2 + peer[3]], got_l.at[n], ls.at[n], lr.at[n], peer).start()
+    late_sum = late[me].astype(F32)
+    for n in range(1, count):
+        wait_for(got_l.at[n], lr.at[n])
+        late_sum = late_sum + got_l[n].astype(F32)
+    late_sum = late_sum.astype(BF)
+    down, up, wide, rest = finish_rows(n_c)
+    for q in range(4):
+        stage[q, :down] = late_sum[q * down : (q + 1) * down]
+        if q < 3:
+            at = 4 * down + q * up
+            stage[q, down : down + up] = late_sum[at : at + up]
+            stage[q, down + up : down + wide] = jnp.zeros((wide - up, SPAN), BF)
+        else:
+            stage[q, down : down + wide] = early[:wide]
+        at = wide + q * rest
+        stage[q, down + wide :] = early[at : at + rest]
+    seq = zh * 2 + zl
+    for q in range(4):
+
+        @pl.when(seq == q)
+        def _():
+            got_z[q] = stage[q]
+
+        @pl.when(seq != q)
+        def _():
+            remote(stage.at[q], got_z.at[seq], zs.at[q], zr.at[seq], (q // 2, q % 2, c, core)).start()
+
+    for k in range(2):
+        for b in range(2):
+            pltpu.make_async_copy(rx.at[b, k], rx.at[b, k], recv.at[b, k]).wait()
+        o_ref[:, k * half : (k + 1) * half] = rx[0, k].astype(F32) + rx[1, k].astype(F32)
+
+    for q in range(4):
+
+        @pl.when(seq != q)
+        def _():
+            wait_for(got_z.at[q], zr.at[q])
+
+    terms = [got_z[q].astype(F32) for q in range(4)]
+    flat[...] = (terms[0] + terms[1]) + (terms[2] + terms[3])
+
+    @pl.when(seq < 3)
+    def _():
+        for b in range(2):
+            pair = got_z[b, down : down + up].astype(F32) + got_z[2 + b, down : down + up].astype(F32)
+            flat[down + b * up : down + (b + 1) * up] = pair
+
+    for s in range(4):
+        pltpu.make_async_copy(sib.at[s], sib.at[s], ss.at[s]).wait()
+
+        @pl.when(jnp.logical_not(is_self(s)))
+        def _():
+            pltpu.make_async_copy(chip.at[s], chip.at[s], send.at[s]).wait()
+
+        @pl.when(seq != s)
+        def _():
+            wait_for(stage.at[s], zs.at[s])
+
+    for n in range(1, count):
+        wait_for(got_l.at[n], ls.at[n])
+
+
+def finish_rows(n_c):
+    n_f = 2 * n_c
+    down, up = MODEL_WIDTH // (4 * n_f), SPAN // n_f
+    return 3 * down, 8 * up, 16 * up, 2 * down + 16
+
+
+def finish(parts, late, early, n_c):
+    _, tok, width = parts.shape
+    half = width // 2
+    down, up, wide, rest = finish_rows(n_c)
+    n_f = 2 * n_c
+    dma = pltpu.SemaphoreType.DMA
+    vmem = pl.BlockSpec(memory_space=VMEM)
+    return pl.pallas_call(
+        functools.partial(finish_kernel, n_c),
+        out_shape=(
+            jax.ShapeDtypeStruct((tok, width), F32),
+            jax.ShapeDtypeStruct((down + wide + rest, SPAN), F32),
+        ),
+        in_specs=[vmem] * 3,
+        out_specs=[vmem] * 2,
+        scratch_shapes=[
+            VMEM((4, tok, half), BF),
+            VMEM((4, tok, half), BF),
+            VMEM((2, 2, tok, half), BF),
+            VMEM(late.shape, BF),
+            VMEM((4, down + wide + rest, SPAN), BF),
+            VMEM((4, down + wide + rest, SPAN), BF),
+            dma((4,)),
+            dma((4,)),
+            dma((4,)),
+            dma((2, 2)),
+            dma((n_f,)),
+            dma((n_f,)),
+            dma((4,)),
+            dma((4,)),
+        ],
+        compiler_params=pltpu.CompilerParams(
+            collective_id=7, has_side_effects=True, vmem_limit_bytes=50 * 2**20
+        ),
+        name="finish",
+    )(parts, late, early)
 
 
 def group_sum_kernel(x_ref, o_ref, rx, send, recv):
@@ -540,6 +678,8 @@
 WIDE_IN = MODEL_WIDTH + 2 * SPAN
 WIDE_OUT = MODEL_WIDTH + SPAN
 CHUNK = 16
+TERM_PARTS = 4
+TERM_ROWS = MODEL_WIDTH // 4 + 2 * SPAN + SPAN + 2 * SPAN
 
 
 def over_rows(count, body):
@@ -557,16 +697,16 @@
 def experts_kernel(n_c, experts, slots, comm, *refs):
     x_ref, g_ref, h_gu, h_d, h_id, h_iu, h_od, h_ou = refs[:8]
     refs = refs[8:]
-    out_ref, row_ref, gid_o, giu_o, god_o, gou_o = refs[:6]
-    refs = refs[6:]
+    out_ref, row_ref, terms_o = refs[:3]
+    refs = refs[3:]
     if comm:
-        xg_ref, final = refs[:2]
-        refs = refs[2:]
+        xg_ref, final, first_o = refs[:3]
+        refs = refs[3:]
     else:
         xg_ref = x_ref
     (wb, db, xw, gw, xl, dr, gu, hl, dh, dgl, res, pick, gate, mom, mask) = refs[:15]
-    (to, tr, gid, giu, god, gou, wsem, csem, osem) = refs[15:24]
-    refs = refs[24:]
+    (to, tr, gid, giu, god, gou, packed, wsem, csem, osem) = refs[15:25]
+    refs = refs[25:]
     zh, zl, c, core = here()
     tok = xw.shape[1]
     extra = xw.shape[2] - MODEL_WIDTH
@@ -592,17 +732,56 @@
         yield pltpu.make_async_copy(h_od.at[expert], db.at[:EXPERT_HIDDEN, MODEL_WIDTH:], wsem.at[5])
         yield pltpu.make_async_copy(h_ou.at[expert], db.at[EXPERT_HIDDEN:, :MODEL_WIDTH], wsem.at[6])
 
-    terms = ((gid, gid_o), (giu, giu_o), (god, god_o), (gou, gou_o))
-
-    def term_copies(e):
-        return [pltpu.make_async_copy(a, b.at[e], osem.at[n]) for n, (a, b) in enumerate(terms)]
+    terms = (gid, giu, god, gou)
+
+    def term_copy(e):
+        return pltpu.make_async_copy(packed, terms_o if comm else terms_o.at[:, e], osem.at[0])
+
+    def send_first_terms():
+        pltpu.make_async_copy(packed.at[seq], first_o.at[seq], osem.at[0]).start()
+        for q in range(TERM_PARTS):
+
+            @pl.when(seq != q)
+            def _():
+                remote(packed.at[q], first_o.at[seq], tsend.at[q], trecv.at[seq], (q // 2, q % 2, c, core)).start()
+
+    def wait_first_terms(sent):
+        for q in range(TERM_PARTS):
+
+            @pl.when(seq != q)
+            def _():
+                if sent:
+                    wait_for(packed.at[q], tsend.at[q])
+                else:
+                    wait_for(first_o.at[q], trecv.at[q])
+
+        if sent:
+            wait_for(packed.at[0], osem.at[0])
+
+    def pack_terms():
+        for q in range(TERM_PARTS):
+            rows, columns = MODEL_WIDTH // 4, EXPERT_HIDDEN // 4
+            packed[q, :rows] = gid[q * rows : (q + 1) * rows].astype(BF)
+            for j in range(2):
+                at = rows + j * SPAN
+                packed[q, at : at + SPAN] = giu[j, :, q * columns : (q + 1) * columns].astype(BF)
+            at = rows + 2 * SPAN
+            for j in range(2):
+                half = slice(j * SPAN, (j + 1) * SPAN)
+                row = q * columns + j * SPAN
+                packed[q, at : at + SPAN, half] = god[row : row + SPAN].astype(BF)
+                column = q * rows + j * 256
+                low = at + (j + 1) * SPAN
+                packed[q, low : low + SPAN] = gou[:, column : column + 256].astype(BF)
 
     if comm:
-        sib, la, lb, fx, fy, sums, sendx, recvx, sends, recvs = refs
+        sib, la, lb, fx, fy, sums, sendx, recvx, sends, recvs, tsend, trecv = refs
+        seq = zh * 2 + zl
         same = lambda i: (zh, zl, near(i), core)
         sibling = (zh, zl, c, 1 - core)
         low_half, high_half = pl.ds(0, tok // 2), pl.ds(tok // 2, tok // 2)
-        signal_all([sibling, same(1), same(2)])
+        column = [(zh ^ 1, zl, c, core), (zh, zl ^ 1, c, core), (zh ^ 1, zl ^ 1, c, core)]
+        signal_all([sibling, same(1), same(2), *column])
         first = [
             remote(x_ref, xg_ref.at[f], sendx.at[n], recvx.at[n], to_)
             for n, to_ in enumerate((sibling, same(1), same(2)))
@@ -623,7 +802,7 @@
     spare = EXPERT_HIDDEN
     wb[MODEL_WIDTH : MODEL_WIDTH + SPAN, spare:] = jnp.zeros((SPAN, WIDE_IN - spare), BF)
     wb[MODEL_WIDTH + SPAN :, :spare] = jnp.zeros((SPAN, spare), BF)
-    for ref, _ in terms:
+    for ref in terms:
         ref[...] = jnp.zeros_like(ref)
 
     def order(s):
@@ -720,9 +899,9 @@
 
         @pl.when(s == tiles)
         def _():
-            for copy in (*load_in(1), *load_out(1), *term_copies(0)):
+            for copy in (*load_in(1), *load_out(1), *(() if comm else (term_copy(0),))):
                 copy.wait()
-            for ref, _ in terms:
+            for ref in terms:
                 ref[...] = jnp.zeros_like(ref)
 
         mask2 = lambda: jnp.concatenate([mask[...], mask[...]], axis=1)
@@ -862,8 +1041,11 @@
 
         @pl.when(s == tiles - 1)
         def _():
-            for copy in term_copies(0):
-                copy.start()
+            pack_terms()
+            if comm:
+                send_first_terms()
+            else:
+                term_copy(0).start()
 
         if comm:
             half = tok // 2
@@ -917,8 +1099,10 @@
         return carry
 
     lax.fori_loop(0, steps, step, 0)
-    for copy in term_copies(1):
-        copy.start()
+    if comm:
+        wait_first_terms(True)
+    pack_terms()
+    term_copy(1).start()
     _, _, last = order(steps - 1)
     write_out(last).wait()
     if comm:
@@ -939,10 +1123,10 @@
         for copy in forward:
             copy.wait_send()
         across.wait_send()
+        wait_first_terms(False)
     else:
         write_row(last).wait()
-    for copy in term_copies(1):
-        copy.wait()
+    term_copy(1).wait()
 
 
 def run_experts(x, g, weights, experts, slots, n_c, comm):
@@ -960,9 +1144,11 @@
     out_shape = [
         jax.ShapeDtypeStruct((sources, tok, MODEL_WIDTH), BF),
         jax.ShapeDtypeStruct((sources, tok, wide), BF),
-        *(jax.ShapeDtypeStruct((EXP_DEV, *s), F32) for s in term_shapes),
+        jax.ShapeDtypeStruct(
+            (TERM_PARTS, TERM_ROWS, 256) if comm else (TERM_PARTS, EXP_DEV, TERM_ROWS, 256), BF
+        ),
     ]
-    out_specs = [any_spec] * 6
+    out_specs = [any_spec] * 3
     scratch = [
         VMEM((WIDE_IN, WIDE_IN), BF),
         VMEM((EXPERT_HIDDEN + SPAN, WIDE_OUT), BF),
@@ -982,17 +1168,19 @@
         VMEM((2, tok, MODEL_WIDTH), BF),
         VMEM((2, tok, wide), BF),
         *(VMEM(s, F32) for s in term_shapes),
+        VMEM((TERM_PARTS, TERM_ROWS, 256), BF),
         dma((7,)),
         dma((6,)),
-        dma((4,)),
+        dma((1,)),
     ]
     params = {}
     if comm:
         out_shape += [
             jax.ShapeDtypeStruct((sources, tok, wide), BF),
             jax.ShapeDtypeStruct((tok, wide), BF),
+            jax.ShapeDtypeStruct((TERM_PARTS, TERM_ROWS, 256), BF),
         ]
-        out_specs += [any_spec, pl.BlockSpec(memory_space=VMEM)]
+        out_specs += [any_spec, pl.BlockSpec(memory_space=VMEM), any_spec]
         scratch += [
             VMEM((2, tok, wide), BF),
             VMEM((tok // 2, wide), BF),
@@ -1004,6 +1192,8 @@
             dma((8,)),
             dma((6,)),
             dma((6,)),
+            dma((TERM_PARTS,)),
+            dma((TERM_PARTS,)),
         ]
         params = dict(collective_id=6, has_side_effects=True)
     flops = 2 * sources * EXP_DEV * slots * MODEL_WIDTH * EXPERT_HIDDEN * 8
@@ -1017,7 +1207,51 @@
         cost_estimate=pl.CostEstimate(flops=flops, bytes_accessed=10**8, transcendentals=10**7),
         name="experts",
     )(x, g, *weights)
-    return results[0], (results[7] if comm else results[1]), results[2:6]
+    if comm:
+        return results[0], results[4], (results[5], results[2])
+    return results[0], results[1], results[2]
+
+
+def late_kernel(n_f, dp, up, mask, low, x, dlow, packed):
+    core = lax.axis_index("core")
+    down_rows = MODEL_WIDTH // (4 * n_f)
+    up_rows = SPAN // n_f
+    base = 12 * down_rows
+    packed[:, base:] = jnp.zeros((n_f, 24 * up_rows, SPAN), BF)
+    for j in range(3):
+        own = slice(j * SPAN, (j + 1) * SPAN)
+        wide = slice(j * GROUP_WIDTH, (j + 1) * GROUP_WIDTH)
+        lowered = (mm_t(dp[:, wide], up[own]) * mask[...]).astype(BF)
+        dlow[:, own] = lowered
+        grad_up = t_mm(low[:, own], dp[:, wide]).astype(BF)
+        grad_down = t_mm(x[...], lowered).astype(BF)
+        for f in range(n_f):
+            for b in range(4):
+                at = base + (j * 8 + core * 4 + b) * up_rows
+                packed[f, pl.ds(pl.multiple_of(at, up_rows), up_rows)] = grad_up[
+                    f * up_rows : (f + 1) * up_rows, b * SPAN : (b + 1) * SPAN
+                ]
+            for q in range(4):
+                row = (q * n_f + f) * down_rows
+                at = (q * 3 + j) * down_rows
+                packed[f, at : at + down_rows] = grad_down[row : row + down_rows]
+
+
+def late_gradients(grad_projected, up_own, mask, lowered, x, n_f):
+    block = x.shape[0]
+    rows = 12 * MODEL_WIDTH // (4 * n_f) + 24 * SPAN // n_f
+    return pl.pallas_call(
+        functools.partial(late_kernel, n_f),
+        out_shape=(
+            jax.ShapeDtypeStruct((block, 3 * SPAN), BF),
+            jax.ShapeDtypeStruct((n_f, rows, SPAN), BF),
+        ),
+        in_specs=[pl.BlockSpec(memory_space=VMEM)] * 5,
+        out_specs=[pl.BlockSpec(memory_space=VMEM)] * 2,
+        compiler_params=pltpu.CompilerParams(vmem_limit_bytes=50 * 2**20),
+        cost_estimate=pl.CostEstimate(flops=4 * 10**9, bytes_accessed=2 * 10**7, transcendentals=0),
+        name="late_gradients",
+    )(grad_projected, up_own, mask, lowered, x)
 
 
 def on_device(
@@ -1102,7 +1336,8 @@
     seq_block, block_offsets, block_sets = token_meta(
         held_lengths[:count], held_lengths[count:], jnp.arange(block, dtype=jnp.int32)
     )
-    mask3 = jnp.tile(set_mask(block_sets), (1, 3))
+    mask1 = set_mask(block_sets)
+    mask3 = jnp.tile(mask1, (1, 3))
     half = HD // 2
     freqs = THETA ** (-(jnp.arange(half, dtype=F32) * 2.0 / HD))
     angles = block_offsets.astype(F32)[:, None] * freqs[None, :]
@@ -1192,8 +1427,6 @@
     mixed = lax.psum_scatter(
         out_parts.reshape(n_fsdp * tok, -1), FSDP, scatter_dimension=0, tiled=True
     )
-    output = (middle + mixed.astype(F32)).astype(BF)
-
     grad_out = cotangent[0].astype(F32)
     returned = returned.astype(F32)
     back = returned[:, MODEL_WIDTH:]
@@ -1212,8 +1445,27 @@
     grad_out_lower = (mm_t(grad_branch, up_o) * mask).astype(BF)
     grad_attended = (mm_t(grad_branch, out_full) + mm_t(grad_out_lower, down_o)).astype(BF)
     head_grad = to_heads(grad_attended).reshape(block, GROUP_WIDTH)
+    if n_c == 4:
+        first_terms, second_terms = expert_terms
+        second_terms, head_grad = lax.optimization_barrier((second_terms, head_grad))
+        second_terms = lax.all_to_all(second_terms, SEQ, split_axis=0, concat_axis=0, tiled=True)
+    else:
+        expert_terms = lax.psum_scatter(expert_terms, SEQ, scatter_dimension=0, tiled=True)
     grad_up_o = t_mm(out_lower, grad_branch)
     grad_down_o = t_mm(attended, grad_out_lower)
+    if n_c == 4:
+        up_rows = SPAN // n_fsdp
+        up_blocks = grad_up_o.astype(BF).reshape(n_fsdp, up_rows, 16, SPAN).transpose(0, 2, 1, 3)
+        by_owner = lambda t: t.astype(BF).reshape(n_seq, n_fsdp, -1, SPAN).transpose(1, 0, 2, 3)
+        rup_rows = jnp.pad(grad_rup.reshape(n_seq * n_fsdp, 1, -1), ((0, 0), (0, 15), (0, 0)))
+        rup_rows = jnp.pad(rup_rows, ((0, 0), (0, 0), (0, SPAN - rup_rows.shape[2])))
+        rest = jnp.concatenate(
+            [by_owner(grad_down_o), by_owner(grad_rdown), by_owner(rup_rows)], axis=2
+        )
+        early = jnp.concatenate(
+            [up_blocks.reshape(n_fsdp, -1, SPAN), rest.reshape(n_fsdp, -1, SPAN)], axis=1
+        )
+        early = lax.psum_scatter(early.reshape(-1, SPAN), FSDP, scatter_dimension=0, tiled=True)
 
     uq, uk, grad_v, mq, mk = attend_back(
         q, k, v, head_grad, lse, projected, *gains, cosine, sine, seg_c, seg_r
@@ -1231,44 +1483,89 @@
         ],
         axis=1,
     )
-    grad_lowered = (mm_t(grad_projected, up_diagonal) * mask3).astype(BF)
-    grad_up_own = [
-        t_mm(
-            lowered[:, j * SPAN : (j + 1) * SPAN],
-            grad_projected[:, j * GROUP_WIDTH : (j + 1) * GROUP_WIDTH],
+    if n_c == 4:
+        grad_lowered, late = late_gradients(
+            grad_projected, up_own, mask1, lowered, x_all, n_fsdp
         )
-        for j in range(3)
-    ]
-    grad_down_qkv = t_mm(x_all, grad_lowered)
+    else:
+        grad_lowered = (mm_t(grad_projected, up_diagonal) * mask3).astype(BF)
     grad_normed_part = (mm_t(grad_projected, qkv_rows) + mm_t(grad_lowered, down3)).astype(BF)
-    grad_normed = sum_to_tokens(grad_normed_part.reshape(4, tok, MODEL_WIDTH))
+    grad_normed_part = grad_normed_part.reshape(4, tok, MODEL_WIDTH)
+    if n_c == 4:
+        grad_normed, flat = finish(grad_normed_part, late, early, n_c)
+    else:
+        grad_normed = sum_to_tokens(grad_normed_part)
     grad_inputs = grad_middle + rms_back(inputs, gain_attn, grad_normed)
 
-    grad_down_all = jnp.concatenate([grad_down_qkv, grad_down_o], axis=1).astype(BF)
-    wide_up = lax.dynamic_update_slice_in_dim(
-        jnp.zeros((span3, MODEL_WIDTH), F32),
-        jnp.concatenate(grad_up_own, axis=0),
-        group * GROUP_WIDTH,
-        1,
-    )
-    grad_up_all = jnp.concatenate([wide_up, grad_up_o], axis=0).astype(BF)
-    terms = (grad_down_all, grad_up_all, grad_rdown.astype(BF), grad_rup.astype(BF))
-    own_shapes = [(t.shape[0] // (n_seq * n_fsdp), t.shape[1]) for t in terms]
-    flat = jnp.concatenate(
-        [t.reshape(n_seq, n_fsdp, -1).transpose(1, 0, 2) for t in terms], axis=2
-    )
-    used = flat.shape[2]
-    flat = jnp.pad(flat, ((0, 0), (0, 0), (0, -used % 1024))).reshape(n_fsdp * n_seq, -1, 128)
-    flat = lax.psum_scatter(flat, FSDP, scatter_dimension=0, tiled=True)
-    flat = lax.psum_scatter(flat, SEQ, scatter_dimension=0, tiled=True).astype(F32).reshape(-1)
-    summed, at = [], 0
-    for shape in own_shapes:
-        size = shape[0] * shape[1]
-        summed.append(flat[at : at + size].reshape(shape))
-        at += size
+    down_rows, up_rows = MODEL_WIDTH // (n_seq * n_fsdp), SPAN // n_fsdp
+    rup_shape = (SPAN // (n_seq * n_fsdp), experts)
+    if n_c == 4:
+        blocks = [flat[j * down_rows : (j + 1) * down_rows] for j in range(3)]
+        at = 3 * down_rows
+        up_blocks = [flat[at + n * up_rows : at + (n + 1) * up_rows] for n in range(16)]
+        at += 16 * up_rows
+        blocks.append(flat[at : at + down_rows])
+        at += down_rows
+        summed = [
+            jnp.concatenate(blocks, axis=1),
+            jnp.concatenate(up_blocks, axis=1),
+            flat[at : at + down_rows],
+        ]
+        at += down_rows
+        summed.append(flat[at, : rup_shape[0] * rup_shape[1]].reshape(rup_shape))
+    else:
+        grad_up_own = [
+            t_mm(
+                lowered[:, j * SPAN : (j + 1) * SPAN],
+                grad_projected[:, j * GROUP_WIDTH : (j + 1) * GROUP_WIDTH],
+            )
+            for j in range(3)
+        ]
+        grad_down_qkv = t_mm(x_all, grad_lowered)
+        grad_down_all = jnp.concatenate([grad_down_qkv, grad_down_o], axis=1).astype(BF)
+        wide_up = lax.dynamic_update_slice_in_dim(
+            jnp.zeros((span3, MODEL_WIDTH), F32),
+            jnp.concatenate(grad_up_own, axis=0),
+            group * GROUP_WIDTH,
+            1,
+        )
+        grad_up_all = jnp.concatenate([wide_up, grad_up_o], axis=0).astype(BF)
+        terms = (grad_down_all, grad_up_all, grad_rdown.astype(BF), grad_rup.astype(BF))
+        own_shapes = [(t.shape[0] // (n_seq * n_fsdp), t.shape[1]) for t in terms]
+        flat = jnp.concatenate(
+            [t.reshape(n_seq, n_fsdp, -1).transpose(1, 0, 2) for t in terms], axis=2
+        )
+        used = flat.shape[2]
+        flat = jnp.pad(flat, ((0, 0), (0, 0), (0, -used % 1024))).reshape(n_fsdp * n_seq, -1, 128)
+        flat = lax.psum_scatter(flat, FSDP, scatter_dimension=0, tiled=True)
+        flat = lax.psum_scatter(flat, SEQ, scatter_dimension=0, tiled=True)
+        flat = flat.astype(F32).reshape(-1)
+        summed, at = [], 0
+        for shape in own_shapes:
+            size = shape[0] * shape[1]
+            summed.append(flat[at : at + size].reshape(shape))
+            at += size
+
+    mixed, grad_inputs = lax.optimization_barrier((mixed, grad_inputs))
+    output = (middle + mixed.astype(F32)).astype(BF)
+    if n_c == 4:
+        expert_terms = jnp.stack(
+            [jnp.sum(t.astype(F32), axis=0) for t in (first_terms, second_terms)]
+        )
+    else:
+        expert_terms = expert_terms[0].astype(F32)
+    rows = MODEL_WIDTH // 4
+    at = rows + 2 * SPAN
+    halves = expert_terms[:, at : at + SPAN]
+    low = at + SPAN
     expert_sums = [
-        lax.psum_scatter(t.astype(BF), SEQ, scatter_dimension=d, tiled=True).astype(F32)
-        for t, d in zip(expert_terms, (1, 3, 1, 2), strict=True)
+        expert_terms[:, :rows],
+        expert_terms[:, rows:at].reshape(EXP_DEV, 2, SPAN, EXPERT_HIDDEN // 4),
+        jnp.concatenate([halves[..., :SPAN], halves[..., SPAN:]], axis=1),
+        jnp.concatenate(
+            [expert_terms[:, low : low + SPAN], expert_terms[:, low + SPAN : low + 2 * SPAN]],
+            axis=2,
+        ),
     ]
     return (output[None], grad_inputs[None], *summed, *expert_sums)
 

time: 839 us -> 717 us (0.85)
  waiting for transfers between devices: 89.6 us -> 1.96 us
  local copies, waits for them, and re-layouts: 66.9 us -> 38.8 us
  other arithmetic: 60.5 us -> 46.6 us
  Pallas kernels: 512 us -> 525 us
  matrix products: 78 us -> 69.3 us
    reduce_scatter x1, waiting for transfers between devices: 57 us -> 0.01 us  [on_device(): lax.psum_scatter(out_parts.reshape(n_fsdp * tok, -1), FSDP, scatter_dimen...]
    reduce_scatter x5 -> x1, waiting for transfers between devices: 31.1 us -> 0.01 us  [on_device(): lax.psum_scatter(early.reshape(-1, SPAN), FSDP, scatter_dimension=0, tile...]
    pallas_call x1 -> x2, Pallas kernels: 69.1 us -> 93.5 us  [the longest x1 81.3 us: finish(): pl.pallas_call(functools.partial(finish_kernel, n_c), out_shape=(jax.Shap...]
    convert_element_type x9 -> x0, other arithmetic: 18.4 us -> none  [the longest x4 11.1 us: on_device(): t.astype(BF)]
    pallas_call x1, Pallas kernels: 51 us -> 34.3 us  [to_heads(): pl.pallas_call(to_heads_kernel, out_shape=jax.ShapeDtypeStruct((4, tok, G...]
    reshape x6 -> x3, local copies, waits for them, and re-layouts: 11.3 us -> 0.17 us  [the longest x1 0.09 us: on_device(): grad_rup.reshape(n_seq * n_fsdp, 1, -1)]
    convert_element_type x3 -> x1, local copies, waits for them, and re-layouts: 8.64 us -> 0.23 us  [set_mask(): return (chosen[..., None] == column_range).astype(F32)]
    dot_general x8 -> x7, matrix products: 38.3 us -> 30.9 us  [mm_t(): lax.dot_general(left, right, (((1,), (1,)), ((), ())), preferred_element_...]
  transfers between devices with their start and end apart: 10 -> 6, of which waited for: 2 -> 0; matrix products, arithmetic and copies ran while one was open for 23% -> 18% of each run, Pallas kernels for 37% -> 45%
where the time goes in v3:
time: 717 us; the launch traced here: 708 us
  Pallas kernels  525 us (73%)
  matrix products  69.3 us (10%)
  other arithmetic  46.6 us (6%)
  local copies, waits for them, and re-layouts  38.8 us (5%)
  between operations  19.7 us (3%)
    pallas_call x1, Pallas kernels, run_experts(): pl.pallas_call(functools.partial(experts_kernel, n_c, experts, slots, com...  209 us
    pallas_call x1, Pallas kernels, gather_to_heads(): pl.pallas_call(functools.partial(gather_kernel, n_c), out_shape=(jax.Shap...  93.7 us
    pallas_call x1, Pallas kernels, finish(): pl.pallas_call(functools.partial(finish_kernel, n_c), out_shape=(jax.Shap...  81.3 us
    dot_general x10, matrix products, mm(): lax.dot_general(left, right, (((1,), (0,)), ((), ())), preferred_element_...  34.7 us
    pallas_call x1, Pallas kernels, to_heads(): pl.pallas_call(to_heads_kernel, out_shape=jax.ShapeDtypeStruct((4, tok, G...  34.3 us
    pallas_call x1, Pallas kernels, to_tokens(): pl.pallas_call(to_tokens_kernel, out_shape=jax.ShapeDtypeStruct((tok, MOD...  33.3 us
    dot_general x7, matrix products, mm_t(): lax.dot_general(left, right, (((1,), (1,)), ((), ())), preferred_element_...  30.9 us
    pallas_call x1, Pallas kernels, attend_back(): pl.pallas_call(attend_back_kernel, grid=(HEADS,), out_shape=(wide(F32), w...  25.3 us
  transfers between devices with their start and end apart: 6, of which 0 were waited for; matrix products, arithmetic and copies ran while one was open for 18% of the time, Pallas kernels for 45%

profile of v3, /device:TPU:9, one launch (start us, length us, event | category | flops | bytes accessed | tf_op | source)
XLA Modules:
  0.0 708.0 jit_solution(4899216128256501136)
XLA Ops:
  15.1 2.1 all-reduce.7
  33.4 2.9 copy.81
  38.1 93.7 %gather_to_heads.1 = (bf16[4,320,2048]{2,1,0:T(8,128)(2,1)}, bf16[2048,1536]{1,0:T(8,128)(2,1)}) custom-call(bf16[320,2048]{1,0:T(8,128)(2,1)} %fusion.5.x_ref, bf16[256,6144]{1,0:T(8,128)(2,1)} %w_ref.1), custom_call_target="tpu_custom_call" | custom-call | tf_op jit(solution)/shard_map/gather_to_heads/pallas_call | solution.py:191
  132.7 2.4 fusion.48
  136.5 12.9 %fusion.78 = f32[1280,1536]{1,0:T(8,128)} fusion(bf16[1280,2048]{1,0:T(8,128)(2,1)S(1)} %bitcast.155, bf16[2048,1536]{1,0:T(8,128)(2,1)} %get-tuple-element.35), kind=kOutput, calls=%fused_computation.206 | convolution fusion | flops 8053063680 | bytes 19398656 | tf_op jit(solution)/shard_map/dot_general | solution.py:35
  153.9 2.5 slice.210
  157.8 6.7 fusion.3.low
  167.0 2.7 copy-done.6
  170.3 4.8 group_sum.2
  178.6 21.1 %attend.1 = (bf16[1280,512]{1,0:T(8,128)(2,1)}, bf16[1280,512]{1,0:T(8,128)(2,1)}, bf16[1280,512]{1,0:T(8,128)(2,1)}, bf16[1280,512]{1,0:T(8,128)(2,1)}, f32[4,1280,1]{2,1,0:T(8,128)}) custom-call(f32[1280,1536]{1,0:T(8,128)} %copy-done.6, f32[1280,1536]{1,0:T(8,128)} %copy-done.6, f32[1280,1536]{1,0:T(8,128)} %copy-done.6, f32[1280,1]{1,0:T(8,128)} %bitcast.133, ...), custom_call_target="tpu_custom_call" | custom-call | tf_op jit(solution)/shard_map/attend/pallas_call | solution.py:564
  199.7 33.3 %to_tokens.1 = bf16[320,2048]{1,0:T(8,128)(2,1)} custom-call(bf16[4,320,512]{2,1,0:T(8,128)(2,1)} %bitcast.139), custom_call_target="tpu_custom_call" | custom-call | tf_op jit(solution)/shard_map/to_tokens/pallas_call | solution.py:245
  235.0 5.7 fusion.79
  241.8 2.2 fusion.43
  247.6 209.3 %experts.1 = (bf16[8,320,2048]{2,1,0:T(8,128)(2,1)}, bf16[8,320,2176]{2,1,0:T(8,128)(2,1)}, bf16[4,1152,256]{2,1,0:T(8,128)(2,1)}, bf16[8,320,2176]{2,1,0:T(8,12...) custom-call(bf16[320,2176]{1,0:T(8,128)(2,1)} %pad_maximum_fusion.2.refs_0_, ...), custom_call_target="tpu_custom_call" | custom-call | flops 111669149696 | bytes 100000000 | tf_op jit(solution)/shard_map/experts/pallas_call | solution.py:1200
  474.2 5.3 fusion.69
  479.5 2.7 fusion.4.a_ref
  482.2 34.3 %to_heads.1 = bf16[4,320,512]{2,1,0:T(8,128)(2,1)} custom-call(bf16[320,2048]{1,0:T(8,128)(2,1)} %fusion.4.a_ref), custom_call_target="tpu_custom_call" | custom-call | tf_op jit(solution)/shard_map/to_heads/pallas_call | solution.py:286
  516.5 4.5 all-to-all-start
  521.0 25.3 %attend_back.1 = (f32[1280,512]{1,0:T(8,128)}, f32[1280,512]{1,0:T(8,128)}, bf16[1280,512]{1,0:T(8,128)(2,1)}, f32[4,1280,1]{2,1,0:T(8,128)}, f32[4,1280,1]{2,1,0:T(8,128)}) custom-call(bf16[1280,512]{1,0:T(8,128)(2,1)} %get-tuple-element.39.q_ref, bf16[1280,512]{1,0:T(8,128)(2,1)} %get-tuple-element.40.k_ref, bf16[1280,512]{1,0:T(8,128)(2,1)} %get-tuple-element.41.v_ref, ...), custom_call_target="tpu_custom_call" | custom-call | tf_op jit(solution)/shard_map/attend_back/pallas_call | solution.py:652
  546.4 2.2 reduce_sum.173
  550.1 9.6 %group_sum.3 = f32[20,128]{1,0:T(8,128)} custom-call(f32[20,128]{1,0:T(8,128)} %reshape.288.x_ref), custom_call_target="tpu_custom_call" | custom-call | tf_op jit(solution)/shard_map/group_sum/pallas_call | solution.py:514
  560.5 3.1 convert_reduce_fusion.1
  563.7 4.2 subtract_convert_fusion.1
  567.9 2.3 pad_maximum_fusion.dp
  570.2 12.2 %late_gradients.1 = (bf16[1280,384]{1,0:T(8,128)(2,1)S(1)}, bf16[8,1152,128]{2,1,0:T(8,128)(2,1)}) custom-call(bf16[1280,1536]{1,0:T(8,128)(2,1)} %pad_maximum_fusion.dp, bf16[384,512]{1,0:T(8,128)(2,1)S(1)} %constant_dynamic-slice_fusion.1.up, f32[1280,128]{1,0:T(8,128)S(1)} %copy-done.1, bf16[1280,384]{1,0:T(8,128)(2,1)S(1)} %copy-done.4, ...), custom_call_target="tpu_custom_call" | custom-call | flops 4000000000 | bytes 20000000 | tf_op jit(solution)/shard_map/late_gradients/pallas_call | solution.py:1243
  582.4 11.0 %fusion.72 = f32[1280,2048]{1,0:T(8,128)} fusion(bf16[2048,1536]{1,0:T(8,128)(2,1)S(1)} %bitcast.152, bf16[1280,512]{1,0:T(8,128)(2,1)S(1)} %copy-done.22, bf16[1280,512]{1,0:T(8,128)(2,1)S(1)} %get-tuple-element.64, bf16[1280,512]{1,0:T(8,128)(2,1)S(1)} %get-tuple-element.63), kind=kOutput, calls=%fused_computation.200 | convolution fusion | flops 8064860160 | bytes 20709376 | tf_op jit(solution)/shard_map/dot_general | solution.py:39
  593.4 7.8 %add_convert_fusion = bf16[1280,2048]{1,0:T(8,128)(2,1)} fusion(f32[1280,2048]{1,0:T(8,128)} %fusion.72, bf16[1280,384]{1,0:T(8,128)(2,1)S(1)} %get-tuple-element.50, bf16[2048,1280]{1,0:T(8,128)(2,1)} %all-gather.6.cloned.1.call-done), kind=kOutput, calls=%fused_computation | convolution fusion | flops 2018508800 | bytes 18284544 | tf_op jit(solution)/shard_map/dot_general | solution.py:39
  602.2 81.3 %finish.1 = (f32[320,2048]{1,0:T(8,128)}, f32[592,128]{1,0:T(8,128)S(1)}) custom-call(bf16[4,320,2048]{2,1,0:T(8,128)(2,1)} %bitcast.124, bf16[8,1152,128]{2,1,0:T(8,128)(2,1)S(1)} %copy-done.2, bf16[832,128]{1,0:T(8,128)(2,1)S(1)} %copy-done.5), custom_call_target="tpu_custom_call" | custom-call | tf_op jit(solution)/shard_map/finish/pallas_call | solution.py:469
  683.6 2.3 fusion.11
  688.1 4.5 fusion.9
  692.6 2.2 convert_reduce_fusion
  698.5 2.8 fusion.16
  (244 shorter events, 68.5 us)
Async XLA Ops:
  7.2 142.2 %all-gather.6.cloned.1.call-start = ((), (), s32[]{:S(2)}) async-start(), calls=%async_computation.3 | async-start | bytes 5898240 | tf_op jit(solution)/shard_map/all_gather | solution.py:1318
  10.0 4.9 copy-start.39
  10.0 4.9 copy-start.41
  11.1 18.7 %copy-start.40 = (s32[1,320,8]{1,2,0:T(8,128)S(1)}, s32[1,320,8]{1,2,0:T(8,128)}, u32[]{:S(2)}) copy-start(s32[1,320,8]{1,2,0:T(8,128)} %param.26) | copy-start | bytes 30724
  12.1 222.9 %all-gather.8.cloned.1.call-start = ((), (), s32[]{:S(2)}) async-start(), calls=%async_computation.4 | async-start | bytes 9437184 | tf_op jit(solution)/shard_map/all_gather | solution.py:1329
  12.8 234.8 %all-gather.10.cloned.1.call-start = ((), (), s32[]{:S(2)}) async-start(), calls=%async_computation.7 | async-start | bytes 11796480 | tf_op jit(solution)/shard_map/all_gather | solution.py:1330
  13.5 587.7 %reduce-scatter.5.cloned.1.call-start = ((), (), s32[]{:S(2)}) async-start(), calls=%async_computation.6 | async-start | bytes 1916928 | tf_op jit(solution)/shard_map/reduce_scatter | solution.py:1468
  31.7 4.6 copy-start
  36.7 95.1 %copy-start.37 = (f32[320]{0:T(512)}, f32[320]{0:T(512)S(1)}, u32[]{:S(2)}) copy-start(f32[320]{0:T(512)S(1)} %add_rsqrt_fusion.2) | copy-start | bytes 3844
  156.5 8.1 %slice-start = ((s8[7864320]{0:T(1024)(128)(4,1)}), s8[4194304]{0:T(1024)(128)(4,1)S(1)}, s32[]{:S(2)}) async-start(s8[7864320]{0:T(1024)(128)(4,1)} %bitcast.126), calls=%async_computation.8 | async-start | bytes 8388608
  157.7 6.8 slice-start.1
  175.8 23.9 %copy-start.27 = (f32[20,128]{1,0:T(8,128)}, f32[20,128]{1,0:T(8,128)S(1)}, u32[]{:S(2)}) copy-start(f32[20,128]{1,0:T(8,128)S(1)} %add_rsqrt_fusion) | copy-start | bytes 30724
  235.0 5.7 copy-start.24
  241.8 4.6 copy-start.16
  241.8 4.4 copy-start.26
  241.8 4.4 copy-start.29
  465.5 8.7 %copy-start.12 = (f32[320,2048]{1,0:T(8,128)}, f32[320,2048]{1,0:T(8,128)S(1)}, u32[]{:S(2)}) copy-start(f32[320,2048]{1,0:T(8,128)S(1)} %convert_add_fusion.1) | copy-start | bytes 7864324
  472.5 225.9 %reduce-scatter.3.cloned.1.call-start = ((), (), s32[]{:S(2)}) async-start(), calls=%async_computation.5 | async-start | bytes 11796480 | tf_op jit(solution)/shard_map/reduce_scatter | solution.py:1427
  516.5 176.1 %all-to-all-start = ((bf16[4,1152,256]{2,1,0:T(8,128)(2,1)}), bf16[4,1152,256]{2,1,0:T(8,128)(2,1)}, u32[]{:S(2)}, u32[]{:S(2)}) async-start(bf16[4,1152,256]{2,1,0:T(8,128)(2,1)} %get-tuple-element.57), calls=%async_computation.2 | async-start | bytes 4718592 | tf_op jit(solution)/shard_map/all_to_all | solution.py:1451
  549.2 14.4 %copy-start.32 = (f32[512]{0:T(512)S(1)}, f32[512]{0:T(512)}, u32[]{:S(2)}) copy-start(f32[512]{0:T(512)} %dynamic_slice.15) | copy-start | bytes 6148
  549.2 14.4 %copy-start.33 = (f32[512]{0:T(512)S(1)}, f32[512]{0:T(512)}, u32[]{:S(2)}) copy-start(f32[512]{0:T(512)} %dynamic_slice.16) | copy-start | bytes 6148
  549.2 14.4 %copy-start.34 = (f32[1280]{0:T(1024)S(1)}, f32[1280]{0:T(1024)}, u32[]{:S(2)}) copy-start(f32[1280]{0:T(1024)} %get-tuple-element.77) | copy-start | bytes 15364
  549.2 14.4 %copy-start.35 = (f32[1280]{0:T(1024)S(1)}, f32[1280]{0:T(1024)}, u32[]{:S(2)}) copy-start(f32[1280]{0:T(1024)} %get-tuple-element.78) | copy-start | bytes 15364
  549.5 14.2 %copy-start.21 = (f32[1280,512]{1,0:T(8,128)S(1)}, f32[1280,512]{1,0:T(8,128)}, u32[]{:S(2)}) copy-start(f32[1280,512]{1,0:T(8,128)} %get-tuple-element.45) | copy-start | bytes 7864324
  567.9 14.5 %slice-start.2 = ((s8[6291456]{0:T(1024)(128)(4,1)}), s8[4194304]{0:T(1024)(128)(4,1)S(1)}, s32[]{:S(2)}) async-start(s8[6291456]{0:T(1024)(128)(4,1)} %bitcast.151), calls=%async_computation.10 | async-start | bytes 8388608
  570.2 12.2 %slice-start.3 = ((s8[6291456]{0:T(1024)(128)(4,1)}), s8[2097152]{0:T(1024)(128)(4,1)S(1)}, s32[]{:S(2)}) async-start(s8[6291456]{0:T(1024)(128)(4,1)} %bitcast.151), calls=%async_computation.11 | async-start | bytes 4194304
  593.4 7.9 %copy-start.2 = (bf16[8,1152,128]{2,1,0:T(8,128)(2,1)S(1)}, bf16[8,1152,128]{2,1,0:T(8,128)(2,1)}, u32[]{:S(2)}) copy-start(bf16[8,1152,128]{2,1,0:T(8,128)(2,1)} %get-tuple-element.51.late) | copy-start | bytes 7077892
  602.2 81.4 %copy-start.15 = (bf16[1,320,2048]{2,1,0:T(8,128)(2,1)S(1)}, bf16[1,320,2048]{2,1,0:T(8,128)(2,1)}, u32[]{:S(2)}) copy-start(bf16[1,320,2048]{2,1,0:T(8,128)(2,1)} %param.22) | copy-start | bytes 3932164
  602.2 81.4 %copy-start.31 = (f32[2048]{0:T(1024)S(1)}, f32[2048]{0:T(1024)}, u32[]{:S(2)}) copy-start(f32[2048]{0:T(1024)} %param.27) | copy-start | bytes 24580
  683.5 4.5 copy-start.13
  683.6 4.5 copy-start.38
  688.1 4.6 copy-start.42
  (23 other events, 56.2 us)
Sparse Core Ops, SparseCore 0:
  12.2 83.9 all-gather.5
  98.0 66.0 all-gather.7
  166.0 63.2 all-gather.9
  472.7 37.9 reduce-scatter.4
  514.4 81.5 reduce-scatter.2

commit v4 on v3

--- a/solution.py
+++ b/solution.py
@@ -208,6 +208,195 @@
         compiler_params=pltpu.CompilerParams(collective_id=0, has_side_effects=True),
         name="gather_to_heads",
     )(x, w)
+
+
+PROJECT_WIDTH = 3 * GROUP_WIDTH + 3 * SPAN
+
+
+def project_kernel(x_ref, w_ref, down_ref, up_ref, mask, xg_o, wg_o, upg, proj_o, low, acc, xg, wg, xs, xr, fs, fr, ws, wr, us, ur, own, out):
+    zh, zl, c, core = here()
+    tok = x_ref.shape[0]
+    half = tok // 2
+    rows = w_ref.shape[0]
+    up_rows = up_ref.shape[0]
+    near = lambda i: (
+        lax.rem(c // 2 + i // 2, 2) * 2 + lax.rem(lax.rem(c, 2) + lax.rem(i, 2), 2)
+    )
+    chips = [near(i) for i in range(4)]
+    plane = [(zh, zl, chips[i], core ^ k) for i in range(4) for k in range(2)]
+    sibling, beside, above = plane[1], plane[2], plane[4]
+    signal_all(column_peers(zh, zl, c, core) + plane[2:])
+    me = zh * 2 + zl
+    f = c * 2 + core
+    block = lambda source: wg.at[pl.ds(pl.multiple_of(source * rows, rows), rows)]
+    source = lambda i, k: chips[i] * 2 + k
+
+    def pieces(group):
+        to = pl.ds(pl.multiple_of(f * rows, rows), rows)
+        for j in range(3):
+            start = pl.multiple_of(j * MODEL_WIDTH + group * GROUP_WIDTH, GROUP_WIDTH)
+            yield (
+                w_ref.at[:, pl.ds(start, GROUP_WIDTH)],
+                wg.at[to, pl.ds(j * GROUP_WIDTH, GROUP_WIDTH)],
+            )
+        yield down_ref, wg.at[to, pl.ds(3 * GROUP_WIDTH, 3 * SPAN)]
+
+    for src, dst in pieces(zl * 2 + core):
+        pltpu.make_async_copy(src, dst, own.at[0]).start()
+    for src, dst in pieces(zl * 2 + 1 - core):
+        remote(src, dst, ws.at[0], wr.at[0], sibling).start()
+    for a in range(2):
+        for k in range(2):
+            piece = pl.ds(k * half, half)
+            src, dst = x_ref.at[piece], xg.at[me, piece]
+            is_self = (core == zh) & (zl == a) & (core == k)
+
+            @pl.when(is_self)
+            def _():
+                pltpu.make_async_copy(src, dst, xr.at[me]).start()
+
+            @pl.when(jnp.logical_not(is_self))
+            def _():
+                remote(src, dst, xs.at[a, k], xr.at[me], (core, a, c, k)).start()
+
+    wait_for(block(f), own.at[0])
+    remote(block(f), block(f), ws.at[1], wr.at[1], beside).start()
+    remote(block(f), block(f), ws.at[2], wr.at[2], above).start()
+    up_to = pl.ds(pl.multiple_of(f * up_rows, up_rows), up_rows)
+    for n, peer in enumerate(plane):
+        start = pl.multiple_of((zl * 2 + peer[3]) * GROUP_WIDTH, GROUP_WIDTH)
+        src, dst = up_ref.at[:, pl.ds(start, GROUP_WIDTH)], upg.at[up_to]
+        if n:
+            remote(src, dst, us.at[n], ur.at[n], peer).start()
+        else:
+            pltpu.make_async_copy(src, dst, own.at[1]).start()
+    other = c * 2 + 1 - core
+    wait_for(block(other), wr.at[0])
+    remote(block(other), block(other), ws.at[3], wr.at[3], beside).start()
+    remote(block(other), block(other), ws.at[4], wr.at[4], above).start()
+    mine = pl.ds(pl.multiple_of(core * half, half), half)
+    theirs = pl.ds(pl.multiple_of((1 - core) * half, half), half)
+
+    shards = [k + zh * (3 - 2 * k) for k in range(4)]
+
+    def pass_tokens(k):
+        s = shards[k]
+        wait_for(xg.at[s, mine], xr.at[s])
+        remote(xg.at[s, mine], xg.at[s, mine], fs.at[s], fr.at[s], sibling).start()
+
+    def take_tokens(k):
+        s = shards[k]
+        wait_for(xg.at[s, theirs], fr.at[s])
+        pltpu.make_async_copy(xg.at[s], xg_o.at[s], out.at[0]).start()
+
+    def multiply(i, k):
+        at = pl.ds(pl.multiple_of(chips[i] * (2 * rows), 2 * rows), 2 * rows)
+        s = shards[k]
+        value = mm(xg[s, :, at], wg[at, :])
+        acc[s] = value if i == 0 else acc[s] + value
+
+    own_x, other_x = source(1, core), source(1, 1 - core)
+    own_y, other_y = source(2, core), source(2, 1 - core)
+    pass_tokens(0)
+    take_tokens(0)
+    multiply(0, 0)
+    wait_for(block(own_x), wr.at[1])
+    remote(block(own_x), block(own_x), ws.at[5], wr.at[5], above).start()
+    pass_tokens(1)
+    take_tokens(1)
+    multiply(0, 1)
+    wait_for(block(own_y), wr.at[2])
+    wait_for(block(other_y), wr.at[4])
+    remote(block(other_y), block(other_y), ws.at[6], wr.at[6], beside).start()
+    pass_tokens(2)
+    wait_for(block(other_x), wr.at[3])
+    for k in range(2):
+        multiply(1, k)
+        multiply(2, k)
+    take_tokens(2)
+    for i in range(3):
+        multiply(i, 2)
+    pass_tokens(3)
+    take_tokens(3)
+    for i in range(3):
+        multiply(i, 3)
+    wait_for(block(source(3, core)), wr.at[5])
+    wait_for(block(source(3, 1 - core)), wr.at[6])
+    save = pltpu.make_async_copy(wg, wg_o, out.at[1])
+    save.start()
+    for k in range(4):
+        multiply(3, k)
+    up_block = lambda n: upg.at[pl.ds(pl.multiple_of(n * up_rows, up_rows), up_rows)]
+    wait_for(up_block(f), own.at[1])
+    for n, peer in enumerate(plane):
+        if n:
+            wait_for(up_block(peer[2] * 2 + peer[3]), ur.at[n])
+
+    for s in range(4):
+        for j in range(3):
+            span = slice(j * SPAN, (j + 1) * SPAN)
+            wide = slice(j * GROUP_WIDTH, (j + 1) * GROUP_WIDTH)
+            at = 3 * GROUP_WIDTH + j * SPAN
+            lowered = (acc[s, :, at : at + SPAN] * mask[s]).astype(BF)
+            low[s, :, span] = lowered
+            acc[s, :, wide] = acc[s, :, wide] + mm(lowered, upg[span])
+        pltpu.make_async_copy(acc.at[s, :, pl.ds(0, 3 * GROUP_WIDTH)], proj_o.at[s], out.at[2]).start()
+
+    for s in range(4):
+        wait_for(xg.at[s, mine], fs.at[s])
+    for a in range(2):
+        for k in range(2):
+            is_self = (core == zh) & (zl == a) & (core == k)
+
+            @pl.when(jnp.logical_not(is_self))
+            def _():
+                wait_for(x_ref.at[pl.ds(k * half, half)], xs.at[a, k])
+
+    save.wait()
+    wait_for(xg_o, out.at[0])
+    wait_for(proj_o, out.at[2])
+    for n in range(7):
+        wait_for(block(f), ws.at[n])
+    for n in range(1, 8):
+        wait_for(up_block(f), us.at[n])
+
+
+def gather_project(x, w, down3, up, mask):
+    tok, rows = x.shape[0], w.shape[0]
+    dma = pltpu.SemaphoreType.DMA
+    vmem = pl.BlockSpec(memory_space=VMEM)
+    hbm = pl.BlockSpec(memory_space=ANY)
+    return pl.pallas_call(
+        project_kernel,
+        out_shape=(
+            jax.ShapeDtypeStruct((4, tok, MODEL_WIDTH), BF),
+            jax.ShapeDtypeStruct((8 * rows, PROJECT_WIDTH), BF),
+            jax.ShapeDtypeStruct((8 * up.shape[0], GROUP_WIDTH), BF),
+            jax.ShapeDtypeStruct((4, tok, 3 * GROUP_WIDTH), F32),
+            jax.ShapeDtypeStruct((4, tok, 3 * SPAN), BF),
+        ),
+        in_specs=[vmem] * 5,
+        out_specs=[hbm, hbm, vmem, hbm, vmem],
+        scratch_shapes=[
+            VMEM((4, tok, PROJECT_WIDTH), F32),
+            VMEM((4, tok, MODEL_WIDTH), BF),
+            VMEM((8 * rows, PROJECT_WIDTH), BF),
+            dma((2, 2)),
+            dma((4,)),
+            dma((4,)),
+            dma((4,)),
+            dma((7,)),
+            dma((7,)),
+            dma((8,)),
+            dma((8,)),
+            dma((2,)),
+            dma((3,)),
+        ],
+        compiler_params=pltpu.CompilerParams(
+            collective_id=8, has_side_effects=True, vmem_limit_bytes=58 * 2**20
+        ),
+        name="gather_project",
+    )(x, w, down3, up, mask)
 
 
 def to_tokens_kernel(a_ref, o_ref, send, recv):
@@ -584,6 +773,87 @@
     )(projected, projected, projected, rq, rk, gq, gk, cosine, sine, seg_c, seg_r)
 
 
+def attend_send_kernel(
+    pq, pk, pv, rq, rk, gq, gk, cosine, sine, seg_c, seg_r, q_ref, k_ref, v_ref, lse_ref, o_ref, held, send, recv
+):
+    zh, zl, c, core = here()
+    h = pl.program_id(0)
+    tok = o_ref.shape[0]
+    group = zl * 2 + core
+
+    @pl.when(h == 0)
+    def _():
+        signal_all(column_peers(zh, zl, c, core))
+
+    attend_kernel(
+        pq, pk, pv, rq, rk, gq, gk, cosine, sine, seg_c, seg_r, q_ref, k_ref, v_ref, held.at[h], lse_ref
+    )
+    columns = pl.ds(pl.multiple_of(group * GROUP_WIDTH + h * HD, HD), HD)
+    is_self = lambda s: (s // 2 == zh) & (s % 2 == zl) & (core == zh)
+    for s in range(4):
+        src, dst = held.at[h, pl.ds(s * tok, tok)], o_ref.at[:, columns]
+
+        @pl.when(is_self(s))
+        def _():
+            pltpu.make_async_copy(src, dst, recv.at[group, h]).start()
+
+        @pl.when(jnp.logical_not(is_self(s)))
+        def _():
+            remote(src, dst, send.at[s, h], recv.at[group, h], (s // 2, s % 2, c, zh)).start()
+
+    @pl.when(h == HEADS - 1)
+    def _():
+        for n in range(HEADS):
+            for s in range(4):
+                got = o_ref.at[:, pl.ds(s * GROUP_WIDTH + n * HD, HD)]
+                wait_for(got, recv.at[s, n])
+
+                @pl.when(jnp.logical_not(is_self(s)))
+                def _():
+                    wait_for(held.at[n, pl.ds(0, tok)], send.at[s, n])
+
+
+def attend_send(projected, rq, rk, gq, gk, cosine, sine, seg_c, seg_r):
+    block = projected.shape[0]
+    tok = block // 4
+    dma = pltpu.SemaphoreType.DMA
+    head = lambda off: pl.BlockSpec((block, HD), lambda h: (0, off + h))
+    gain = pl.BlockSpec((1, HD), lambda h: (0, h))
+    fixed = lambda shape: pl.BlockSpec(shape, lambda h: (0, 0))
+    wide = jax.ShapeDtypeStruct((block, GROUP_WIDTH), BF)
+    return pl.pallas_call(
+        attend_send_kernel,
+        grid=(HEADS,),
+        out_shape=(
+            wide,
+            wide,
+            wide,
+            jax.ShapeDtypeStruct((HEADS, block, 1), F32),
+            jax.ShapeDtypeStruct((tok, MODEL_WIDTH), BF),
+        ),
+        in_specs=[
+            head(0),
+            head(HEADS),
+            head(2 * HEADS),
+            fixed((block, 1)),
+            fixed((block, 1)),
+            gain,
+            gain,
+            fixed((block, HD)),
+            fixed((block, HD)),
+            fixed((block, 1)),
+            fixed((1, block)),
+        ],
+        out_specs=[head(0)] * 3
+        + [pl.BlockSpec((1, block, 1), lambda h: (h, 0, 0)), pl.BlockSpec(memory_space=ANY)],
+        scratch_shapes=[VMEM((HEADS, block, HD), BF), dma((4, HEADS)), dma((4, HEADS))],
+        compiler_params=pltpu.CompilerParams(
+            collective_id=9, has_side_effects=True, vmem_limit_bytes=60 * 2**20
+        ),
+        name="attend_send",
+    )(projected, projected, projected, rq, rk, gq, gk, cosine, sine, seg_c, seg_r)
+
+
 def attend_back_kernel(
     q_ref,
     k_ref,
@@ -695,8 +965,11 @@
 
 
 def experts_kernel(n_c, experts, slots, comm, *refs):
-    x_ref, g_ref, h_gu, h_d, h_id, h_iu, h_od, h_ou = refs[:8]
-    refs = refs[8:]
+    n_g = 10 if comm else 1
+    x_ref, g_refs = refs[0], refs[1 : 1 + n_g]
+    refs = refs[1 + n_g :]
+    h_gu, h_d, h_id, h_iu, h_od, h_ou = refs[:6]
+    refs = refs[6:]
     out_ref, row_ref, terms_o = refs[:3]
     refs = refs[3:]
     if comm:
@@ -818,15 +1091,27 @@
         pltpu.make_async_copy(x_ref, xw.at[core], csem.at[0]).start()
         pltpu.make_async_copy(other, xw.at[1 - core], csem.at[0]).start()
 
-    def fetch_g(p):
-        return pltpu.make_async_copy(pair(g_ref, p), gw, csem.at[1])
+    def fetch_g(i):
+        if not comm:
+            pltpu.make_async_copy(pair(g_refs[0], i), gw, csem.at[1]).start()
+            return
+        for n in range(4):
+
+            @pl.when(i == n)
+            def _():
+                for k, held in ((core, g_refs[:5]), (1 - core, g_refs[5:])):
+                    if n < 3:
+                        pltpu.make_async_copy(held[n], gw.at[k], csem.at[1]).start()
+                    else:
+                        pltpu.make_async_copy(held[3], gw.at[k, low_half], csem.at[1]).start()
+                        pltpu.make_async_copy(held[4], gw.at[k, high_half], csem.at[1]).start()
 
     if comm:
-        fetch_g(c).start()
+        fetch_g(0)
         wait_for(xg_ref.at[c * 2 + 1 - core], recvx.at[0])
         fetch_own()
     else:
-        fetch_g(0).start()
+        fetch_g(0)
         fetch_x(0).start()
 
     def write_out(p):
@@ -856,10 +1141,10 @@
 
     def step(s, carry):
         e, i, p = order(s)
-        _, _, after = order(jnp.minimum(s + 1, steps - 1))
+        _, after_i, after = order(jnp.minimum(s + 1, steps - 1))
         number = c * (2 * EXP_DEV) + core * EXP_DEV + e
         fetch_x(p).wait()
-        fetch_g(p).wait()
+        wait_for(gw, csem.at[1])
         lane = lax.broadcasted_iota(jnp.int32, (tok, extra), 1)
         lane_s = lax.broadcasted_iota(jnp.int32, (slots, extra), 1)
         for d in range(2):
@@ -934,7 +1219,7 @@
 
         @pl.when(s < steps - 1)
         def _():
-            fetch_g(after).start()
+            fetch_g(after_i)
 
         dr[:, MODEL_WIDTH:] = (
             mm_t(dr[:, :MODEL_WIDTH], db[EXPERT_HIDDEN:, :MODEL_WIDTH]) * mask[...]
@@ -1197,16 +1482,17 @@
         ]
         params = dict(collective_id=6, has_side_effects=True)
     flops = 2 * sources * EXP_DEV * slots * MODEL_WIDTH * EXPERT_HIDDEN * 8
+    g = g if comm else [g]
     results = pl.pallas_call(
         functools.partial(experts_kernel, n_c, experts, slots, comm),
         out_shape=out_shape,
-        in_specs=[any_spec] * 8,
+        in_specs=[any_spec] * (7 + len(g)),
         out_specs=out_specs,
         scratch_shapes=scratch,
         compiler_params=pltpu.CompilerParams(vmem_limit_bytes=63 * 2**20, **params),
         cost_estimate=pl.CostEstimate(flops=flops, bytes_accessed=10**8, transcendentals=10**7),
         name="experts",
-    )(x, g, *weights)
+    )(x, *g, *weights)
     if comm:
         return results[0], results[4], (results[5], results[2])
     return results[0], results[1], results[2]
@@ -1252,6 +1538,16 @@
         cost_estimate=pl.CostEstimate(flops=4 * 10**9, bytes_accessed=2 * 10**7, transcendentals=0),
         name="late_gradients",
     )(grad_projected, up_own, mask, lowered, x)
+
+
+def plane_rows(rows):
+    half = rows.shape[0] // 2
+    along_x = lambda t: lax.ppermute(t, "c", [(0, 1), (1, 0), (2, 3), (3, 2)])
+    along_y = lambda t: lax.ppermute(t, "c", [(0, 2), (2, 0), (1, 3), (3, 1)])
+    to_sibling = lambda t: lax.ppermute(t, "core", [(0, 1), (1, 0)])
+    beside, above = along_x(rows), along_y(rows)
+    parts = [rows, beside, above, along_y(beside[:half]), along_x(above[half:])]
+    return parts + [to_sibling(t) for t in parts]
 
 
 def on_device(
@@ -1300,12 +1596,28 @@
 
     inputs = tokens[0].astype(F32)
     normalized = rms_scale(inputs, gain_attn).astype(BF)
-    x_shards, qkv_rows = gather_to_heads(normalized, query_key_value_weight, n_c)
-
+    seq_block, block_offsets, block_sets = token_meta(
+        held_lengths[:count], held_lengths[count:], jnp.arange(block, dtype=jnp.int32)
+    )
+    mask1 = set_mask(block_sets)
+    if n_c == 4:
+        x_shards, head_rows, up_group, projected, lowered = gather_project(
+            normalized,
+            query_key_value_weight,
+            attention_down_factors[:, :span3],
+            attention_up_factors,
+            mask1.reshape(4, tok, SPAN),
+        )
+        projected, lowered = projected.reshape(block, -1), lowered.reshape(block, span3)
+        up_own = up_group[:span3]
+    else:
+        x_shards, qkv_rows = gather_to_heads(normalized, query_key_value_weight, n_c)
+
+    first_column = span3 if n_c == 4 else 0
     rows_local = query_key_value_weight.shape[0]
     factors = jnp.concatenate(
         [
-            attention_down_factors,
+            attention_down_factors[:, first_column:],
             attention_up_factors.reshape(rows_local, -1),
             router_down_factors,
             router_weight,
@@ -1317,8 +1629,9 @@
     factors = jnp.pad(factors, ((0, 0), (0, -factor_width % 128)))
     factors = lax.all_gather(factors, FSDP, axis=0, tiled=True)
     up_columns = attention_up_factors.size // rows_local
-    down_full = factors[:, : 4 * SPAN]
-    at = 4 * SPAN
+    at = 4 * SPAN - first_column
+    down_full = factors[:, :at]
+    down_o = down_full[:, span3 - first_column :]
     up_full = factors[:, at : at + up_columns].reshape(4 * SPAN, MODEL_WIDTH)
     at += up_columns
     rdown_full = factors[:, at : at + SPAN]
@@ -1326,18 +1639,19 @@
     router_full = factors[:, at : at + experts]
     at += experts
     rup_full = factors[:, at:factor_width].reshape(SPAN, experts)
+    if n_c == 4:
+        projected, out_weight, rows = lax.optimization_barrier(
+            (projected, out_weight, cotangent[0])
+        )
+        grads_all = plane_rows(rows)
+    else:
+        grads_all = lax.all_gather(cotangent[0], FSDP, axis=0, tiled=False)
     out_full = lax.all_gather(out_weight, FSDP, axis=0, tiled=True)
-    grad_rows_all = lax.all_gather(cotangent[0], FSDP, axis=0, tiled=True)
 
     seq_local, _, chosen = token_meta(
         lengths[0], sets[0], shard * tok + jnp.arange(tok, dtype=jnp.int32)
     )
     mask = set_mask(chosen)
-    seq_block, block_offsets, block_sets = token_meta(
-        held_lengths[:count], held_lengths[count:], jnp.arange(block, dtype=jnp.int32)
-    )
-    mask1 = set_mask(block_sets)
-    mask3 = jnp.tile(mask1, (1, 3))
     half = HD // 2
     freqs = THETA ** (-(jnp.arange(half, dtype=F32) * 2.0 / HD))
     angles = block_offsets.astype(F32)[:, None] * freqs[None, :]
@@ -1347,20 +1661,22 @@
     seg_c, seg_r = seq_block[:, None], seq_block[None, :]
 
     x_all = x_shards.reshape(block, MODEL_WIDTH)
-    down3 = down_full[:, :span3]
-    lowered = (mm(x_all, down3) * mask3).astype(BF)
-    up_own = lax.dynamic_slice_in_dim(up_full[:span3], group * GROUP_WIDTH, GROUP_WIDTH, 1)
-    none = jnp.zeros((SPAN, GROUP_WIDTH), BF)
-    up_diagonal = jnp.concatenate(
-        [
-            jnp.concatenate(
-                [up_own[j * SPAN : (j + 1) * SPAN] if i == j else none for i in range(3)], axis=1
-            )
-            for j in range(3)
-        ],
-        axis=0,
-    )
-    projected = mm(x_all, qkv_rows) + mm(lowered, up_diagonal)
+    if n_c != 4:
+        mask3 = jnp.tile(mask1, (1, 3))
+        down3 = down_full[:, :span3]
+        lowered = (mm(x_all, down3) * mask3).astype(BF)
+        up_own = lax.dynamic_slice_in_dim(up_full[:span3], group * GROUP_WIDTH, GROUP_WIDTH, 1)
+        none = jnp.zeros((SPAN, GROUP_WIDTH), BF)
+        up_diagonal = jnp.concatenate(
+            [
+                jnp.concatenate(
+                    [up_own[j * SPAN : (j + 1) * SPAN] if i == j else none for i in range(3)], axis=1
+                )
+                for j in range(3)
+            ],
+            axis=0,
+        )
+        projected = mm(x_all, qkv_rows) + mm(lowered, up_diagonal)
     part_q, part_k = projected[:, :GROUP_WIDTH], projected[:, GROUP_WIDTH : 2 * GROUP_WIDTH]
 
     def over_group(first, second, identity):
@@ -1374,12 +1690,17 @@
         lax.dynamic_slice_in_dim(g, group * GROUP_WIDTH, GROUP_WIDTH)[None, :]
         for g in (gain_query, gain_key)
     ]
-    q, k, v, attended_heads, lse = attend(
-        projected, rq, rk, *gains, cosine, sine, seg_c, seg_r
-    )
-    attended = to_tokens(attended_heads.reshape(4, tok, GROUP_WIDTH))
-
-    down_o, up_o = down_full[:, span3:], up_full[span3:]
+    if n_c == 4:
+        q, k, v, lse, attended = attend_send(
+            projected, rq, rk, *gains, cosine, sine, seg_c, seg_r
+        )
+    else:
+        q, k, v, attended_heads, lse = attend(
+            projected, rq, rk, *gains, cosine, sine, seg_c, seg_r
+        )
+        attended = to_tokens(attended_heads.reshape(4, tok, GROUP_WIDTH))
+
+    up_o = up_full[span3:]
     out_lower = (mm(attended, down_o) * mask).astype(BF)
     branch = mm(attended, out_full) + mm(out_lower, up_o)
     middle = inputs + branch
@@ -1411,7 +1732,6 @@
         expert_output_down,
         expert_output_up,
     )
-    grads_all = grad_rows_all.reshape(n_fsdp, tok, MODEL_WIDTH)
     if n_c == 4:
         out_parts, returned, expert_terms = run_experts(
             payload, grads_all, weights, experts, slots, n_c, True
@@ -1489,7 +1809,13 @@
         )
     else:
         grad_lowered = (mm_t(grad_projected, up_diagonal) * mask3).astype(BF)
-    grad_normed_part = (mm_t(grad_projected, qkv_rows) + mm_t(grad_lowered, down3)).astype(BF)
+    if n_c == 4:
+        both = jnp.concatenate([grad_projected, grad_lowered], axis=1)
+        grad_normed_part = mm_t(both, head_rows).astype(BF)
+    else:
+        grad_normed_part = (
+            mm_t(grad_projected, qkv_rows) + mm_t(grad_lowered, down3)
+        ).astype(BF)
     grad_normed_part = grad_normed_part.reshape(4, tok, MODEL_WIDTH)
     if n_c == 4:
         grad_normed, flat = finish(grad_normed_part, late, early, n_c)

time: 717 us -> 686 us (0.957)
  matrix products: 69.3 us -> 43.5 us
  Pallas kernels: 525 us -> 513 us
  local copies, waits for them, and re-layouts: 38.8 us -> 28.6 us
  waiting for transfers between devices: 1.96 us -> 11.9 us
    dot_general x10 -> x7, matrix products: 34.7 us -> 12.8 us  [mm(): lax.dot_general(left, right, (((1,), (0,)), ((), ())), preferred_element_...]
    ppermute x0 -> x9, waiting for transfers between devices: none -> 11.4 us  [the longest x2 11.4 us: plane_rows(): along_x = lambda t: lax.ppermute(t, 'c', [(0, 1), (1, 0), (2, 3), (3, 2)])]
    pallas_call x3 -> x2, Pallas kernels: 148 us -> 141 us  [the longest x1 95.6 us: gather_project(): pl.pallas_call(project_kernel, out_shape=(jax.ShapeDtypeStruct((4, tok, M...]
    dot_general x7 -> x6, matrix products: 30.9 us -> 28.6 us  [mm_t(): lax.dot_general(left, right, (((1,), (1,)), ((), ())), preferred_element_...]
  transfers between devices with their start and end apart: 6 -> 14, of which waited for: 0 -> 1; matrix products, arithmetic and copies ran while one was open for 18% -> 14% of each run, Pallas kernels for 45% -> 45%
where the time goes in v4:
time: 686 us; the launch traced here: 681 us
  Pallas kernels  513 us (75%)
  other arithmetic  50.3 us (7%)
  matrix products  43.5 us (6%)
  local copies, waits for them, and re-layouts  28.6 us (4%)
  between operations  19.7 us (3%)
  waiting for transfers between devices  11.9 us (2%)
  starting transfers between devices  11.3 us (2%)
    pallas_call x1, Pallas kernels, run_experts(): pl.pallas_call(functools.partial(experts_kernel, n_c, experts, slots, com...  207 us
    pallas_call x1, Pallas kernels, gather_project(): pl.pallas_call(project_kernel, out_shape=(jax.ShapeDtypeStruct((4, tok, M...  95.6 us
    pallas_call x1, Pallas kernels, finish(): pl.pallas_call(functools.partial(finish_kernel, n_c), out_shape=(jax.Shap...  81.5 us
    pallas_call x1, Pallas kernels, attend_send(): pl.pallas_call(attend_send_kernel, grid=(HEADS,), out_shape=(wide, wide,...  45.4 us
    pallas_call x1, Pallas kernels, to_heads(): pl.pallas_call(to_heads_kernel, out_shape=jax.ShapeDtypeStruct((4, tok, G...  34 us
    dot_general x6, matrix products, mm_t(): lax.dot_general(left, right, (((1,), (1,)), ((), ())), preferred_element_...  28.6 us
    pallas_call x1, Pallas kernels, attend_back(): pl.pallas_call(attend_back_kernel, grid=(HEADS,), out_shape=(wide(F32), w...  25 us
    pallas_call x2, Pallas kernels, group_sum(): pl.pallas_call(group_sum_kernel, out_shape=jax.ShapeDtypeStruct(values.sh...  13.8 us
  transfers between devices with their start and end apart: 14, of which 1 were waited for; matrix products, arithmetic and copies ran while one was open for 14% of the time, Pallas kernels for 45%

profile of v4, /device:TPU:9, one launch (start us, length us, event | category | flops | bytes accessed | tf_op | source)
XLA Modules:
  0.0 680.9 jit_solution(13648794005915489909)
XLA Ops:
  14.5 2.1 all-reduce.5
  24.5 95.6 %gather_project.1 = (bf16[4,320,2048]{2,1,0:T(8,128)(2,1)}, bf16[2048,1920]{1,0:T(8,128)(2,1)}, bf16[512,512]{1,0:T(8,128)(2,1)}, f32[4,320,1536]{2,1,0:T(8,128)}, bf16[4,320,384]{2,1,0:T(8,128)(2,1)}) custom-call(bf16[320,2048]{1,0:T(8,128)(2,1)} %fusion.10.x_ref, bf16[256,6144]{1,0:T(8,128)(2,1)} %w_ref.1, bf16[256,384]{1,0:T(8,128)(2,1)} %slice.195.down_ref, ...), custom_call_target="tpu_custom_call" | custom-call | tf_op jit(solution)/shard_map/gather_project/pallas_call | solution.py:369
  121.6 2.4 collective-permute-start.4
  125.8 3.0 multiply_reduce_fusion.3
  129.4 5.1 group_sum.2
  146.3 2.4 fusion.37
  148.6 11.3 %collective-permute-done.refs_2_ = bf16[320,2048]{1,0:T(8,128)(2,1)} collective-permute-done((bf16[320,2048]{1,0:T(8,128)(2,1)}, bf16[320,2048]{1,0:T(8,128)(2,1)}, u32[]{:S(2)}, u32[]{:S(2)}) %collective-permute-start) | collective-permute-done | bytes 1310752 | tf_op jit(solution)/shard_map/ppermute | solution.py:1545
  165.8 45.4 %attend_send.1 = (bf16[1280,512]{1,0:T(8,128)(2,1)}, bf16[1280,512]{1,0:T(8,128)(2,1)}, bf16[1280,512]{1,0:T(8,128)(2,1)}, f32[4,1280,1]{2,1,0:T(8,128)}, bf16[320,2048]{1,0:T(8,128)(2,1)}) custom-call(f32[1280,1536]{1,0:T(8,128)} %bitcast.109, f32[1280,1536]{1,0:T(8,128)} %bitcast.110, f32[1280,1536]{1,0:T(8,128)} %bitcast.111, f32[1280,1]{1,0:T(8,128)} %bitcast.130, ...), custom_call_target="tpu_custom_call" | custom-call | tf_op jit(solution)/shard_map/attend_send/pallas_call | solution.py:824
  215.5 1.9 fusion.21
  217.5 5.7 fusion.65
  224.3 2.1 fusion.22
  229.8 206.6 %experts.1 = (bf16[8,320,2048]{2,1,0:T(8,128)(2,1)}, bf16[8,320,2176]{2,1,0:T(8,128)(2,1)}, bf16[4,1152,256]{2,1,0:T(8,128)(2,1)}, bf16[8,320,2176]{2,1,0:T(8,12...) custom-call(bf16[320,2176]{1,0:T(8,128)(2,1)} %pad_maximum_fusion.2.refs_0_, ...), custom_call_target="tpu_custom_call" | custom-call | flops 111669149696 | bytes 100000000 | tf_op jit(solution)/shard_map/experts/pallas_call | solution.py:1486
  436.4 1.5 convert_element_type.145
  440.1 2.0 multiply_reduce_fusion
  442.1 2.1 subtract_add_fusion
  451.6 6.2 fusion.59
  457.8 2.6 fusion.9.a_ref
  460.4 34.0 %to_heads.1 = bf16[4,320,512]{2,1,0:T(8,128)(2,1)} custom-call(bf16[320,2048]{1,0:T(8,128)(2,1)} %fusion.9.a_ref), custom_call_target="tpu_custom_call" | custom-call | tf_op jit(solution)/shard_map/to_heads/pallas_call | solution.py:475
  494.5 4.5 all-to-all-start
  499.0 25.0 %attend_back.1 = (f32[1280,512]{1,0:T(8,128)}, f32[1280,512]{1,0:T(8,128)}, bf16[1280,512]{1,0:T(8,128)(2,1)}, f32[4,1280,1]{2,1,0:T(8,128)}, f32[4,1280,1]{2,1,0:T(8,128)}) custom-call(bf16[1280,512]{1,0:T(8,128)(2,1)} %get-tuple-element.47.q_ref, bf16[1280,512]{1,0:T(8,128)(2,1)} %get-tuple-element.48.k_ref, bf16[1280,512]{1,0:T(8,128)(2,1)} %get-tuple-element.49.v_ref, ...), custom_call_target="tpu_custom_call" | custom-call | tf_op jit(solution)/shard_map/attend_back/pallas_call | solution.py:922
  524.0 2.1 reduce_sum.173
  526.2 2.1 reduce_sum.174
  529.0 8.7 %group_sum.3 = f32[20,128]{1,0:T(8,128)} custom-call(f32[20,128]{1,0:T(8,128)} %reshape.267.x_ref), custom_call_target="tpu_custom_call" | custom-call | tf_op jit(solution)/shard_map/group_sum/pallas_call | solution.py:703
  540.0 4.1 subtract_convert_fusion.1
  544.2 2.2 pad_maximum_fusion.dp
  546.5 11.5 %late_gradients.1 = (bf16[1280,384]{1,0:T(8,128)(2,1)S(1)}, bf16[8,1152,128]{2,1,0:T(8,128)(2,1)}) custom-call(bf16[1280,1536]{1,0:T(8,128)(2,1)} %pad_maximum_fusion.dp, bf16[384,512]{1,0:T(8,128)(2,1)S(1)} %slice.224.up, f32[1280,128]{1,0:T(8,128)S(1)} %compare_convert_fusion.mask, bf16[1280,384]{1,0:T(8,128)(2,1)S(1)} %bitcast.107, ...), custom_call_target="tpu_custom_call" | custom-call | flops 4000000000 | bytes 20000000 | tf_op jit(solution)/shard_map/late_gradients/pallas_call | solution.py:1529
  558.0 15.9 %convolution_convert_fusion = bf16[1280,2048]{1,0:T(8,128)(2,1)} fusion(bf16[2048,1920]{1,0:T(8,128)(2,1)} %get-tuple-element.62, bf16[1280,384]{1,0:T(8,128)(2,1)S(1)} %get-tuple-element.61, bf16[1280,512]{1,0:T(8,128)(2,1)} %get-tuple-element.57, bf16[1280,512]{1,0:T(8,128)(2,1)} %copy-done.14, bf16[1280,512]{1,0:T(8,128)(2,1)S(1)} %get-tuple-element.75), kind=kOutput, calls=%fused_computation | convolution fusion | flops 10088611840 | bytes 18022400 | tf_op jit(solution)/shard_map/dot_general | solution.py:39
  574.9 81.5 %finish.1 = (f32[320,2048]{1,0:T(8,128)}, f32[592,128]{1,0:T(8,128)S(1)}) custom-call(bf16[4,320,2048]{2,1,0:T(8,128)(2,1)} %bitcast.128, bf16[8,1152,128]{2,1,0:T(8,128)(2,1)S(1)} %copy-done, bf16[832,128]{1,0:T(8,128)(2,1)S(1)} %copy-done.1), custom_call_target="tpu_custom_call" | custom-call | tf_op jit(solution)/shard_map/finish/pallas_call | solution.py:658
  656.4 2.3 fusion.16
  660.9 4.5 fusion.14
  665.5 2.2 convert_reduce_fusion
  671.4 2.8 fusion.19
  (254 shorter events, 59.5 us)
Async XLA Ops:
  7.2 5.8 copy-start.46
  7.2 9.5 %copy-start.23 = (bf16[256,512]{1,0:T(8,128)(2,1)S(1)}, bf16[256,512]{1,0:T(8,128)(2,1)}, u32[]{:S(2)}) copy-start(bf16[256,512]{1,0:T(8,128)(2,1)} %param.36) | copy-start | bytes 786436
  7.2 7.0 %copy-start.44 = (s32[1,3]{1,0:T(1,128)S(1)}, s32[1,3]{1,0:T(1,128)}, u32[]{:S(2)}) copy-start(s32[1,3]{1,0:T(1,128)} %param.25) | copy-start | bytes 40
  7.2 7.0 %copy-start.40 = (s32[1,3]{1,0:T(1,128)S(1)}, s32[1,3]{1,0:T(1,128)}, u32[]{:S(2)}) copy-start(s32[1,3]{1,0:T(1,128)} %param.24) | copy-start | bytes 40
  7.2 14.4 %copy-start.10 = (bf16[1,320,2048]{2,1,0:T(8,128)(2,1)S(1)}, bf16[1,320,2048]{2,1,0:T(8,128)(2,1)}, u32[]{:S(2)}) copy-start(bf16[1,320,2048]{2,1,0:T(8,128)(2,1)} %param.22) | copy-start | bytes 3932164
  7.2 205.8 %all-gather.6.cloned.1.call-start = ((), (), s32[]{:S(2)}) async-start(), calls=%async_computation.4 | async-start | bytes 4128768 | tf_op jit(solution)/shard_map/all_gather | solution.py:1630
  9.5 13.5 %copy-start.27 = (f32[2048]{0:T(1024)S(1)}, f32[2048]{0:T(1024)}, u32[]{:S(2)}) copy-start(f32[2048]{0:T(1024)} %param.27) | copy-start | bytes 24580
  12.9 204.6 %all-gather.4.cloned.1.call-start = ((), (), s32[]{:S(2)}) async-start(), calls=%async_computation.3 | async-start | bytes 9437184 | tf_op jit(solution)/shard_map/all_gather | solution.py:1649
  21.5 98.6 %copy-start.29 = (s32[1280]{0:T(1024)}, s32[1280]{0:T(1024)S(1)}, u32[]{:S(2)}) copy-start(s32[1280]{0:T(1024)S(1)} %get-tuple-element.74) | copy-start | bytes 15364
  21.6 202.7 %copy-start.42 = (s32[128]{0:T(128)}, s32[128]{0:T(128)S(1)}, u32[]{:S(2)}) copy-start(s32[128]{0:T(128)S(1)} %and_select_fusion) | copy-start | bytes 1540
  21.9 98.1 %copy-start.36 = (f32[320]{0:T(512)}, f32[320]{0:T(512)S(1)}, u32[]{:S(2)}) copy-start(f32[320]{0:T(512)S(1)} %add_rsqrt_fusion.2) | copy-start | bytes 3844
  120.1 453.9 %reduce-scatter.5.cloned.1.call-start = ((), (), s32[]{:S(2)}) async-start(), calls=%async_computation.6 | async-start | bytes 1916928 | tf_op jit(solution)/shard_map/reduce_scatter | solution.py:1788
  120.5 39.4 %collective-permute-start = (bf16[320,2048]{1,0:T(8,128)(2,1)}, bf16[320,2048]{1,0:T(8,128)(2,1)}, u32[]{:S(2)}, u32[]{:S(2)}) collective-permute-start(bf16[320,2048]{1,0:T(8,128)(2,1)} %bitcast.11.refs_1_), channel_id=1, source_target_pairs={{0,2},{2,0},{4,6},{6,4},{1,3},{3,1},{5,7},{7,5},{8,10},{10,8},{12,... | collective-permute-start | bytes 3932168 | tf_op jit(solution)/shard_map/ppermute | solution.py:1545
  121.4 40.0 %collective-permute-start.1 = (bf16[320,2048]{1,0:T(8,128)(2,1)}, bf16[320,2048]{1,0:T(8,128)(2,1)}, u32[]{:S(2)}, u32[]{:S(2)}) collective-permute-start(bf16[320,2048]{1,0:T(8,128)(2,1)} %bitcast.11.refs_1_), channel_id=1, source_target_pairs={{0,4},{4,0},{2,6},{6,2},{1,5},{5,1},{3,7},{7,3},{8,12},{12,8},{10,... | collective-permute-start | bytes 3932168 | tf_op jit(solution)/shard_map/ppermute | solution.py:1546
  121.6 108.2 %collective-permute-start.4 = (bf16[320,2048]{1,0:T(8,128)(2,1)}, bf16[320,2048]{1,0:T(8,128)(2,1)}, u32[]{:S(2)}, u32[]{:S(2)}) collective-permute-start(bf16[320,2048]{1,0:T(8,128)(2,1)} %bitcast.11.refs_1_), channel_id=1, source_target_pairs={{0,1},{1,0},{2,3},{3,2},{4,5},{5,4},{6,7},{7,6},{8,9},{9,8},{10,11... | collective-permute-start | bytes 3932168 | tf_op jit(solution)/shard_map/ppermute | solution.py:1547
  125.8 15.5 %copy-start.41 = (s32[1,320,8]{1,2,0:T(8,128)S(1)}, s32[1,320,8]{1,2,0:T(8,128)}, u32[]{:S(2)}) copy-start(s32[1,320,8]{1,2,0:T(8,128)} %param.26) | copy-start | bytes 30724
  161.1 51.4 %collective-permute-start.2 = (bf16[160,2048]{1,0:T(8,128)(2,1)S(1)}, bf16[160,2048]{1,0:T(8,128)(2,1)}, u32[]{:S(2)}, u32[]{:S(2)}) collective-permute-start(bf16[160,2048]{1,0:T(8,128)(2,1)S(1)} %slice.260), channel_id=1, source_target_pairs={{0,4},{4,0},{2,6},{6,2},{1,5},{5,1},{3,7},{7,3},{8,12},{12,8},{10,... | collective-permute-start | bytes 1966088 | tf_op jit(solution)/shard_map/ppermute | solution.py:1546
  162.7 49.8 %collective-permute-start.3 = (bf16[160,2048]{1,0:T(8,128)(2,1)S(1)}, bf16[160,2048]{1,0:T(8,128)(2,1)}, u32[]{:S(2)}, u32[]{:S(2)}) collective-permute-start(bf16[160,2048]{1,0:T(8,128)(2,1)S(1)} %slice.261), channel_id=1, source_target_pairs={{0,2},{2,0},{4,6},{6,4},{1,3},{3,1},{5,7},{7,5},{8,10},{10,8},{12,... | collective-permute-start | bytes 1966088 | tf_op jit(solution)/shard_map/ppermute | solution.py:1545
  212.0 17.8 %collective-permute-start.5 = (bf16[320,2048]{1,0:T(8,128)(2,1)}, bf16[320,2048]{1,0:T(8,128)(2,1)}, u32[]{:S(2)}, u32[]{:S(2)}) collective-permute-start(bf16[320,2048]{1,0:T(8,128)(2,1)} %collective-permute-done.refs_2_), channel_id=1, source_target_pairs={{0,1},{1,0},{2,3},{3,2},{4,5},{5,4},{6,7},{7,6},{8,9},{9,8},{10,11... | collective-permute-start | bytes 3932168 | tf_op jit(solution)/shard_map/ppermute | solution.py:1547
  212.0 17.8 %collective-permute-start.6 = (bf16[320,2048]{1,0:T(8,128)(2,1)}, bf16[320,2048]{1,0:T(8,128)(2,1)}, u32[]{:S(2)}, u32[]{:S(2)}) collective-permute-start(bf16[320,2048]{1,0:T(8,128)(2,1)} %collective-permute-done.1.refs_3_), channel_id=1, source_target_pairs={{0,1},{1,0},{2,3},{3,2},{4,5},{5,4},{6,7},{7,6},{8,9},{9,8},{10,11... | collective-permute-start | bytes 3932168 | tf_op jit(solution)/shard_map/ppermute | solution.py:1547
  212.5 17.3 %collective-permute-start.7 = (bf16[160,2048]{1,0:T(8,128)(2,1)}, bf16[160,2048]{1,0:T(8,128)(2,1)}, u32[]{:S(2)}, u32[]{:S(2)}) collective-permute-start(bf16[160,2048]{1,0:T(8,128)(2,1)} %collective-permute-done.2.refs_4_), channel_id=1, source_target_pairs={{0,1},{1,0},{2,3},{3,2},{4,5},{5,4},{6,7},{7,6},{8,9},{9,8},{10,11... | collective-permute-start | bytes 1966088 | tf_op jit(solution)/shard_map/ppermute | solution.py:1547
  212.5 17.3 %collective-permute-start.8 = (bf16[160,2048]{1,0:T(8,128)(2,1)}, bf16[160,2048]{1,0:T(8,128)(2,1)}, u32[]{:S(2)}, u32[]{:S(2)}) collective-permute-start(bf16[160,2048]{1,0:T(8,128)(2,1)} %collective-permute-done.3.refs_5_), channel_id=1, source_target_pairs={{0,1},{1,0},{2,3},{3,2},{4,5},{5,4},{6,7},{7,6},{8,9},{9,8},{10,11... | collective-permute-start | bytes 1966088 | tf_op jit(solution)/shard_map/ppermute | solution.py:1547
  450.2 221.0 %reduce-scatter.3.cloned.1.call-start = ((), (), s32[]{:S(2)}) async-start(), calls=%async_computation.5 | async-start | bytes 11796480 | tf_op jit(solution)/shard_map/reduce_scatter | solution.py:1747
  494.5 171.0 %all-to-all-start = ((bf16[4,1152,256]{2,1,0:T(8,128)(2,1)}), bf16[4,1152,256]{2,1,0:T(8,128)(2,1)}, u32[]{:S(2)}, u32[]{:S(2)}) async-start(bf16[4,1152,256]{2,1,0:T(8,128)(2,1)} %get-tuple-element.69), calls=%async_computation.2 | async-start | bytes 4718592 | tf_op jit(solution)/shard_map/all_to_all | solution.py:1771
  524.0 14.6 %copy-start.16 = (bf16[4,1152,256]{2,1,0:T(8,128)(2,1)S(1)}, bf16[4,1152,256]{2,1,0:T(8,128)(2,1)}, u32[]{:S(2)}) copy-start(bf16[4,1152,256]{2,1,0:T(8,128)(2,1)} %get-tuple-element.68) | copy-start | bytes 7077892
  526.2 13.8 %copy-start.31 = (f32[512]{0:T(512)S(1)}, f32[512]{0:T(512)}, u32[]{:S(2)}) copy-start(f32[512]{0:T(512)} %dynamic_slice.11) | copy-start | bytes 6148
  526.2 13.8 %copy-start.32 = (f32[512]{0:T(512)S(1)}, f32[512]{0:T(512)}, u32[]{:S(2)}) copy-start(f32[512]{0:T(512)} %dynamic_slice.12) | copy-start | bytes 6148
  526.2 13.8 %copy-start.33 = (f32[1280]{0:T(1024)S(1)}, f32[1280]{0:T(1024)}, u32[]{:S(2)}) copy-start(f32[1280]{0:T(1024)} %get-tuple-element.86) | copy-start | bytes 15364
  526.2 13.8 %copy-start.34 = (f32[1280]{0:T(1024)S(1)}, f32[1280]{0:T(1024)}, u32[]{:S(2)}) copy-start(f32[1280]{0:T(1024)} %get-tuple-element.87) | copy-start | bytes 15364
  558.0 15.9 %copy-start = (bf16[8,1152,128]{2,1,0:T(8,128)(2,1)S(1)}, bf16[8,1152,128]{2,1,0:T(8,128)(2,1)}, u32[]{:S(2)}) copy-start(bf16[8,1152,128]{2,1,0:T(8,128)(2,1)} %get-tuple-element.63.late) | copy-start | bytes 7077892
  574.9 81.5 %copy-start.11 = (bf16[1,320,2048]{2,1,0:T(8,128)(2,1)S(1)}, bf16[1,320,2048]{2,1,0:T(8,128)(2,1)}, u32[]{:S(2)}) copy-start(bf16[1,320,2048]{2,1,0:T(8,128)(2,1)} %param.22) | copy-start | bytes 3932164
  574.9 81.5 %copy-start.28 = (f32[2048]{0:T(1024)S(1)}, f32[2048]{0:T(1024)}, u32[]{:S(2)}) copy-start(f32[2048]{0:T(1024)} %param.27) | copy-start | bytes 24580
  (29 other events, 69.9 us)
Sparse Core Ops, SparseCore 0:
  13.0 46.7 all-gather.5
  120.2 82.0 all-gather.3
  450.4 38.5 reduce-scatter.4
  492.7 81.5 reduce-scatter.2

commit v5 on v4

--- a/solution.py
+++ b/solution.py
@@ -548,43 +548,125 @@
     )(parts)
 
 
-def finish_kernel(n_c, p_ref, late, early, o_ref, flat, sib, chip, rx, got_l, stage, got_z, ss, sr, send, recv, ls, lr, zs, zr):
+def finish_kernel(
+    n_c,
+    both,
+    weight,
+    late,
+    early,
+    middle,
+    mixed,
+    tokens,
+    grad_middle,
+    gain,
+    output,
+    grad_tokens,
+    grad_down,
+    grad_up,
+    grad_rdown,
+    grad_rup,
+    give,
+    keep,
+    sib,
+    fwd,
+    rx,
+    got_l,
+    got_e,
+    stage,
+    got_z,
+    ss,
+    sr,
+    gs,
+    gr,
+    send,
+    recv,
+    ls,
+    lr,
+    es,
+    er,
+    zs,
+    zr,
+):
     zh, zl, c, core = here()
     plane = [(zh, zl, lax.rem(c + i, n_c), core ^ k) for i in range(n_c) for k in range(2)]
     signal_all(column_peers(zh, zl, c, core) + plane[2:])
-    width = o_ref.shape[1]
+    tok, width = output.shape
     half = width // 2
     sibling = (zh, zl, c, 1 - core)
     mine = pl.ds(pl.multiple_of(core * half, half), half)
     theirs = pl.ds(pl.multiple_of((1 - core) * half, half), half)
-    for s in range(4):
-        remote(p_ref.at[s, :, theirs], sib.at[s], ss.at[s], sr.at[s], sibling).start()
     me = c * 2 + core
-    def is_self(s):
-        return (s // 2 == zh) & (s % 2 == zl) & (core == zh)
-
-    for s in range(4):
-        pltpu.make_async_copy(sib.at[s], sib.at[s], sr.at[s]).wait()
-        chip[s] = (p_ref[s, :, mine].astype(F32) + sib[s].astype(F32)).astype(BF)
-        src, dst = chip.at[s], rx.at[zl, core]
-
-        @pl.when(is_self(s))
-        def _():
-            pltpu.make_async_copy(src, dst, recv.at[zl, core]).start()
-
-        @pl.when(jnp.logical_not(is_self(s)))
-        def _():
-            remote(src, dst, send.at[s], recv.at[zl, core], (s // 2, s % 2, c, zh)).start()
-
     count = len(plane)
     for n in range(1, count):
         peer = plane[n]
-        remote(late.at[peer[2] * 2 + peer[3]], got_l.at[n], ls.at[n], lr.at[n], peer).start()
-    late_sum = late[me].astype(F32)
-    for n in range(1, count):
-        wait_for(got_l.at[n], lr.at[n])
-        late_sum = late_sum + got_l[n].astype(F32)
-    late_sum = late_sum.astype(BF)
+        f = peer[2] * 2 + peer[3]
+        remote(early.at[f], got_e.at[n], es.at[n], er.at[n], peer).start()
+        remote(late.at[f], got_l.at[n], ls.at[n], lr.at[n], peer).start()
+    at_end = zl == zh
+    inner = zl != zh
+    shard = lambda p: p + zh * (3 - 2 * p)
+    owner = lambda p: (shard(p) // 2, lax.rem(shard(p), 2), c, zh)
+    local = core == zh
+
+    def deliver(n, p, slot):
+        remote(give.at[n], rx.at[slot, core], send.at[n], recv.at[slot, core], owner(p)).start()
+
+    def stay(n, slot):
+        pltpu.make_async_copy(give.at[n], rx.at[slot, core], recv.at[slot, core]).start()
+
+    def settle(n, p):
+        pltpu.make_async_copy(sib.at[n], sib.at[n], sr.at[n]).wait()
+        wait_for(give.at[n], ss.at[n])
+        give[n] = (keep[n] + sib[n].astype(F32)).astype(BF)
+        if p >= 2:
+
+            @pl.when(at_end)
+            def _():
+                remote(give.at[n], fwd.at[n], gs.at[n], gr.at[n], (zh, 1 - zl, c, core)).start()
+
+        else:
+            home = at_end if p == 0 else inner
+
+            @pl.when(home & local)
+            def _():
+                stay(n, p)
+
+            @pl.when(home & jnp.logical_not(local))
+            def _():
+                deliver(n, p, p)
+
+            @pl.when(jnp.logical_not(home))
+            def _():
+                deliver(n, p, 1 - p)
+
+    order = (3, 2, 1, 0)
+    for n, p in enumerate(order):
+        rows = pl.ds(pl.multiple_of(shard(p) * tok, tok), tok)
+        give[n] = mm_t(both[rows], weight[theirs]).astype(BF)
+        remote(give.at[n], sib.at[n], ss.at[n], sr.at[n], sibling).start()
+        keep[n] = mm_t(both[rows], weight[mine])
+        if n:
+            settle(n - 1, order[n - 1])
+    settle(3, 0)
+
+    @pl.when(inner)
+    def _():
+        for n in range(2):
+            wait_for(fwd.at[n], gr.at[n])
+            give[n] = (give[n].astype(F32) + fwd[n].astype(F32)).astype(BF)
+            deliver(n, order[n], 1)
+
+    output[...] = (middle[...] + mixed[...].astype(F32)).astype(BF)
+
+    def total(own, got, arrived):
+        value = own[me].astype(F32)
+        for n in range(1, count):
+            wait_for(got.at[n], arrived.at[n])
+            value = value + got[n].astype(F32)
+        return value.astype(BF)
+
+    early_sum = total(early, got_e, er)
+    late_sum = total(late, got_l, lr)
     down, up, wide, rest = finish_rows(n_c)
     for q in range(4):
         stage[q, :down] = late_sum[q * down : (q + 1) * down]
@@ -593,9 +675,9 @@
             stage[q, down : down + up] = late_sum[at : at + up]
             stage[q, down + up : down + wide] = jnp.zeros((wide - up, SPAN), BF)
         else:
-            stage[q, down : down + wide] = early[:wide]
+            stage[q, down : down + wide] = early_sum[:wide]
         at = wide + q * rest
-        stage[q, down + wide :] = early[at : at + rest]
+        stage[q, down + wide :] = early_sum[at : at + rest]
     seq = zh * 2 + zl
     for q in range(4):
 
@@ -607,10 +689,25 @@
         def _():
             remote(stage.at[q], got_z.at[seq], zs.at[q], zr.at[seq], (q // 2, q % 2, c, core)).start()
 
+    paired = zh == core
+
+    @pl.when(paired)
+    def _():
+        for k in range(2):
+            wait_for(rx.at[0, k], recv.at[0, k])
+
+    @pl.when(jnp.logical_not(paired))
+    def _():
+        rx[0] = jnp.zeros_like(rx[0])
+
     for k in range(2):
-        for b in range(2):
-            pltpu.make_async_copy(rx.at[b, k], rx.at[b, k], recv.at[b, k]).wait()
-        o_ref[:, k * half : (k + 1) * half] = rx[0, k].astype(F32) + rx[1, k].astype(F32)
+        wait_for(rx.at[1, k], recv.at[1, k])
+    for n in range(tok // 32):
+        rows = slice(n * 32, (n + 1) * 32)
+        grad = jnp.concatenate(
+            [rx[0, k, rows].astype(F32) + rx[1, k, rows].astype(F32) for k in range(2)], axis=1
+        )
+        grad_tokens[rows] = grad_middle[rows] + rms_back(tokens[rows].astype(F32), gain[...], grad)
 
     for q in range(4):
 
@@ -618,28 +715,51 @@
         def _():
             wait_for(got_z.at[q], zr.at[q])
 
-    terms = [got_z[q].astype(F32) for q in range(4)]
-    flat[...] = (terms[0] + terms[1]) + (terms[2] + terms[3])
-
-    @pl.when(seq < 3)
-    def _():
-        for b in range(2):
-            pair = got_z[b, down : down + up].astype(F32) + got_z[2 + b, down : down + up].astype(F32)
-            flat[down + b * up : down + (b + 1) * up] = pair
+    def along_z(rows):
+        return (got_z[0, rows].astype(F32) + got_z[1, rows].astype(F32)) + (
+            got_z[2, rows].astype(F32) + got_z[3, rows].astype(F32)
+        )
+
+    r, u = down // 3, up // 8
+    for j in range(4):
+        start = j * r if j < 3 else down + wide
+        grad_down[:, j * SPAN : (j + 1) * SPAN] = along_z(slice(start, start + r))
+    grad_rdown[...] = along_z(slice(down + wide + r, down + wide + 2 * r))
+    grad_rup[...] = along_z(slice(down + wide + 2 * r, down + wide + rest))
+    for n in range(16):
+        b, m = n // 8, n % 8
+        part = slice(down + m * u, down + (m + 1) * u)
+        halves = got_z[b, part].astype(F32) + got_z[2 + b, part].astype(F32)
+        whole = along_z(slice(down + n * u, down + (n + 1) * u))
+        grad_up[:, n * SPAN : (n + 1) * SPAN] = jnp.where(seq < 3, halves, whole)
 
     for s in range(4):
-        pltpu.make_async_copy(sib.at[s], sib.at[s], ss.at[s]).wait()
-
-        @pl.when(jnp.logical_not(is_self(s)))
-        def _():
-            pltpu.make_async_copy(chip.at[s], chip.at[s], send.at[s]).wait()
 
         @pl.when(seq != s)
         def _():
             wait_for(stage.at[s], zs.at[s])
+
+    for n, p in enumerate(order):
+        if p >= 2:
+
+            @pl.when(at_end)
+            def _():
+                wait_for(give.at[n], gs.at[n])
+
+            @pl.when(inner)
+            def _():
+                wait_for(give.at[n], send.at[n])
+
+        else:
+            home = at_end if p == 0 else inner
+
+            @pl.when(jnp.logical_not(home & local))
+            def _():
+                wait_for(give.at[n], send.at[n])
 
     for n in range(1, count):
         wait_for(got_l.at[n], ls.at[n])
+        wait_for(got_e.at[n], es.at[n])
 
 
 def finish_rows(n_c):
@@ -648,8 +768,8 @@
     return 3 * down, 8 * up, 16 * up, 2 * down + 16
 
 
-def finish(parts, late, early, n_c):
-    _, tok, width = parts.shape
+def finish(both, weight, late, early, middle, mixed, tokens, grad_middle, gain, n_c):
+    tok, width = middle.shape
     half = width // 2
     down, up, wide, rest = finish_rows(n_c)
     n_f = 2 * n_c
@@ -658,32 +778,43 @@
     return pl.pallas_call(
         functools.partial(finish_kernel, n_c),
         out_shape=(
+            jax.ShapeDtypeStruct((tok, width), BF),
             jax.ShapeDtypeStruct((tok, width), F32),
-            jax.ShapeDtypeStruct((down + wide + rest, SPAN), F32),
+            jax.ShapeDtypeStruct((down // 3, 4 * SPAN), F32),
+            jax.ShapeDtypeStruct((up // 8, 16 * SPAN), F32),
+            jax.ShapeDtypeStruct((down // 3, SPAN), F32),
+            jax.ShapeDtypeStruct((16, SPAN), F32),
         ),
-        in_specs=[vmem] * 3,
-        out_specs=[vmem] * 2,
+        in_specs=[vmem] * 9,
+        out_specs=[vmem] * 6,
         scratch_shapes=[
             VMEM((4, tok, half), BF),
+            VMEM((4, tok, half), F32),
             VMEM((4, tok, half), BF),
+            VMEM((2, tok, half), BF),
             VMEM((2, 2, tok, half), BF),
             VMEM(late.shape, BF),
+            VMEM(early.shape, BF),
             VMEM((4, down + wide + rest, SPAN), BF),
             VMEM((4, down + wide + rest, SPAN), BF),
             dma((4,)),
             dma((4,)),
+            dma((2,)),
+            dma((2,)),
             dma((4,)),
             dma((2, 2)),
+            dma((n_f,)),
+            dma((n_f,)),
             dma((n_f,)),
             dma((n_f,)),
             dma((4,)),
             dma((4,)),
         ],
         compiler_params=pltpu.CompilerParams(
-            collective_id=7, has_side_effects=True, vmem_limit_bytes=50 * 2**20
+            collective_id=7, has_side_effects=True, vmem_limit_bytes=60 * 2**20
         ),
         name="finish",
-    )(parts, late, early)
+    )(both, weight, late, early, middle, mixed, tokens, grad_middle, gain)
 
 
 def group_sum_kernel(x_ref, o_ref, rx, send, recv):
@@ -882,6 +1013,12 @@
     dk_acc[...] = jnp.zeros_like(dk_acc)
     dv_acc[...] = jnp.zeros_like(dv_acc)
 
+    @pl.when(pl.program_id(0) == 0)
+    def _():
+        mq_ref[...] = jnp.zeros_like(mq_ref)
+        mk_ref[...] = jnp.zeros_like(mk_ref)
+
+
     def back(grad, raw, gain):
         turned = turn(grad.astype(BF).astype(F32), cosine_of, -sine_of)
         return turned, jnp.sum(raw * gain[...] * turned, axis=1, keepdims=True)
@@ -901,13 +1038,13 @@
         cosine_of, sine_of = cosine[own], sine[own]
         turned, moment = back(grad_q, pq[own], gq)
         uq_ref[own] = turned
-        mq_ref[0, own] = moment
+        mq_ref[own] += moment
         dk_acc[:length] += t_mm(grad_scores, q_ref[own])
         dv_acc[:length] += t_mm(probs.astype(BF), g_ref[own])
     cosine_of, sine_of = cosine[...], sine[...]
     turned, moment = back(dk_acc[...] * scale, pk[...], gk)
     uk_ref[...] = turned
-    mk_ref[0] = moment
+    mk_ref[...] += moment
     dv_ref[...] = dv_acc[...].astype(BF)
 
 
@@ -918,7 +1055,7 @@
     fixed = lambda shape: pl.BlockSpec(shape, lambda h: (0, 0))
     column = pl.BlockSpec((1, block, 1), lambda h: (h, 0, 0))
     wide = lambda t: jax.ShapeDtypeStruct((block, GROUP_WIDTH), t)
-    moment = jax.ShapeDtypeStruct((HEADS, block, 1), F32)
+    moment = jax.ShapeDtypeStruct((block, 1), F32)
     return pl.pallas_call(
         attend_back_kernel,
         grid=(HEADS,),
@@ -938,7 +1075,7 @@
             fixed((block, 1)),
             fixed((1, block)),
         ],
-        out_specs=[head(0)] * 3 + [column] * 2,
+        out_specs=[head(0)] * 3 + [fixed((block, 1))] * 2,
         scratch_shapes=[VMEM((block, HD), F32), VMEM((block, HD), F32)],
         compiler_params=pltpu.CompilerParams(vmem_limit_bytes=60 * 2**20),
         name="attend_back",
@@ -1498,7 +1635,7 @@
     return results[0], results[1], results[2]
 
 
-def late_kernel(n_f, dp, up, mask, low, x, dlow, packed):
+def late_kernel(n_f, dp, up, mask, low, x, both, packed):
     core = lax.axis_index("core")
     down_rows = MODEL_WIDTH // (4 * n_f)
     up_rows = SPAN // n_f
@@ -1508,7 +1645,8 @@
         own = slice(j * SPAN, (j + 1) * SPAN)
         wide = slice(j * GROUP_WIDTH, (j + 1) * GROUP_WIDTH)
         lowered = (mm_t(dp[:, wide], up[own]) * mask[...]).astype(BF)
-        dlow[:, own] = lowered
+        both[:, wide] = dp[:, wide]
+        both[:, 3 * GROUP_WIDTH + j * SPAN : 3 * GROUP_WIDTH + (j + 1) * SPAN] = lowered
         grad_up = t_mm(low[:, own], dp[:, wide]).astype(BF)
         grad_down = t_mm(x[...], lowered).astype(BF)
         for f in range(n_f):
@@ -1529,7 +1667,7 @@
     return pl.pallas_call(
         functools.partial(late_kernel, n_f),
         out_shape=(
-            jax.ShapeDtypeStruct((block, 3 * SPAN), BF),
+            jax.ShapeDtypeStruct((block, PROJECT_WIDTH), BF),
             jax.ShapeDtypeStruct((n_f, rows, SPAN), BF),
         ),
         in_specs=[pl.BlockSpec(memory_space=VMEM)] * 5,
@@ -1785,12 +1923,11 @@
         early = jnp.concatenate(
             [up_blocks.reshape(n_fsdp, -1, SPAN), rest.reshape(n_fsdp, -1, SPAN)], axis=1
         )
-        early = lax.psum_scatter(early.reshape(-1, SPAN), FSDP, scatter_dimension=0, tiled=True)
 
     uq, uk, grad_v, mq, mk = attend_back(
         q, k, v, head_grad, lse, projected, *gains, cosine, sine, seg_c, seg_r
     )
-    moments = over_group(jnp.sum(mq[..., 0], axis=0), jnp.sum(mk[..., 0], axis=0), 5) / MODEL_WIDTH
+    moments = over_group(mq[:, 0], mk[:, 0], 5) / MODEL_WIDTH
 
     def rms_inner(values, scale, gain, turned, moment):
         return (scale * gain * turned - values * (scale * scale * scale) * moment).astype(BF)
@@ -1804,41 +1941,35 @@
         axis=1,
     )
     if n_c == 4:
-        grad_lowered, late = late_gradients(
+        both, late = late_gradients(
             grad_projected, up_own, mask1, lowered, x_all, n_fsdp
         )
     else:
         grad_lowered = (mm_t(grad_projected, up_diagonal) * mask3).astype(BF)
     if n_c == 4:
-        both = jnp.concatenate([grad_projected, grad_lowered], axis=1)
-        grad_normed_part = mm_t(both, head_rows).astype(BF)
+        output, grad_inputs, *summed = finish(
+            both,
+            head_rows,
+            late,
+            early,
+            middle,
+            mixed,
+            tokens[0],
+            grad_middle,
+            gain_attn[None, :],
+            n_c,
+        )
     else:
         grad_normed_part = (
             mm_t(grad_projected, qkv_rows) + mm_t(grad_lowered, down3)
         ).astype(BF)
-    grad_normed_part = grad_normed_part.reshape(4, tok, MODEL_WIDTH)
-    if n_c == 4:
-        grad_normed, flat = finish(grad_normed_part, late, early, n_c)
-    else:
-        grad_normed = sum_to_tokens(grad_normed_part)
-    grad_inputs = grad_middle + rms_back(inputs, gain_attn, grad_normed)
-
-    down_rows, up_rows = MODEL_WIDTH // (n_seq * n_fsdp), SPAN // n_fsdp
+        grad_normed = sum_to_tokens(grad_normed_part.reshape(4, tok, MODEL_WIDTH))
+        grad_inputs = grad_middle + rms_back(inputs, gain_attn, grad_normed)
+        output = (middle + mixed.astype(F32)).astype(BF)
+
     rup_shape = (SPAN // (n_seq * n_fsdp), experts)
     if n_c == 4:
-        blocks = [flat[j * down_rows : (j + 1) * down_rows] for j in range(3)]
-        at = 3 * down_rows
-        up_blocks = [flat[at + n * up_rows : at + (n + 1) * up_rows] for n in range(16)]
-        at += 16 * up_rows
-        blocks.append(flat[at : at + down_rows])
-        at += down_rows
-        summed = [
-            jnp.concatenate(blocks, axis=1),
-            jnp.concatenate(up_blocks, axis=1),
-            flat[at : at + down_rows],
-        ]
-        at += down_rows
-        summed.append(flat[at, : rup_shape[0] * rup_shape[1]].reshape(rup_shape))
+        summed[3] = summed[3][0, : rup_shape[0] * rup_shape[1]].reshape(rup_shape)
     else:
         grad_up_own = [
             t_mm(
@@ -1872,8 +2003,6 @@
             summed.append(flat[at : at + size].reshape(shape))
             at += size
 
-    mixed, grad_inputs = lax.optimization_barrier((mixed, grad_inputs))
-    output = (middle + mixed.astype(F32)).astype(BF)
     if n_c == 4:
         expert_terms = jnp.stack(
             [jnp.sum(t.astype(F32), axis=0) for t in (first_terms, second_terms)]

time: 686 us -> 655 us (0.955)
  matrix products: 43.5 us -> 26.1 us
  other arithmetic: 50.3 us -> 35.1 us
    dot_general x6 -> x5, matrix products: 28.6 us -> 9.68 us  [mm_t(): lax.dot_general(left, right, (((1,), (1,)), ((), ())), preferred_element_...]
    unnamed x120 -> x106, local copies, waits for them, and re-layouts: 8.54 us -> 14.9 us
  transfers between devices with their start and end apart: 14 -> 13, of which waited for: 1 -> 1; matrix products, arithmetic and copies ran while one was open for 14% -> 12% of each run, Pallas kernels for 45% -> 34%
where the time goes in v5:
time: 655 us; the launch traced here: 649 us
  Pallas kernels  508 us (78%)
  local copies, waits for them, and re-layouts  35.1 us (5%)
  other arithmetic  35.1 us (5%)
  matrix products  26.1 us (4%)
  between operations  19.6 us (3%)
  waiting for transfers between devices  12 us (2%)
  starting transfers between devices  11.5 us (2%)
    pallas_call x1, Pallas kernels, run_experts(): pl.pallas_call(functools.partial(experts_kernel, n_c, experts, slots, com...  207 us
    pallas_call x1, Pallas kernels, gather_project(): pl.pallas_call(project_kernel, out_shape=(jax.ShapeDtypeStruct((4, tok, M...  95.6 us
    pallas_call x1, Pallas kernels, finish(): pl.pallas_call(functools.partial(finish_kernel, n_c), out_shape=(jax.Shap...  77.3 us
    pallas_call x1, Pallas kernels, attend_send(): pl.pallas_call(attend_send_kernel, grid=(HEADS,), out_shape=(wide, wide,...  45.5 us
    pallas_call x1, Pallas kernels, to_heads(): pl.pallas_call(to_heads_kernel, out_shape=jax.ShapeDtypeStruct((4, tok, G...  35.9 us
    pallas_call x1, Pallas kernels, attend_back(): pl.pallas_call(attend_back_kernel, grid=(HEADS,), out_shape=(wide(F32), w...  24.7 us
    unnamed x106, local copies, waits for them, and re-layouts  14.9 us
  transfers between devices with their start and end apart: 13, of which 1 were waited for; matrix products, arithmetic and copies ran while one was open for 12% of the time, Pallas kernels for 34%

profile of v5, /device:TPU:9, one launch (start us, length us, event | category | flops | bytes accessed | tf_op | source)
XLA Modules:
  0.0 649.4 jit_solution(850013191158178341)
XLA Ops:
  14.5 2.1 all-reduce.5
  23.0 1.4 fusion.3.x_ref
  24.5 95.6 %gather_project.1 = (bf16[4,320,2048]{2,1,0:T(8,128)(2,1)}, bf16[2048,1920]{1,0:T(8,128)(2,1)}, bf16[512,512]{1,0:T(8,128)(2,1)}, f32[4,320,1536]{2,1,0:T(8,128)}, bf16[4,320,384]{2,1,0:T(8,128)(2,1)}) custom-call(bf16[320,2048]{1,0:T(8,128)(2,1)} %fusion.3.x_ref, bf16[256,6144]{1,0:T(8,128)(2,1)} %w_ref.1, bf16[256,384]{1,0:T(8,128)(2,1)} %slice.132.down_ref, ...), custom_call_target="tpu_custom_call" | custom-call | tf_op jit(solution)/shard_map/gather_project/pallas_call | solution.py:369
  121.7 2.4 collective-permute-start.4
  125.8 3.0 multiply_reduce_fusion.3
  129.4 5.1 group_sum.2
  145.8 2.4 fusion.23
  148.2 11.9 %collective-permute-done.refs_2_ = bf16[320,2048]{1,0:T(8,128)(2,1)} collective-permute-done((bf16[320,2048]{1,0:T(8,128)(2,1)}, bf16[320,2048]{1,0:T(8,128)(2,1)}, u32[]{:S(2)}, u32[]{:S(2)}) %collective-permute-start) | collective-permute-done | bytes 1310752 | tf_op jit(solution)/shard_map/ppermute | solution.py:1683
  162.8 1.4 collective-permute-start.3
  164.4 1.5 pad_maximum_fusion.4
  165.9 45.5 %attend_send.1 = (bf16[1280,512]{1,0:T(8,128)(2,1)}, bf16[1280,512]{1,0:T(8,128)(2,1)}, bf16[1280,512]{1,0:T(8,128)(2,1)}, f32[4,1280,1]{2,1,0:T(8,128)}, bf16[320,2048]{1,0:T(8,128)(2,1)}) custom-call(f32[1280,1536]{1,0:T(8,128)} %bitcast.102, f32[1280,1536]{1,0:T(8,128)} %bitcast.103, f32[1280,1536]{1,0:T(8,128)} %bitcast.104, f32[1280,1]{1,0:T(8,128)} %bitcast.122, ...), custom_call_target="tpu_custom_call" | custom-call | tf_op jit(solution)/shard_map/attend_send/pallas_call | solution.py:955
  215.8 1.9 fusion.7
  217.7 5.7 fusion.49
  224.6 2.1 fusion.8
  230.1 206.6 %experts.1 = (bf16[8,320,2048]{2,1,0:T(8,128)(2,1)}, bf16[8,320,2176]{2,1,0:T(8,128)(2,1)}, bf16[4,1152,256]{2,1,0:T(8,128)(2,1)}, bf16[8,320,2176]{2,1,0:T(8,12...) custom-call(bf16[320,2176]{1,0:T(8,128)(2,1)} %pad_maximum_fusion.2.refs_0_, ...), custom_call_target="tpu_custom_call" | custom-call | flops 111669149696 | bytes 100000000 | tf_op jit(solution)/shard_map/experts/pallas_call | solution.py:1623
  439.2 1.4 fusion.33
  440.6 2.1 multiply_reduce_fusion
  442.8 2.3 subtract_add_fusion.grad_middle
  445.9 2.9 fusion.44
  448.8 2.8 fusion.a_ref
  451.6 35.9 %to_heads.1 = bf16[4,320,512]{2,1,0:T(8,128)(2,1)} custom-call(bf16[320,2048]{1,0:T(8,128)(2,1)} %fusion.a_ref), custom_call_target="tpu_custom_call" | custom-call | tf_op jit(solution)/shard_map/to_heads/pallas_call | solution.py:475
  487.6 4.6 all-to-all-start
  492.2 2.1 convolution_convert_fusion.1
  496.8 24.7 %attend_back.1 = (f32[1280,512]{1,0:T(8,128)}, f32[1280,512]{1,0:T(8,128)}, bf16[1280,512]{1,0:T(8,128)(2,1)}, f32[1280,1]{1,0:T(8,128)}, f32[1280,1]{1,0:T(8,128)}) custom-call(bf16[1280,512]{1,0:T(8,128)(2,1)} %get-tuple-element.44.q_ref, bf16[1280,512]{1,0:T(8,128)(2,1)} %get-tuple-element.45.k_ref, bf16[1280,512]{1,0:T(8,128)(2,1)} %get-tuple-element.46.v_ref, ...), custom_call_target="tpu_custom_call" | custom-call | tf_op jit(solution)/shard_map/attend_back/pallas_call | solution.py:1059
  524.9 5.8 group_sum.3
  534.8 3.9 subtract_convert_fusion.1
  538.7 2.2 pad_maximum_fusion.dp
  540.9 11.3 %late_gradients.1 = (bf16[1280,1920]{1,0:T(8,128)(2,1)}, bf16[8,1152,128]{2,1,0:T(8,128)(2,1)}) custom-call(bf16[1280,1536]{1,0:T(8,128)(2,1)} %pad_maximum_fusion.dp, bf16[384,512]{1,0:T(8,128)(2,1)S(1)} %slice.161.up, f32[1280,128]{1,0:T(8,128)S(1)} %compare_convert_fusion.mask, bf16[1280,384]{1,0:T(8,128)(2,1)S(1)} %bitcast.100, bf16[1280,2048]{1,0:T(8,128)(2,1)} %bitcast.144), custom_call_target="tpu_custom_call" | custom-call | flops 4000000000 | bytes 20000000 | tf_op jit(solution)/shard_map/late_gradients/pallas_call | solution.py:1667
  552.2 2.2 convert_reduce_fusion
  557.9 77.3 %finish.1 = (bf16[320,2048]{1,0:T(8,128)(2,1)}, f32[320,2048]{1,0:T(8,128)}, f32[64,512]{1,0:T(8,128)}, f32[16,2048]{1,0:T(8,128)}, f32[64,128]{1,0:T(8,128)}, /*index=5*/f32[16,128]{1,0:T(8,128)}) custom-call(bf16[1280,1920]{1,0:T(8,128)(2,1)} %get-tuple-element.62.both, bf16[2048,1920]{1,0:T(8,128)(2,1)} %get-tuple-element.63.weight, ...), custom_call_target="tpu_custom_call" | custom-call | tf_op jit(solution)/shard_map/finish/pallas_call | solution.py:778
  636.7 2.5 copy.145
  639.2 1.5 copy.146
  (230 shorter events, 55.6 us)
Async XLA Ops:
  7.2 5.8 copy-start.42
  7.2 9.5 %copy-start.18 = (bf16[256,512]{1,0:T(8,128)(2,1)S(1)}, bf16[256,512]{1,0:T(8,128)(2,1)}, u32[]{:S(2)}) copy-start(bf16[256,512]{1,0:T(8,128)(2,1)} %param.36) | copy-start | bytes 786436
  7.2 7.0 %copy-start.41 = (s32[1,3]{1,0:T(1,128)S(1)}, s32[1,3]{1,0:T(1,128)}, u32[]{:S(2)}) copy-start(s32[1,3]{1,0:T(1,128)} %param.25) | copy-start | bytes 40
  7.2 7.0 %copy-start.37 = (s32[1,3]{1,0:T(1,128)S(1)}, s32[1,3]{1,0:T(1,128)}, u32[]{:S(2)}) copy-start(s32[1,3]{1,0:T(1,128)} %param.24) | copy-start | bytes 40
  7.2 14.4 %copy-start.5 = (bf16[1,320,2048]{2,1,0:T(8,128)(2,1)S(1)}, bf16[1,320,2048]{2,1,0:T(8,128)(2,1)}, u32[]{:S(2)}) copy-start(bf16[1,320,2048]{2,1,0:T(8,128)(2,1)} %param.22) | copy-start | bytes 3932164
  7.2 206.0 %all-gather.6.cloned.1.call-start = ((), (), s32[]{:S(2)}) async-start(), calls=%async_computation.3 | async-start | bytes 4128768 | tf_op jit(solution)/shard_map/all_gather | solution.py:1768
  9.5 13.5 %copy-start.25 = (f32[2048]{0:T(1024)S(1)}, f32[2048]{0:T(1024)}, u32[]{:S(2)}) copy-start(f32[2048]{0:T(1024)} %param.27) | copy-start | bytes 24580
  12.9 204.8 %all-gather.4.cloned.1.call-start = ((), (), s32[]{:S(2)}) async-start(), calls=%async_computation.2 | async-start | bytes 9437184 | tf_op jit(solution)/shard_map/all_gather | solution.py:1787
  21.5 98.6 %copy-start.22 = (s32[1280]{0:T(1024)}, s32[1280]{0:T(1024)S(1)}, u32[]{:S(2)}) copy-start(s32[1280]{0:T(1024)S(1)} %get-tuple-element.78) | copy-start | bytes 15364
  21.6 202.9 %copy-start.39 = (s32[128]{0:T(128)}, s32[128]{0:T(128)S(1)}, u32[]{:S(2)}) copy-start(s32[128]{0:T(128)S(1)} %and_select_fusion) | copy-start | bytes 1540
  120.1 437.8 %reduce-scatter.2.cloned.1.call-start = ((), (), s32[]{:S(2)}) async-start(), calls=%async_computation.4 | async-start | bytes 11796480 | tf_op jit(solution)/shard_map/reduce_scatter | solution.py:1885
  120.6 39.4 %collective-permute-start = (bf16[320,2048]{1,0:T(8,128)(2,1)}, bf16[320,2048]{1,0:T(8,128)(2,1)}, u32[]{:S(2)}, u32[]{:S(2)}) collective-permute-start(bf16[320,2048]{1,0:T(8,128)(2,1)} %bitcast.10.refs_1_), channel_id=1, source_target_pairs={{0,2},{2,0},{4,6},{6,4},{1,3},{3,1},{5,7},{7,5},{8,10},{10,8},{12,... | collective-permute-start | bytes 3932168 | tf_op jit(solution)/shard_map/ppermute | solution.py:1683
  121.5 40.0 %collective-permute-start.1 = (bf16[320,2048]{1,0:T(8,128)(2,1)}, bf16[320,2048]{1,0:T(8,128)(2,1)}, u32[]{:S(2)}, u32[]{:S(2)}) collective-permute-start(bf16[320,2048]{1,0:T(8,128)(2,1)} %bitcast.10.refs_1_), channel_id=1, source_target_pairs={{0,4},{4,0},{2,6},{6,2},{1,5},{5,1},{3,7},{7,3},{8,12},{12,8},{10,... | collective-permute-start | bytes 3932168 | tf_op jit(solution)/shard_map/ppermute | solution.py:1684
  121.7 108.4 %collective-permute-start.4 = (bf16[320,2048]{1,0:T(8,128)(2,1)}, bf16[320,2048]{1,0:T(8,128)(2,1)}, u32[]{:S(2)}, u32[]{:S(2)}) collective-permute-start(bf16[320,2048]{1,0:T(8,128)(2,1)} %bitcast.10.refs_1_), channel_id=1, source_target_pairs={{0,1},{1,0},{2,3},{3,2},{4,5},{5,4},{6,7},{7,6},{8,9},{9,8},{10,11... | collective-permute-start | bytes 3932168 | tf_op jit(solution)/shard_map/ppermute | solution.py:1685
  125.8 15.0 %copy-start.38 = (s32[1,320,8]{1,2,0:T(8,128)S(1)}, s32[1,320,8]{1,2,0:T(8,128)}, u32[]{:S(2)}) copy-start(s32[1,320,8]{1,2,0:T(8,128)} %param.26) | copy-start | bytes 30724
  145.0 79.5 %copy-start.28 = (s32[320]{0:T(512)}, s32[320]{0:T(512)S(1)}, u32[]{:S(2)}) copy-start(s32[320]{0:T(512)S(1)} %select_reduce_fusion.3) | copy-start | bytes 3844
  161.2 51.6 %collective-permute-start.2 = (bf16[160,2048]{1,0:T(8,128)(2,1)S(1)}, bf16[160,2048]{1,0:T(8,128)(2,1)}, u32[]{:S(2)}, u32[]{:S(2)}) collective-permute-start(bf16[160,2048]{1,0:T(8,128)(2,1)S(1)} %slice.176), channel_id=1, source_target_pairs={{0,4},{4,0},{2,6},{6,2},{1,5},{5,1},{3,7},{7,3},{8,12},{12,8},{10,... | collective-permute-start | bytes 1966088 | tf_op jit(solution)/shard_map/ppermute | solution.py:1684
  162.8 49.9 %collective-permute-start.3 = (bf16[160,2048]{1,0:T(8,128)(2,1)S(1)}, bf16[160,2048]{1,0:T(8,128)(2,1)}, u32[]{:S(2)}, u32[]{:S(2)}) collective-permute-start(bf16[160,2048]{1,0:T(8,128)(2,1)S(1)} %slice.177), channel_id=1, source_target_pairs={{0,2},{2,0},{4,6},{6,4},{1,3},{3,1},{5,7},{7,5},{8,10},{10,8},{12,... | collective-permute-start | bytes 1966088 | tf_op jit(solution)/shard_map/ppermute | solution.py:1683
  212.2 17.9 %collective-permute-start.5 = (bf16[320,2048]{1,0:T(8,128)(2,1)}, bf16[320,2048]{1,0:T(8,128)(2,1)}, u32[]{:S(2)}, u32[]{:S(2)}) collective-permute-start(bf16[320,2048]{1,0:T(8,128)(2,1)} %collective-permute-done.refs_2_), channel_id=1, source_target_pairs={{0,1},{1,0},{2,3},{3,2},{4,5},{5,4},{6,7},{7,6},{8,9},{9,8},{10,11... | collective-permute-start | bytes 3932168 | tf_op jit(solution)/shard_map/ppermute | solution.py:1685
  212.2 17.9 %collective-permute-start.6 = (bf16[320,2048]{1,0:T(8,128)(2,1)}, bf16[320,2048]{1,0:T(8,128)(2,1)}, u32[]{:S(2)}, u32[]{:S(2)}) collective-permute-start(bf16[320,2048]{1,0:T(8,128)(2,1)} %collective-permute-done.1.refs_3_), channel_id=1, source_target_pairs={{0,1},{1,0},{2,3},{3,2},{4,5},{5,4},{6,7},{7,6},{8,9},{9,8},{10,11... | collective-permute-start | bytes 3932168 | tf_op jit(solution)/shard_map/ppermute | solution.py:1685
  212.7 17.4 %collective-permute-start.7 = (bf16[160,2048]{1,0:T(8,128)(2,1)}, bf16[160,2048]{1,0:T(8,128)(2,1)}, u32[]{:S(2)}, u32[]{:S(2)}) collective-permute-start(bf16[160,2048]{1,0:T(8,128)(2,1)} %collective-permute-done.2.refs_4_), channel_id=1, source_target_pairs={{0,1},{1,0},{2,3},{3,2},{4,5},{5,4},{6,7},{7,6},{8,9},{9,8},{10,11... | collective-permute-start | bytes 1966088 | tf_op jit(solution)/shard_map/ppermute | solution.py:1685
  212.8 17.4 %collective-permute-start.8 = (bf16[160,2048]{1,0:T(8,128)(2,1)}, bf16[160,2048]{1,0:T(8,128)(2,1)}, u32[]{:S(2)}, u32[]{:S(2)}) collective-permute-start(bf16[160,2048]{1,0:T(8,128)(2,1)} %collective-permute-done.3.refs_5_), channel_id=1, source_target_pairs={{0,1},{1,0},{2,3},{3,2},{4,5},{5,4},{6,7},{7,6},{8,9},{9,8},{10,11... | collective-permute-start | bytes 1966088 | tf_op jit(solution)/shard_map/ppermute | solution.py:1685
  224.5 5.5 copy-start.6
  224.6 4.1 copy-start.16
  224.6 4.1 copy-start.21
  440.6 5.0 slice-start
  442.8 3.1 slice-start.1
  445.1 3.7 copy-start.3
  487.6 6.8 %copy-start.7 = (bf16[320,2048]{1,0:T(8,128)(2,1)S(1)}, bf16[320,2048]{1,0:T(8,128)(2,1)}, u32[]{:S(2)}) copy-start(bf16[320,2048]{1,0:T(8,128)(2,1)} %copy-done.6) | copy-start | bytes 3932164
  487.6 64.6 %all-to-all-start = ((bf16[4,1152,256]{2,1,0:T(8,128)(2,1)}), bf16[4,1152,256]{2,1,0:T(8,128)(2,1)}, u32[]{:S(2)}, u32[]{:S(2)}) async-start(bf16[4,1152,256]{2,1,0:T(8,128)(2,1)} %get-tuple-element.73), calls=%async_computation.1 | async-start | bytes 4718592 | tf_op jit(solution)/shard_map/all_to_all | solution.py:1909
  534.8 4.0 copy-start.13
  635.2 4.0 copy-start.8
  (26 other events, 51.4 us)
Sparse Core Ops, SparseCore 0:
  13.0 46.7 all-gather.5
  120.2 82.1 all-gather.3
  436.9 81.0 reduce-scatter.1

commit v6 on v5

--- a/solution.py
+++ b/solution.py
@@ -551,13 +551,13 @@
 def finish_kernel(
     n_c,
     both,
-    weight,
+    h_weight,
     late,
     early,
-    middle,
-    mixed,
-    tokens,
-    grad_middle,
+    h_middle,
+    h_mixed,
+    h_tokens,
+    h_grad_middle,
     gain,
     output,
     grad_tokens,
@@ -586,8 +586,23 @@
     er,
     zs,
     zr,
+    weight,
+    middle,
+    mixed,
+    tokens,
+    grad_middle,
+    loaded,
 ):
     zh, zl, c, core = here()
+    held = (weight, middle, mixed, tokens, grad_middle)
+    loads = [
+        pltpu.make_async_copy(src, dst, loaded.at[n])
+        for n, (src, dst) in enumerate(
+            zip((h_weight, h_middle, h_mixed, h_tokens, h_grad_middle), held, strict=True)
+        )
+    ]
+    for load in loads:
+        load.start()
     plane = [(zh, zl, lax.rem(c + i, n_c), core ^ k) for i in range(n_c) for k in range(2)]
     signal_all(column_peers(zh, zl, c, core) + plane[2:])
     tok, width = output.shape
@@ -640,6 +655,7 @@
                 deliver(n, p, 1 - p)
 
     order = (3, 2, 1, 0)
+    loads[0].wait()
     for n, p in enumerate(order):
         rows = pl.ds(pl.multiple_of(shard(p) * tok, tok), tok)
         give[n] = mm_t(both[rows], weight[theirs]).astype(BF)
@@ -656,6 +672,8 @@
             give[n] = (give[n].astype(F32) + fwd[n].astype(F32)).astype(BF)
             deliver(n, order[n], 1)
 
+    for load in loads[1:]:
+        load.wait()
     output[...] = (middle[...] + mixed[...].astype(F32)).astype(BF)
 
     def total(own, got, arrived):
@@ -775,6 +793,7 @@
     n_f = 2 * n_c
     dma = pltpu.SemaphoreType.DMA
     vmem = pl.BlockSpec(memory_space=VMEM)
+    hbm = pl.BlockSpec(memory_space=ANY)
     return pl.pallas_call(
         functools.partial(finish_kernel, n_c),
         out_shape=(
@@ -785,7 +804,7 @@
             jax.ShapeDtypeStruct((down // 3, SPAN), F32),
             jax.ShapeDtypeStruct((16, SPAN), F32),
         ),
-        in_specs=[vmem] * 9,
+        in_specs=[vmem, hbm, vmem, vmem, hbm, hbm, hbm, hbm, vmem],
         out_specs=[vmem] * 6,
         scratch_shapes=[
             VMEM((4, tok, half), BF),
@@ -809,6 +828,8 @@
             dma((n_f,)),
             dma((4,)),
             dma((4,)),
+            *(VMEM(t.shape, t.dtype) for t in (weight, middle, mixed, tokens, grad_middle)),
+            dma((5,)),
         ],
         compiler_params=pltpu.CompilerParams(
             collective_id=7, has_side_effects=True, vmem_limit_bytes=60 * 2**20

time: 655 us -> 651 us (level)
  transfers between devices with their start and end apart: 13 -> 13, of which waited for: 1 -> 1; matrix products, arithmetic and copies ran while one was open for 12% -> 12% of each run, Pallas kernels for 34% -> 35%
where the time goes in v6:
time: 651 us; the launch traced here: 645 us
  Pallas kernels  503 us (77%)
  local copies, waits for them, and re-layouts  35.1 us (5%)
  other arithmetic  35.1 us (5%)
  matrix products  26.1 us (4%)
  between operations  19.6 us (3%)
  waiting for transfers between devices  12 us (2%)
  starting transfers between devices  11.5 us (2%)
    pallas_call x1, Pallas kernels, run_experts(): pl.pallas_call(functools.partial(experts_kernel, n_c, experts, slots, com...  207 us
    pallas_call x1, Pallas kernels, gather_project(): pl.pallas_call(project_kernel, out_shape=(jax.ShapeDtypeStruct((4, tok, M...  95.6 us
    pallas_call x1, Pallas kernels, finish(): pl.pallas_call(functools.partial(finish_kernel, n_c), out_shape=(jax.Shap...  72.9 us
    pallas_call x1, Pallas kernels, attend_send(): pl.pallas_call(attend_send_kernel, grid=(HEADS,), out_shape=(wide, wide,...  45.5 us
    pallas_call x1, Pallas kernels, to_heads(): pl.pallas_call(to_heads_kernel, out_shape=jax.ShapeDtypeStruct((4, tok, G...  35.9 us
    pallas_call x1, Pallas kernels, attend_back(): pl.pallas_call(attend_back_kernel, grid=(HEADS,), out_shape=(wide(F32), w...  24.7 us
    unnamed x106, local copies, waits for them, and re-layouts  14.9 us
  transfers between devices with their start and end apart: 13, of which 1 were waited for; matrix products, arithmetic and copies ran while one was open for 12% of the time, Pallas kernels for 35%

profile of v6, /device:TPU:9, one launch (start us, length us, event | category | flops | bytes accessed | tf_op | source)
XLA Modules:
  0.0 645.1 jit_solution(12731548850997607759)
XLA Ops:
  14.5 2.1 all-reduce.5
  23.0 1.4 fusion.3.x_ref
  24.5 95.6 %gather_project.1 = (bf16[4,320,2048]{2,1,0:T(8,128)(2,1)}, bf16[2048,1920]{1,0:T(8,128)(2,1)}, bf16[512,512]{1,0:T(8,128)(2,1)}, f32[4,320,1536]{2,1,0:T(8,128)}, bf16[4,320,384]{2,1,0:T(8,128)(2,1)}) custom-call(bf16[320,2048]{1,0:T(8,128)(2,1)} %fusion.3.x_ref, bf16[256,6144]{1,0:T(8,128)(2,1)} %w_ref.1, bf16[256,384]{1,0:T(8,128)(2,1)} %slice.132.down_ref, ...), custom_call_target="tpu_custom_call" | custom-call | tf_op jit(solution)/shard_map/gather_project/pallas_call | solution.py:369
  121.7 2.4 collective-permute-start.4
  125.8 3.0 multiply_reduce_fusion.3
  129.4 5.1 group_sum.2
  145.8 2.4 fusion.23
  148.2 11.9 %collective-permute-done.refs_2_ = bf16[320,2048]{1,0:T(8,128)(2,1)} collective-permute-done((bf16[320,2048]{1,0:T(8,128)(2,1)}, bf16[320,2048]{1,0:T(8,128)(2,1)}, u32[]{:S(2)}, u32[]{:S(2)}) %collective-permute-start) | collective-permute-done | bytes 1310752 | tf_op jit(solution)/shard_map/ppermute | solution.py:1704
  162.8 1.4 collective-permute-start.3
  164.4 1.5 pad_maximum_fusion.4
  165.9 45.5 %attend_send.1 = (bf16[1280,512]{1,0:T(8,128)(2,1)}, bf16[1280,512]{1,0:T(8,128)(2,1)}, bf16[1280,512]{1,0:T(8,128)(2,1)}, f32[4,1280,1]{2,1,0:T(8,128)}, bf16[320,2048]{1,0:T(8,128)(2,1)}) custom-call(f32[1280,1536]{1,0:T(8,128)} %bitcast.102, f32[1280,1536]{1,0:T(8,128)} %bitcast.103, f32[1280,1536]{1,0:T(8,128)} %bitcast.104, f32[1280,1]{1,0:T(8,128)} %bitcast.122, ...), custom_call_target="tpu_custom_call" | custom-call | tf_op jit(solution)/shard_map/attend_send/pallas_call | solution.py:976
  215.8 1.9 fusion.7
  217.7 5.7 fusion.49
  224.6 2.1 fusion.8
  230.1 206.6 %experts.1 = (bf16[8,320,2048]{2,1,0:T(8,128)(2,1)}, bf16[8,320,2176]{2,1,0:T(8,128)(2,1)}, bf16[4,1152,256]{2,1,0:T(8,128)(2,1)}, bf16[8,320,2176]{2,1,0:T(8,12...) custom-call(bf16[320,2176]{1,0:T(8,128)(2,1)} %pad_maximum_fusion.2.refs_0_, ...), custom_call_target="tpu_custom_call" | custom-call | flops 111669149696 | bytes 100000000 | tf_op jit(solution)/shard_map/experts/pallas_call | solution.py:1644
  439.2 1.4 fusion.33
  440.6 2.1 multiply_reduce_fusion
  442.8 2.3 subtract_add_fusion.h_grad_middle
  445.9 2.9 fusion.44
  448.8 2.8 fusion.a_ref
  451.6 35.9 %to_heads.1 = bf16[4,320,512]{2,1,0:T(8,128)(2,1)} custom-call(bf16[320,2048]{1,0:T(8,128)(2,1)} %fusion.a_ref), custom_call_target="tpu_custom_call" | custom-call | tf_op jit(solution)/shard_map/to_heads/pallas_call | solution.py:475
  487.6 4.6 all-to-all-start
  492.2 2.1 convolution_convert_fusion.1
  496.8 24.7 %attend_back.1 = (f32[1280,512]{1,0:T(8,128)}, f32[1280,512]{1,0:T(8,128)}, bf16[1280,512]{1,0:T(8,128)(2,1)}, f32[1280,1]{1,0:T(8,128)}, f32[1280,1]{1,0:T(8,128)}) custom-call(bf16[1280,512]{1,0:T(8,128)(2,1)} %get-tuple-element.44.q_ref, bf16[1280,512]{1,0:T(8,128)(2,1)} %get-tuple-element.45.k_ref, bf16[1280,512]{1,0:T(8,128)(2,1)} %get-tuple-element.46.v_ref, ...), custom_call_target="tpu_custom_call" | custom-call | tf_op jit(solution)/shard_map/attend_back/pallas_call | solution.py:1080
  524.9 5.8 group_sum.3
  534.8 3.9 subtract_convert_fusion.1
  538.7 2.2 pad_maximum_fusion.dp
  540.9 11.3 %late_gradients.1 = (bf16[1280,1920]{1,0:T(8,128)(2,1)}, bf16[8,1152,128]{2,1,0:T(8,128)(2,1)}) custom-call(bf16[1280,1536]{1,0:T(8,128)(2,1)} %pad_maximum_fusion.dp, bf16[384,512]{1,0:T(8,128)(2,1)S(1)} %slice.161.up, f32[1280,128]{1,0:T(8,128)S(1)} %compare_convert_fusion.mask, bf16[1280,384]{1,0:T(8,128)(2,1)S(1)} %bitcast.100, bf16[1280,2048]{1,0:T(8,128)(2,1)} %bitcast.144), custom_call_target="tpu_custom_call" | custom-call | flops 4000000000 | bytes 20000000 | tf_op jit(solution)/shard_map/late_gradients/pallas_call | solution.py:1688
  552.2 2.2 convert_reduce_fusion
  557.9 72.9 %finish.1 = (bf16[320,2048]{1,0:T(8,128)(2,1)}, f32[320,2048]{1,0:T(8,128)}, f32[64,512]{1,0:T(8,128)}, f32[16,2048]{1,0:T(8,128)}, f32[64,128]{1,0:T(8,128)}, /*index=5*/f32[16,128]{1,0:T(8,128)}) custom-call(bf16[1280,1920]{1,0:T(8,128)(2,1)} %get-tuple-element.62.both, bf16[2048,1920]{1,0:T(8,128)(2,1)} %get-tuple-element.63.h_weight, ...), custom_call_target="tpu_custom_call" | custom-call | tf_op jit(solution)/shard_map/finish/pallas_call | solution.py:797
  632.4 2.5 copy.145
  634.9 1.5 copy.146
  (230 shorter events, 55.6 us)
Async XLA Ops:
  7.2 5.8 copy-start.42
  7.2 9.5 %copy-start.18 = (bf16[256,512]{1,0:T(8,128)(2,1)S(1)}, bf16[256,512]{1,0:T(8,128)(2,1)}, u32[]{:S(2)}) copy-start(bf16[256,512]{1,0:T(8,128)(2,1)} %param.36) | copy-start | bytes 786436
  7.2 7.0 %copy-start.41 = (s32[1,3]{1,0:T(1,128)S(1)}, s32[1,3]{1,0:T(1,128)}, u32[]{:S(2)}) copy-start(s32[1,3]{1,0:T(1,128)} %param.25) | copy-start | bytes 40
  7.2 7.0 %copy-start.37 = (s32[1,3]{1,0:T(1,128)S(1)}, s32[1,3]{1,0:T(1,128)}, u32[]{:S(2)}) copy-start(s32[1,3]{1,0:T(1,128)} %param.24) | copy-start | bytes 40
  7.2 14.4 %copy-start.5 = (bf16[1,320,2048]{2,1,0:T(8,128)(2,1)S(1)}, bf16[1,320,2048]{2,1,0:T(8,128)(2,1)}, u32[]{:S(2)}) copy-start(bf16[1,320,2048]{2,1,0:T(8,128)(2,1)} %param.22) | copy-start | bytes 3932164
  7.2 206.0 %all-gather.6.cloned.1.call-start = ((), (), s32[]{:S(2)}) async-start(), calls=%async_computation.3 | async-start | bytes 4128768 | tf_op jit(solution)/shard_map/all_gather | solution.py:1789
  9.5 13.5 %copy-start.25 = (f32[2048]{0:T(1024)S(1)}, f32[2048]{0:T(1024)}, u32[]{:S(2)}) copy-start(f32[2048]{0:T(1024)} %param.27) | copy-start | bytes 24580
  12.9 204.8 %all-gather.4.cloned.1.call-start = ((), (), s32[]{:S(2)}) async-start(), calls=%async_computation.2 | async-start | bytes 9437184 | tf_op jit(solution)/shard_map/all_gather | solution.py:1808
  21.5 98.6 %copy-start.22 = (s32[1280]{0:T(1024)}, s32[1280]{0:T(1024)S(1)}, u32[]{:S(2)}) copy-start(s32[1280]{0:T(1024)S(1)} %get-tuple-element.78) | copy-start | bytes 15364
  21.6 202.9 %copy-start.39 = (s32[128]{0:T(128)}, s32[128]{0:T(128)S(1)}, u32[]{:S(2)}) copy-start(s32[128]{0:T(128)S(1)} %and_select_fusion) | copy-start | bytes 1540
  120.1 437.8 %reduce-scatter.2.cloned.1.call-start = ((), (), s32[]{:S(2)}) async-start(), calls=%async_computation.4 | async-start | bytes 11796480 | tf_op jit(solution)/shard_map/reduce_scatter | solution.py:1906
  120.6 39.4 %collective-permute-start = (bf16[320,2048]{1,0:T(8,128)(2,1)}, bf16[320,2048]{1,0:T(8,128)(2,1)}, u32[]{:S(2)}, u32[]{:S(2)}) collective-permute-start(bf16[320,2048]{1,0:T(8,128)(2,1)} %bitcast.10.refs_1_), channel_id=1, source_target_pairs={{0,2},{2,0},{4,6},{6,4},{1,3},{3,1},{5,7},{7,5},{8,10},{10,8},{12,... | collective-permute-start | bytes 3932168 | tf_op jit(solution)/shard_map/ppermute | solution.py:1704
  121.5 40.0 %collective-permute-start.1 = (bf16[320,2048]{1,0:T(8,128)(2,1)}, bf16[320,2048]{1,0:T(8,128)(2,1)}, u32[]{:S(2)}, u32[]{:S(2)}) collective-permute-start(bf16[320,2048]{1,0:T(8,128)(2,1)} %bitcast.10.refs_1_), channel_id=1, source_target_pairs={{0,4},{4,0},{2,6},{6,2},{1,5},{5,1},{3,7},{7,3},{8,12},{12,8},{10,... | collective-permute-start | bytes 3932168 | tf_op jit(solution)/shard_map/ppermute | solution.py:1705
  121.7 108.4 %collective-permute-start.4 = (bf16[320,2048]{1,0:T(8,128)(2,1)}, bf16[320,2048]{1,0:T(8,128)(2,1)}, u32[]{:S(2)}, u32[]{:S(2)}) collective-permute-start(bf16[320,2048]{1,0:T(8,128)(2,1)} %bitcast.10.refs_1_), channel_id=1, source_target_pairs={{0,1},{1,0},{2,3},{3,2},{4,5},{5,4},{6,7},{7,6},{8,9},{9,8},{10,11... | collective-permute-start | bytes 3932168 | tf_op jit(solution)/shard_map/ppermute | solution.py:1706
  125.8 15.0 %copy-start.38 = (s32[1,320,8]{1,2,0:T(8,128)S(1)}, s32[1,320,8]{1,2,0:T(8,128)}, u32[]{:S(2)}) copy-start(s32[1,320,8]{1,2,0:T(8,128)} %param.26) | copy-start | bytes 30724
  145.0 79.5 %copy-start.28 = (s32[320]{0:T(512)}, s32[320]{0:T(512)S(1)}, u32[]{:S(2)}) copy-start(s32[320]{0:T(512)S(1)} %select_reduce_fusion.3) | copy-start | bytes 3844
  161.2 51.6 %collective-permute-start.2 = (bf16[160,2048]{1,0:T(8,128)(2,1)S(1)}, bf16[160,2048]{1,0:T(8,128)(2,1)}, u32[]{:S(2)}, u32[]{:S(2)}) collective-permute-start(bf16[160,2048]{1,0:T(8,128)(2,1)S(1)} %slice.176), channel_id=1, source_target_pairs={{0,4},{4,0},{2,6},{6,2},{1,5},{5,1},{3,7},{7,3},{8,12},{12,8},{10,... | collective-permute-start | bytes 1966088 | tf_op jit(solution)/shard_map/ppermute | solution.py:1705
  162.8 49.9 %collective-permute-start.3 = (bf16[160,2048]{1,0:T(8,128)(2,1)S(1)}, bf16[160,2048]{1,0:T(8,128)(2,1)}, u32[]{:S(2)}, u32[]{:S(2)}) collective-permute-start(bf16[160,2048]{1,0:T(8,128)(2,1)S(1)} %slice.177), channel_id=1, source_target_pairs={{0,2},{2,0},{4,6},{6,4},{1,3},{3,1},{5,7},{7,5},{8,10},{10,8},{12,... | collective-permute-start | bytes 1966088 | tf_op jit(solution)/shard_map/ppermute | solution.py:1704
  212.2 17.9 %collective-permute-start.5 = (bf16[320,2048]{1,0:T(8,128)(2,1)}, bf16[320,2048]{1,0:T(8,128)(2,1)}, u32[]{:S(2)}, u32[]{:S(2)}) collective-permute-start(bf16[320,2048]{1,0:T(8,128)(2,1)} %collective-permute-done.refs_2_), channel_id=1, source_target_pairs={{0,1},{1,0},{2,3},{3,2},{4,5},{5,4},{6,7},{7,6},{8,9},{9,8},{10,11... | collective-permute-start | bytes 3932168 | tf_op jit(solution)/shard_map/ppermute | solution.py:1706
  212.2 17.9 %collective-permute-start.6 = (bf16[320,2048]{1,0:T(8,128)(2,1)}, bf16[320,2048]{1,0:T(8,128)(2,1)}, u32[]{:S(2)}, u32[]{:S(2)}) collective-permute-start(bf16[320,2048]{1,0:T(8,128)(2,1)} %collective-permute-done.1.refs_3_), channel_id=1, source_target_pairs={{0,1},{1,0},{2,3},{3,2},{4,5},{5,4},{6,7},{7,6},{8,9},{9,8},{10,11... | collective-permute-start | bytes 3932168 | tf_op jit(solution)/shard_map/ppermute | solution.py:1706
  212.7 17.4 %collective-permute-start.7 = (bf16[160,2048]{1,0:T(8,128)(2,1)}, bf16[160,2048]{1,0:T(8,128)(2,1)}, u32[]{:S(2)}, u32[]{:S(2)}) collective-permute-start(bf16[160,2048]{1,0:T(8,128)(2,1)} %collective-permute-done.2.refs_4_), channel_id=1, source_target_pairs={{0,1},{1,0},{2,3},{3,2},{4,5},{5,4},{6,7},{7,6},{8,9},{9,8},{10,11... | collective-permute-start | bytes 1966088 | tf_op jit(solution)/shard_map/ppermute | solution.py:1706
  212.8 17.4 %collective-permute-start.8 = (bf16[160,2048]{1,0:T(8,128)(2,1)}, bf16[160,2048]{1,0:T(8,128)(2,1)}, u32[]{:S(2)}, u32[]{:S(2)}) collective-permute-start(bf16[160,2048]{1,0:T(8,128)(2,1)} %collective-permute-done.3.refs_5_), channel_id=1, source_target_pairs={{0,1},{1,0},{2,3},{3,2},{4,5},{5,4},{6,7},{7,6},{8,9},{9,8},{10,11... | collective-permute-start | bytes 1966088 | tf_op jit(solution)/shard_map/ppermute | solution.py:1706
  224.5 5.5 copy-start.6
  224.6 4.1 copy-start.16
  224.6 4.1 copy-start.21
  440.6 5.0 slice-start
  442.8 3.1 slice-start.1
  445.1 3.7 copy-start.3
  487.6 6.8 %copy-start.7 = (bf16[320,2048]{1,0:T(8,128)(2,1)S(1)}, bf16[320,2048]{1,0:T(8,128)(2,1)}, u32[]{:S(2)}) copy-start(bf16[320,2048]{1,0:T(8,128)(2,1)} %copy-done.6) | copy-start | bytes 3932164
  487.6 64.6 %all-to-all-start = ((bf16[4,1152,256]{2,1,0:T(8,128)(2,1)}), bf16[4,1152,256]{2,1,0:T(8,128)(2,1)}, u32[]{:S(2)}, u32[]{:S(2)}) async-start(bf16[4,1152,256]{2,1,0:T(8,128)(2,1)} %get-tuple-element.73), calls=%async_computation.1 | async-start | bytes 4718592 | tf_op jit(solution)/shard_map/all_to_all | solution.py:1930
  534.8 4.0 copy-start.13
  630.8 4.0 copy-start.8
  (26 other events, 51.4 us)
Sparse Core Ops, SparseCore 0:
  13.0 46.7 all-gather.5
  120.2 82.1 all-gather.3
  436.9 81.0 reduce-scatter.1
